TPU v7x, 512 devices: a whole 4x8x8 slice. The times are simulated.
512 devices in a mesh: dp: 8 (over z), tile: 64 (over x, y, core).
Axes of the slice: x: 4, y: 8, z: 8, core: 2. Of those that a mesh axis runs over, the one named last changes fastest.
Arguments:
- features: bfloat16 [8, 64, 16, 16, 256], P('dp', 'tile'), may hold values from -6 to 6
- cotangent: bfloat16 [8, 64, 16, 16, 256], P('dp', 'tile'), may hold values from -6 to 6
- weight: bfloat16 [3, 3, 256, 256], replicated, may hold values from -0.125 to 0.125
- tile_owner: int32 [8, 64], P('dp'), may hold values from 0 to 63, as said below
- tile_neighbors: int32 [8, 64, 8], P('dp'), may hold values from -1 to 63, as said below
- tile_counts: int32 [8], P('dp'), may hold values from 32 to 64, as said below
Outputs:
- out_features: bfloat16 [8, 64, 16, 16, 256], P('dp', 'tile')
- grad_features: bfloat16 [8, 64, 16, 16, 256], P('dp', 'tile')
- grad_weight: bfloat16 [3, 3, 256, 256], replicated
Inputs may be any that keep to these rules, and one draw needn't show every extreme that they name: `tile_owner`: each slide's row is a permutation of the devices 0 to 63. `tile_neighbors`: entries name list positions below the slide's count, each tile's neighbors are distinct and the relation is symmetric (opposite directions); list positions at or above the count have only -1. `tile_counts`: slide 0 has all 64 slots live.
All inputs are finite; a program needn't handle non-finite values.
Results may differ from a plain program's by a relative error of at most 0.001.
Values may be sent and summed in bfloat16 or wider, within the bound.
No kernel may reach another device: no remote copies, remote signals or barrier semaphores. Data moves between devices by JAX's collectives and lax.ppermute only.
A program may use at most 64 MiB of HBM per device.

v0:
```python
import math

import jax
import jax.numpy as jnp
from jax import lax
from jax.sharding import PartitionSpec as P

DILATION_SPAN = 4


def outgoing(feature_field, select):
    edge_strip = feature_field.shape[0]

    def corner_patch(tile_piece):
        return jnp.pad(tile_piece, ((0, 0), (0, edge_strip - DILATION_SPAN), (0, 0)))

    strips = jnp.stack(
        [
            corner_patch(feature_field[:DILATION_SPAN, :DILATION_SPAN]),
            feature_field[:DILATION_SPAN],
            corner_patch(feature_field[:DILATION_SPAN, edge_strip - DILATION_SPAN :]),
            jnp.swapaxes(feature_field[:, :DILATION_SPAN], 0, 1),
            jnp.swapaxes(feature_field[:, edge_strip - DILATION_SPAN :], 0, 1),
            corner_patch(feature_field[edge_strip - DILATION_SPAN :, :DILATION_SPAN]),
            feature_field[edge_strip - DILATION_SPAN :],
            corner_patch(feature_field[edge_strip - DILATION_SPAN :, edge_strip - DILATION_SPAN :]),
        ]
    )
    return jnp.einsum("pd,dabc->pabc", select, strips, preferred_element_type=jnp.float32).astype(
        jnp.bfloat16
    )


def attach(center, incoming, select):
    border_cells = jnp.einsum(
        "pd,pabc->dabc", select, incoming, preferred_element_type=jnp.float32
    ).astype(jnp.bfloat16)
    top_band = jnp.concatenate(
        [border_cells[0][:, :DILATION_SPAN], border_cells[1], border_cells[2][:, :DILATION_SPAN]],
        axis=1,
    )
    middle_band = jnp.concatenate(
        [jnp.swapaxes(border_cells[3], 0, 1), center, jnp.swapaxes(border_cells[4], 0, 1)], axis=1
    )
    bottom_band = jnp.concatenate(
        [border_cells[5][:, :DILATION_SPAN], border_cells[6], border_cells[7][:, :DILATION_SPAN]],
        axis=1,
    )
    return jnp.concatenate([top_band, middle_band, bottom_band], axis=0)


def forward_taps(padded_tile, weight):
    edge_strip = padded_tile.shape[0] - 2 * DILATION_SPAN
    width = padded_tile.shape[2]
    summed = jnp.zeros((edge_strip * edge_strip, width), jnp.float32)
    for first_operand in range(3):
        for second_operand in range(3):
            sliding_window = padded_tile[
                DILATION_SPAN * first_operand : DILATION_SPAN * first_operand + edge_strip,
                DILATION_SPAN * second_operand : DILATION_SPAN * second_operand + edge_strip,
            ].reshape(edge_strip * edge_strip, width)
            summed = summed + jnp.dot(
                sliding_window,
                weight[first_operand, second_operand],
                preferred_element_type=jnp.float32,
            )
    return summed.reshape(edge_strip, edge_strip, width)


def backward_taps(padded_tile, weight):
    edge_strip = padded_tile.shape[0] - 2 * DILATION_SPAN
    width = padded_tile.shape[2]
    summed = jnp.zeros((edge_strip * edge_strip, width), jnp.float32)
    for first_operand in range(3):
        for second_operand in range(3):
            row_begin = 2 * DILATION_SPAN - DILATION_SPAN * first_operand
            column_begin = 2 * DILATION_SPAN - DILATION_SPAN * second_operand
            sliding_window = padded_tile[
                row_begin : row_begin + edge_strip, column_begin : column_begin + edge_strip
            ].reshape(edge_strip * edge_strip, width)
            summed = summed + jnp.dot(
                sliding_window,
                weight[first_operand, second_operand].T,
                preferred_element_type=jnp.float32,
            )
    return summed.reshape(edge_strip, edge_strip, width)


def weight_taps(padded_tile, grad_rows):
    edge_strip = padded_tile.shape[0] - 2 * DILATION_SPAN
    width = padded_tile.shape[2]
    result = []
    for first_operand in range(3):
        row_list = []
        for second_operand in range(3):
            sliding_window = padded_tile[
                DILATION_SPAN * first_operand : DILATION_SPAN * first_operand + edge_strip,
                DILATION_SPAN * second_operand : DILATION_SPAN * second_operand + edge_strip,
            ].reshape(edge_strip * edge_strip, width)
            row_list.append(
                jnp.dot(sliding_window.T, grad_rows, preferred_element_type=jnp.float32)
            )
        result.append(jnp.stack(row_list))
    return jnp.stack(result)


def local(features, cotangent, weight, tile_owner, tile_neighbors, tile_counts):
    tile_total = lax.axis_size("tile")
    device = lax.axis_index("tile")
    positions = jnp.arange(tile_total, dtype=jnp.int32)
    owner_row = tile_owner[0]
    held = jnp.sum(jnp.where(owner_row == device, positions, 0))
    is_live = held < tile_counts[0]
    near_pos = lax.dynamic_index_in_dim(tile_neighbors[0], held, 0, keepdims=False)
    peer_dev = jnp.where(near_pos >= 0, owner_row[jnp.maximum(near_pos, 0)], -1)
    masked_x = jnp.where(is_live, features[0, 0], jnp.zeros_like(features[0, 0]))
    masked_g = jnp.where(is_live, cotangent[0, 0], jnp.zeros_like(cotangent[0, 0]))
    edge_strip = masked_x.shape[0]
    width = masked_x.shape[2]
    select = (positions[:, None] == peer_dev[None, :]).astype(jnp.bfloat16)
    in_feat = lax.all_to_all(
        outgoing(masked_x, select), "tile", split_axis=0, concat_axis=0, tiled=True
    )
    padded_x = attach(masked_x, in_feat, select)
    out_tile = forward_taps(padded_x, weight)
    in_grad = lax.all_to_all(
        outgoing(masked_g, select), "tile", split_axis=0, concat_axis=0, tiled=True
    )
    padded_g = attach(masked_g, in_grad, select)
    grad_tile = backward_taps(padded_g, weight)
    local_sum = weight_taps(padded_x, masked_g.reshape(edge_strip * edge_strip, width))
    summed = lax.psum(local_sum, ("dp", "tile"))
    grad_scale = 1.0 / math.sqrt(lax.axis_size("dp") * tile_total * edge_strip * edge_strip)
    out_features = jnp.where(is_live, out_tile, 0.0).astype(jnp.bfloat16).reshape(features.shape)
    grad_features = jnp.where(is_live, grad_tile, 0.0).astype(jnp.bfloat16).reshape(features.shape)
    grad_weight = (summed * grad_scale).astype(jnp.bfloat16)
    return (out_features, grad_features, grad_weight)


def solution(mesh):
    return jax.shard_map(
        local,
        mesh=mesh,
        in_specs=(
            P("dp", "tile", None, None, None),
            P("dp", "tile", None, None, None),
            P(),
            P("dp", None),
            P("dp", None, None),
            P("dp"),
        ),
        out_specs=(P("dp", "tile", None, None, None), P("dp", "tile", None, None, None), P()),
        check_vma=False,
    )
```

profile of v0, /device:TPU:1, one launch (start us, length us, event | category | flops | bytes accessed | tf_op | source)
XLA Modules:
  0.0 438.6 jit_solution(2350745723528833631)
XLA Ops:
  7.8 1.3 fusion.61
  9.8 1.0 broadcast_select_fusion
  12.8 0.9 compare_reduce_fusion
  13.7 0.9 maximum_reduce_fusion
  15.8 0.8 stack.110
  17.4 2.5 copy.545
  19.9 11.6 %all-to-all-start = ((bf16[64,4,16,256]{3,2,1,0:T(8,128)(2,1)}), bf16[64,4,16,256]{3,2,1,0:T(8,128)(2,1)S(1)}, u32[]{:S(2)}, u32[]{:S(2)}) async-start(bf16[64,4,16,256]{3,2,1,0:T(8,128)(2,1)} %copy.545), calls=%async_computation | async-start | bytes 4194304 | tf_op jit(solution)/shard_map/all_to_all | solution.py:121
  32.1 0.8 stack.119
  33.0 0.8 convolution_convert_fusion
  33.8 2.5 copy.559
  36.3 46.4 %all-to-all-done = bf16[64,4,16,256]{3,2,1,0:T(8,128)(2,1)S(1)} async-done(((bf16[64,4,16,256]{3,2,1,0:T(8,128)(2,1)}), bf16[64,4,16,256]{3,2,1,0:T(8,128)(2,1)S(1)}, u32[]{:S(2)}, u32[]{:S(2)}) %all-to-all-start) | async-done | bytes 2097184 | tf_op jit(solution)/shard_map/all_to_all | solution.py:121
  82.8 1.3 copy-done.1
  84.1 5.8 %all-to-all-start.1 = ((bf16[64,4,16,256]{3,2,1,0:T(8,128)(2,1)}), bf16[64,4,16,256]{3,2,1,0:T(8,128)(2,1)S(1)}, u32[]{:S(2)}, u32[]{:S(2)}) async-start(bf16[64,4,16,256]{3,2,1,0:T(8,128)(2,1)} %copy.559), calls=%async_computation.1 | async-start | bytes 4194304 | tf_op jit(solution)/shard_map/all_to_all | solution.py:126
  90.1 0.9 convolution_bitcast_fusion.4
  91.1 2.8 fusion.4
  96.5 0.9 convolution_bitcast_fusion
  97.4 0.9 convolution_bitcast_fusion.1
  98.4 0.9 convolution_bitcast_fusion.2
  100.1 0.9 convolution_bitcast_fusion.6
  101.1 0.9 convolution_bitcast_fusion.7
  102.0 0.9 convolution_bitcast_fusion.8
  102.9 38.2 %all-to-all-done.1 = bf16[64,4,16,256]{3,2,1,0:T(8,128)(2,1)S(1)} async-done(((bf16[64,4,16,256]{3,2,1,0:T(8,128)(2,1)}), bf16[64,4,16,256]{3,2,1,0:T(8,128)(2,1)S(1)}, u32[]{:S(2)}, u32[]{:S(2)}) %all-to-all-start.1) | async-done | bytes 2097184 | tf_op jit(solution)/shard_map/all_to_all | solution.py:126
  141.1 1.2 fusion.7
  143.6 0.8 copy-done.2
  146.2 0.9 copy-done.11
  147.2 0.9 copy-done.15
  148.3 1.6 pad_maximum_fusion
  149.9 0.9 copy-done.9
  152.6 0.8 fusion.12
  155.0 0.9 fusion.13
  155.9 272.9 %all-reduce.10.cloned.1.call-done = f32[3,3,256,256]{3,2,1,0:T(8,128)} async-done(((f32[3,3,256,256]{3,2,1,0:T(8,128)}), f32[3,3,256,256]{3,2,1,0:T(8,128)}) %all-reduce.10.cloned.1.call-update) | async-done | bytes 2359312 | tf_op jit(solution)/shard_map/psum | solution.py:132
  428.9 2.9 multiply_convert_fusion
  (122 shorter events, 12.4 us)
Async XLA Ops:
  7.2 7.9 %copy-start = (s32[1,64]{1,0:T(1,128)S(1)}, s32[1,64]{1,0:T(1,128)}, u32[]{:S(2)}) copy-start(s32[1,64]{1,0:T(1,128)} %param.9) | copy-start | bytes 772
  19.9 62.9 %all-to-all-start = ((bf16[64,4,16,256]{3,2,1,0:T(8,128)(2,1)}), bf16[64,4,16,256]{3,2,1,0:T(8,128)(2,1)S(1)}, u32[]{:S(2)}, u32[]{:S(2)}) async-start(bf16[64,4,16,256]{3,2,1,0:T(8,128)(2,1)} %copy.545), calls=%async_computation | async-start | bytes 4194304 | tf_op jit(solution)/shard_map/all_to_all | solution.py:121
  82.8 1.3 copy-start.1
  84.1 57.1 %all-to-all-start.1 = ((bf16[64,4,16,256]{3,2,1,0:T(8,128)(2,1)}), bf16[64,4,16,256]{3,2,1,0:T(8,128)(2,1)S(1)}, u32[]{:S(2)}, u32[]{:S(2)}) async-start(bf16[64,4,16,256]{3,2,1,0:T(8,128)(2,1)} %copy.559), calls=%async_computation.1 | async-start | bytes 4194304 | tf_op jit(solution)/shard_map/all_to_all | solution.py:126
  89.9 339.0 %all-reduce.10.cloned.1.call-start = ((), (), s32[]{:S(2)}) async-start(), calls=%async_computation.2 | async-start | bytes 4718592 | tf_op jit(solution)/shard_map/psum | solution.py:132
  143.1 1.3 copy-start.2
  143.1 1.3 copy-start.10
  143.3 1.5 copy-start.3
  144.6 0.9 copy-start.4
  145.1 1.0 copy-start.12
  145.1 1.0 copy-start.13
  145.1 1.1 copy-start.14
  146.2 0.9 copy-start.11
  147.1 0.9 copy-start.15
  147.1 1.0 copy-start.16
  147.1 1.1 copy-start.17
  149.9 0.9 copy-start.9
  149.9 1.1 copy-start.8
  151.2 0.9 copy-start.7
  151.4 0.9 copy-start.6
  151.6 0.9 copy-start.5
Sparse Core Ops, SparseCore 0:
  150.1 278.7 all-reduce.9
where the time goes:
time: 439 us
  waiting for transfers between devices  358 us (82%)
  between operations  18.1 us (4%)
  local copies, waits for them, and re-layouts  17.8 us (4%)
  starting transfers between devices  17.7 us (4%)
  matrix products  17.6 us (4%)
  other arithmetic  9.97 us (2%)
    psum x1, waiting for transfers between devices, local(): summed = lax.psum(local_sum, ('dp', 'tile'))  273 us
    all_to_all x1, waiting for transfers between devices, local(): lax.all_to_all(outgoing(masked_x, select), 'tile', split_axis=0, concat_a...  46.4 us
    all_to_all x1, waiting for transfers between devices, local(): lax.all_to_all(outgoing(masked_g, select), 'tile', split_axis=0, concat_a...  38.2 us
    all_to_all x1, starting transfers between devices, local(): lax.all_to_all(outgoing(masked_x, select), 'tile', split_axis=0, concat_a...  11.6 us
  transfers between devices with their start and end apart: 3, of which 3 were waited for; matrix products, arithmetic and copies ran while one was open for 5% of the time, Pallas kernels for 0%

commit v1 on v0

v1 whole, which is shorter than its diff:
```python
import functools
import math

import jax
import jax.numpy as jnp
from jax import lax
from jax.experimental import pallas as pl
from jax.experimental.pallas import tpu as pltpu
from jax.sharding import PartitionSpec as P

SPAN = 4
CELLS = SPAN * SPAN
CLASSES = SPAN * SPAN
PAD = SPAN + 2
HALF = 128
QUARTER = 64
bf16, f32 = jnp.bfloat16, jnp.float32


def device_of(m, hi, ho):
    return m * 4 + ho * 2 + hi


def vmem(n):
    return [pl.BlockSpec(memory_space=pltpu.VMEM)] * n


PARAMS = pltpu.CompilerParams(vmem_limit_bytes=24 * 1024 * 1024)


def live_mask(owner, device, count):
    positions = lax.broadcasted_iota(jnp.int32, owner.shape, 1)
    held = jnp.sum(jnp.where(owner == device, positions, 0).astype(f32), axis=1, keepdims=True)
    return held < count.astype(f32)


def class_order(transposed):
    n = CLASSES * CELLS
    o = lax.broadcasted_iota(jnp.int32, (n, n), 1 if transposed else 0)
    c = lax.broadcasted_iota(jnp.int32, (n, n), 0 if transposed else 1)
    mr, mc, r, k = o >> 6, (o >> 4) & 3, (o >> 2) & 3, o & 3
    return c == (r * SPAN + mr) * 16 + k * SPAN + mc


def swap16():
    o = lax.broadcasted_iota(jnp.int32, (256, 256), 0)
    c = lax.broadcasted_iota(jnp.int32, (256, 256), 1)
    return jnp.where(c == ((o & 15) << 4) + (o >> 4), 1.0, 0.0).astype(bf16)


def dot(a, b):
    return jnp.dot(a, b, preferred_element_type=f32)


def split_kernel(place_ref, x_ref, g_ref, owner_ref, send_ref):
    live = live_mask(owner_ref[...], place_ref[0], place_ref[1])
    order = jnp.where(class_order(False) & live, 1.0, 0.0).astype(bf16)
    x = dot(order, x_ref[...]).astype(bf16)
    g = dot(order, g_ref[...]).astype(bf16)
    for m in range(CLASSES):
        for hi in range(2):
            for ho in range(2):
                rows = slice(m * CELLS, (m + 1) * CELLS)
                j = device_of(m, hi, ho)
                send_ref[j, :, :HALF] = x[rows, hi * HALF : (hi + 1) * HALF]
                send_ref[j, :, HALF:] = g[rows, ho * HALF : (ho + 1) * HALF]


def surround(padded, cells, sel_ref):
    def put(d, sources, targets):
        width = cells[0].shape[1]
        got = dot(sel_ref[d], jnp.concatenate([cells[s] for s in sources], axis=1)).astype(bf16)
        for n, (r, c) in enumerate(targets):
            padded[r * PAD + c] = got[:, n * width : (n + 1) * width]

    for r in range(SPAN):
        for c in range(SPAN):
            padded[(r + 1) * PAD + c + 1] = cells[r * SPAN + c]
    last, side = SPAN - 1, range(SPAN)
    put(0, [last * SPAN + last], [(0, 0)])
    put(1, [last * SPAN + c for c in side], [(0, c + 1) for c in side])
    put(2, [last * SPAN], [(0, PAD - 1)])
    put(3, [r * SPAN + last for r in side], [(r + 1, 0) for r in side])
    put(4, [r * SPAN for r in side], [(r + 1, PAD - 1) for r in side])
    put(5, [last], [(PAD - 1, 0)])
    put(6, [c for c in side], [(PAD - 1, c + 1) for c in side])
    put(7, [0], [(PAD - 1, PAD - 1)])


def window(padded, a, b):
    rows = [padded[(r + a) * PAD + c + b] for r in range(SPAN) for c in range(SPAN)]
    return jnp.concatenate(rows, axis=0)


def weight_kernel(recv_ref, sel_ref, sum_ref, x_ref, g_ref, padded):
    swap = swap16()
    for k in range(recv_ref.shape[0] // 16):
        rows = recv_ref[k * 16 : (k + 1) * 16].reshape(256, 2 * HALF)
        turned = dot(swap, rows).astype(bf16)
        for s in range(CELLS):
            x_ref[s, k * 16 : (k + 1) * 16, :] = turned[s * 16 : (s + 1) * 16, :HALF]
            g_ref[s, k * 16 : (k + 1) * 16, :] = turned[s * 16 : (s + 1) * 16, HALF:]
    surround(padded, [x_ref[s] for s in range(CELLS)], sel_ref)
    grad = g_ref[...].reshape(-1, HALF).T
    for a in range(3):
        for b in range(3):
            tap = a * 3 + b
            sum_ref[tap * HALF : (tap + 1) * HALF, :] = dot(grad, window(padded, a, b)).T


def conv_kernel(xa_ref, xb_ref, ga_ref, gb_ref, sel_ref, wo_ref, wg_ref, out_ref, padded):
    def taps(a_ref, b_ref, w_ref, flip):
        surround(padded, [jnp.concatenate([a_ref[s], b_ref[s]], axis=1) for s in range(CELLS)], sel_ref)
        total = jnp.zeros((CELLS * a_ref.shape[1], QUARTER), f32)
        for a in range(3):
            for b in range(3):
                view = window(padded, 2 - a, 2 - b) if flip else window(padded, a, b)
                total = total + dot(view, w_ref[a * 3 + b])
        return total

    forward = taps(xa_ref, xb_ref, wo_ref, False)
    backward = taps(ga_ref, gb_ref, wg_ref, True)
    both = jnp.concatenate([forward, backward], axis=1).astype(bf16)
    tiles = xa_ref.shape[1]
    swap = swap16()
    for k in range(tiles // 16):
        rows = [both[s * tiles + k * 16 : s * tiles + (k + 1) * 16] for s in range(CELLS)]
        turned = dot(swap, jnp.concatenate(rows, axis=0)).astype(bf16)
        out_ref[k * 16 : (k + 1) * 16] = turned.reshape(16, CELLS, 2 * QUARTER)


def join_kernel(place_ref, recv_ref, owner_ref, out_ref, grad_ref):
    live = live_mask(owner_ref[...], place_ref[0], place_ref[1])
    order = jnp.where(class_order(True) & live, 1.0, 0.0).astype(bf16)

    def join(low):
        rows = []
        for m in range(CLASSES):
            parts = [recv_ref[device_of(m, hi, ho), :, low : low + QUARTER] for hi in range(2) for ho in range(2)]
            rows.append(jnp.concatenate(parts, axis=1))
        return dot(order, jnp.concatenate(rows, axis=0)).astype(bf16)

    out_ref[...] = join(0)
    grad_ref[...] = join(QUARTER)


def neighbour_table(owner, neighbors):
    tiles = owner.shape[0]
    positions = jnp.arange(tiles, dtype=jnp.int32)
    beside = jnp.sum(jnp.where(neighbors[:, :, None] == positions, owner + 1, 0), axis=2) - 1
    peer = jnp.sum(jnp.where((owner == positions[:, None])[:, :, None], beside[None], 0), axis=1)
    return (peer.T[:, :, None] == positions).astype(bf16)


def local(features, cotangent, weight, tile_owner, tile_neighbors, tile_counts):
    tiles = lax.axis_size("tile")
    slides = lax.axis_size("dp")
    device = lax.axis_index("tile")
    hi, ho = device % 2, (device // 2) % 2
    width = features.shape[-1]
    cells = features.shape[2] * features.shape[3]
    place = jnp.stack([device, tile_counts[0]])
    smem = pl.BlockSpec(memory_space=pltpu.SMEM)

    send = pl.pallas_call(
        split_kernel,
        out_shape=jax.ShapeDtypeStruct((tiles, CELLS, 2 * HALF), bf16),
        in_specs=[smem, *vmem(3)],
        out_specs=vmem(1)[0],
        compiler_params=PARAMS,
        name="split",
    )(place, features.reshape(cells, width), cotangent.reshape(cells, width), tile_owner)
    recv = lax.all_to_all(send, "tile", 0, 0, tiled=True)

    sel = neighbour_table(tile_owner[0], tile_neighbors[0])
    taps = weight.shape[0] * weight.shape[1]
    block = (CELLS, tiles, HALF)
    partial, x_own, g_own = pl.pallas_call(
        weight_kernel,
        out_shape=[
            jax.ShapeDtypeStruct((taps * HALF, HALF), f32),
            jax.ShapeDtypeStruct(block, bf16),
            jax.ShapeDtypeStruct(block, bf16),
        ],
        in_specs=vmem(2),
        out_specs=vmem(3),
        scratch_shapes=[pltpu.VMEM((PAD * PAD, tiles, HALF), bf16)],
        compiler_params=PARAMS,
        name="weight_taps",
    )(recv, sel)

    groups = [[device_of(m, i, o) for m in range(CLASSES)] for o in range(2) for i in range(2)]
    rows = taps * HALF // CLASSES
    parts = lax.all_to_all(
        partial.reshape(CLASSES, rows, HALF), "tile", 0, 0, tiled=True, axis_index_groups=groups
    )
    part = jnp.sum(parts, axis=0)
    parts = lax.all_to_all(jnp.broadcast_to(part, (slides, rows, HALF)), "dp", 0, 0, tiled=True)
    scale = 1.0 / math.sqrt(slides * tiles * cells)
    part = (jnp.sum(parts, axis=0) * scale).astype(bf16)
    groups = [[device_of(m, i, o) for o in range(2) for m in range(CLASSES)] for i in range(2)]
    mine = lax.all_to_all(
        jnp.broadcast_to(part, (2 * CLASSES, rows, HALF)), "tile", 0, 0, tiled=True, axis_index_groups=groups
    )
    core = [(j, j ^ 1) for j in range(tiles)]
    other = lax.ppermute(mine, "tile", core)
    low = jnp.where(hi == 0, mine, other)
    high = jnp.where(hi == 0, other, mine)

    def whole_rows(half):
        return half.reshape(2, taps, HALF, HALF).transpose(1, 2, 0, 3).reshape(taps, HALF, 2 * HALF)

    grad_weight = jnp.concatenate([whole_rows(low), whole_rows(high)], axis=1).reshape(weight.shape)

    x_other = lax.ppermute(x_own, "tile", core)
    g_other = lax.ppermute(g_own, "tile", [(j, j ^ 2) for j in range(tiles)])
    quarter = (2 * hi + ho) * QUARTER
    flat = weight.reshape(taps, width, width)

    def half_first(array, half):
        swapped = jnp.concatenate([array[:, HALF:], array[:, :HALF]], axis=1)
        return jnp.where(half == 0, array, swapped)

    w_out = half_first(lax.dynamic_slice_in_dim(flat, quarter, QUARTER, axis=2), hi)
    w_grad = half_first(lax.dynamic_slice_in_dim(flat, quarter, QUARTER, axis=1).transpose(0, 2, 1), ho)
    back = pl.pallas_call(
        conv_kernel,
        out_shape=jax.ShapeDtypeStruct((tiles, CELLS, 2 * QUARTER), bf16),
        in_specs=vmem(7),
        out_specs=vmem(1)[0],
        scratch_shapes=[pltpu.VMEM((PAD * PAD, tiles, 2 * HALF), bf16)],
        compiler_params=PARAMS,
        name="conv_taps",
    )(x_own, x_other, g_own, g_other, sel, w_out, w_grad)
    back = lax.all_to_all(back, "tile", 0, 0, tiled=True)
    out, grad = pl.pallas_call(
        join_kernel,
        out_shape=[jax.ShapeDtypeStruct((cells, width), bf16)] * 2,
        in_specs=[smem, *vmem(2)],
        out_specs=vmem(2),
        compiler_params=PARAMS,
        name="join",
    )(place, back, tile_owner)
    return out.reshape(features.shape), grad.reshape(features.shape), grad_weight


def solution(mesh):
    return jax.shard_map(
        local,
        mesh=mesh,
        in_specs=(
            P("dp", "tile", None, None, None),
            P("dp", "tile", None, None, None),
            P(),
            P("dp", None),
            P("dp", None, None),
            P("dp"),
        ),
        out_specs=(P("dp", "tile", None, None, None), P("dp", "tile", None, None, None), P()),
        check_vma=False,
    )
```

time: 439 us -> 136 us (0.31)
  waiting for transfers between devices: 358 us -> 17.1 us
  blocking collectives: 0 us -> 58.3 us
  starting transfers between devices: 17.7 us -> 37.4 us
  matrix products: 17.6 us -> 0 us
  between operations: 18.1 us -> 1.54 us
  local copies, waits for them, and re-layouts: 17.8 us -> 8.82 us
  Pallas kernels: 0 us -> 8.11 us
  other arithmetic: 9.97 us -> 4.39 us
    psum x1 -> x0, waiting for transfers between devices: 273 us -> none  [local(): summed = lax.psum(local_sum, ('dp', 'tile'))]
    all_to_all x2, waiting for transfers between devices: 84.7 us -> 17.1 us  [the longest x1 14.5 us: local(): recv = lax.all_to_all(send, 'tile', 0, 0, tiled=True)]
    all_to_all x0 -> x3, blocking collectives: none -> 58.3 us  [the longest x1 20.8 us: local(): lax.all_to_all(partial.reshape(CLASSES, rows, HALF), 'tile', 0, 0, tiled=...]
    dot_general x31 -> x0, matrix products: 17.6 us -> none  [the longest x9 6.98 us: weight_taps(): jnp.dot(sliding_window.T, grad_rows, preferred_element_type=jnp.float32)]
    ppermute x0 -> x3, starting transfers between devices: none -> 16.5 us  [the longest x1 8.29 us: local(): other = lax.ppermute(mine, 'tile', core)]
    pallas_call x0 -> x4, Pallas kernels: none -> 8.11 us  [the longest x1 3.52 us: local(): pl.pallas_call(conv_kernel, out_shape=jax.ShapeDtypeStruct((tiles, CELLS,...]
    convert_element_type x2 -> x0, local copies, waits for them, and re-layouts: 5.03 us -> none  [outgoing(): jnp.einsum('pd,dabc->pabc', select, strips, preferred_element_type=jnp.fl...]
  transfers between devices with their start and end apart: 3 -> 5, of which waited for: 3 -> 2; matrix products, arithmetic and copies ran while one was open for 5% -> 5% of each run, Pallas kernels for 0% -> 4%
where the time goes in v1:
time: 136 us
  blocking collectives  58.3 us (43%)
  starting transfers between devices  37.4 us (28%)
  waiting for transfers between devices  17.1 us (13%)
  local copies, waits for them, and re-layouts  8.82 us (6%)
  Pallas kernels  8.11 us (6%)
  other arithmetic  4.39 us (3%)
  between operations  1.54 us (1%)
    all_to_all x1, blocking collectives, local(): lax.all_to_all(partial.reshape(CLASSES, rows, HALF), 'tile', 0, 0, tiled=...  20.8 us
    all_to_all x1, blocking collectives, local(): lax.all_to_all(jnp.broadcast_to(part, (slides, rows, HALF)), 'dp', 0, 0,...  19.5 us
    all_to_all x1, blocking collectives, local(): back = lax.all_to_all(back, 'tile', 0, 0, tiled=True)  18.1 us
    all_to_all x1, waiting for transfers between devices, local(): recv = lax.all_to_all(send, 'tile', 0, 0, tiled=True)  14.5 us
    all_to_all x1, starting transfers between devices, local(): recv = lax.all_to_all(send, 'tile', 0, 0, tiled=True)  11.6 us
    all_to_all x1, starting transfers between devices, local(): lax.all_to_all(jnp.broadcast_to(part, (2 * CLASSES, rows, HALF)), 'tile',...  9.23 us
    ppermute x1, starting transfers between devices, local(): other = lax.ppermute(mine, 'tile', core)  8.29 us
    unnamed x12, local copies, waits for them, and re-layouts  5.58 us
  transfers between devices with their start and end apart: 5, of which 2 were waited for; matrix products, arithmetic and copies ran while one was open for 5% of the time, Pallas kernels for 4%

profile of v1, /device:TPU:1, one launch (start us, length us, event | category | flops | bytes accessed | tf_op | source)
XLA Modules:
  0.0 135.7 jit_solution(2487175303189477435)
XLA Ops:
  1.4 0.9 copy-done
  2.3 0.9 copy-done.1
  3.2 0.7 copy-done.2
  3.9 1.6 %split.1 = bf16[64,16,256]{2,1,0:T(8,128)(2,1)} custom-call(s32[2]{0:T(128)S(1)} %pad_add_fusion.place_ref, bf16[256,256]{1,0:T(8,128)(2,1)S(1)} %bitcast.24, bf16[256,256]{1,0:T(8,128)(2,1)S(1)} %bitcast.25, s32[1,64]{1,0:T(1,128)S(1)} %copy-done.2), custom_call_target="tpu_custom_call" | custom-call | tf_op jit(solution)/shard_map/split/pallas_call | solution.py:165
  5.5 11.6 %all-to-all-start = ((bf16[64,16,256]{2,1,0:T(8,128)(2,1)}), bf16[64,16,256]{2,1,0:T(8,128)(2,1)S(1)}, u32[]{:S(2)}, u32[]{:S(2)}) async-start(bf16[64,16,256]{2,1,0:T(8,128)(2,1)} %split.1), calls=%async_computation | async-start | bytes 1048576 | tf_op jit(solution)/shard_map/all_to_all | solution.py:173
  17.1 0.1 copy.29
  17.2 1.2 select_reduce_fusion.1
  18.5 1.2 select_reduce_fusion
  19.8 0.1 fusion.sel_ref
  19.9 14.5 %all-to-all-done.recv_ref = bf16[64,16,256]{2,1,0:T(8,128)(2,1)S(1)} async-done(((bf16[64,16,256]{2,1,0:T(8,128)(2,1)}), bf16[64,16,256]{2,1,0:T(8,128)(2,1)S(1)}, u32[]{:S(2)}, u32[]{:S(2)}) %all-to-all-start) | async-done | bytes 524320 | tf_op jit(solution)/shard_map/all_to_all | solution.py:173
  34.4 1.4 %weight_taps.1 = (f32[1152,128]{1,0:T(8,128)S(1)}, bf16[16,64,128]{2,1,0:T(8,128)(2,1)S(1)}, bf16[16,64,128]{2,1,0:T(8,128)(2,1)S(1)}) custom-call(bf16[64,16,256]{2,1,0:T(8,128)(2,1)S(1)} %all-to-all-done.recv_ref, bf16[8,64,64]{2,1,0:T(8,128)(2,1)S(1)} %fusion.sel_ref), custom_call_target="tpu_custom_call" | custom-call | tf_op jit(solution)/shard_map/weight_taps/pallas_call | solution.py:178
  35.8 20.8 %all_to_all.25 = f32[16,72,128]{2,1,0:T(8,128)S(1)} all-to-all(f32[16,72,128]{2,1,0:T(8,128)S(1)} %bitcast.23), channel_id=1, replica_groups={{0,4,8,12,16,20,24,28,32,36,40,44,48,52,56,60},{1,5,9,13,17,21,25,29,33..., dimensions={0} | all-to-all | bytes 1179648 | tf_op jit(solution)/shard_map/all_to_all | solution.py:194
  56.6 19.5 %all_to_all.26 = f32[8,72,128]{2,1,0:T(8,128)S(1)} all-to-all(f32[8,72,128]{2,1,0:T(8,128)S(1)} %broadcast_in_dim.45), channel_id=1, replica_groups=mesh['dp'=8,'tile'=64] {'dp'}, dimensions={0} | all-to-all | bytes 589824 | tf_op jit(solution)/shard_map/all_to_all | solution.py:198
  76.2 0.9 broadcast_in_dim.46
  77.1 9.2 %all-to-all-start.4 = ((bf16[32,72,128]{2,1,0:T(8,128)(2,1)}), bf16[32,72,128]{2,1,0:T(8,128)(2,1)S(1)}, u32[]{:S(2)}, u32[]{:S(2)}) async-start(bf16[32,72,128]{2,1,0:T(8,128)(2,1)} %broadcast_in_dim.46), calls=%async_computation.4 | async-start | bytes 1179648 | tf_op jit(solution)/shard_map/all_to_all | solution.py:202
  86.4 1.6 %copy.32 = bf16[3,3,256,256]{2,3,1,0:T(8,128)(2,1)S(1)} copy(bf16[3,3,256,256]{3,2,1,0:T(8,128)(2,1)} %param.8) | data formatting | bytes 2359296 | tf_op args[2]
  88.0 0.1 maximum_select_fusion.1
  88.1 0.3 copy.33.wo_ref
  88.4 0.2 dynamic-slice_bitcast_fusion
  88.7 4.8 %collective-permute-start = (bf16[16,64,128]{2,1,0:T(8,128)(2,1)S(1)}, bf16[16,64,128]{2,1,0:T(8,128)(2,1)S(1)}, u32[]{:S(2)}, u32[]{:S(2)}) collective-permute-start(bf16[16,64,128]{2,1,0:T(8,128)(2,1)S(1)} %get-tuple-element.8.xa_ref), channel_id=1, source_target_pairs={{0,1},{1,0},{2,3},{3,2},{4,5},{5,4},{6,7},{7,6},{8,9},{9,8},{10,11... | collective-permute-start | bytes 786440 | tf_op jit(solution)/shard_map/ppermute | solution.py:215
  93.5 3.4 %collective-permute-start.1 = (bf16[16,64,128]{2,1,0:T(8,128)(2,1)S(1)}, bf16[16,64,128]{2,1,0:T(8,128)(2,1)S(1)}, u32[]{:S(2)}, u32[]{:S(2)}) collective-permute-start(bf16[16,64,128]{2,1,0:T(8,128)(2,1)S(1)} %get-tuple-element.9.ga_ref), channel_id=1, source_target_pairs={{0,2},{1,3},{2,0},{3,1},{4,6},{5,7},{6,4},{7,5},{8,10},{9,11},{10,... | collective-permute-start | bytes 786440 | tf_op jit(solution)/shard_map/ppermute | solution.py:216
  96.9 0.9 fusion.1
  97.8 2.6 %all-to-all-done.4 = bf16[32,72,128]{2,1,0:T(8,128)(2,1)S(1)} async-done(((bf16[32,72,128]{2,1,0:T(8,128)(2,1)}), bf16[32,72,128]{2,1,0:T(8,128)(2,1)S(1)}, u32[]{:S(2)}, u32[]{:S(2)}) %all-to-all-start.4) | async-done | bytes 589856 | tf_op jit(solution)/shard_map/all_to_all | solution.py:202
  100.4 8.3 %collective-permute-start.2 = (bf16[32,72,128]{2,1,0:T(8,128)(2,1)S(1)}, bf16[32,72,128]{2,1,0:T(8,128)(2,1)S(1)}, u32[]{:S(2)}, u32[]{:S(2)}) collective-permute-start(bf16[32,72,128]{2,1,0:T(8,128)(2,1)S(1)} %all-to-all-done.4), channel_id=1, source_target_pairs={{0,1},{1,0},{2,3},{3,2},{4,5},{5,4},{6,7},{7,6},{8,9},{9,8},{10,11... | collective-permute-start | bytes 1769480 | tf_op jit(solution)/shard_map/ppermute | solution.py:206
  108.7 1.4 %maximum_select_fusion.wg_ref = bf16[9,256,64]{2,1,0:T(8,128)(2,1)S(1)} fusion(bf16[9,128,64]{2,1,0:T(8,128)(2,1)} %get-tuple-element.27, bf16[9,128,64]{2,1,0:T(8,128)(2,1)} %get-tuple-element.26, pred[]{:T(512)S(6)} %eq.70, bf16[9,256,256]{1,2,0:T(8,128)(2,1)S(1)} %bitcast.30, s32[]{:T(128)S(6)} %select_n.59), kind=kLoop, calls=%fused_computation.1 | loop fusion | flops 737280 | bytes 884741 | tf_op jit(solution)/shard_map/jit(_where)/select_n | solution.py:222
  110.1 3.5 %conv_taps.1 = bf16[64,16,128]{2,1,0:T(8,128)(2,1)S(1)} custom-call(bf16[16,64,128]{2,1,0:T(8,128)(2,1)S(1)} %get-tuple-element.8.xa_ref, bf16[16,64,128]{2,1,0:T(8,128)(2,1)S(1)} %collective-permute-done.xb_ref, bf16[16,64,128]{2,1,0:T(8,128)(2,1)S(1)} %get-tuple-element.9.ga_ref, bf16[16,64,128]{2,1,0:T(8,128)(2,1)S(1)} %collective-permute-done.1.gb_ref, ...), custom_call_target="tpu_custom_call" | custom-call | tf_op jit(solution)/shard_map/conv_taps/pallas_call | solution.py:226
  113.6 18.1 %all_to_all.27.recv_ref = bf16[64,16,128]{2,1,0:T(8,128)(2,1)S(1)} all-to-all(bf16[64,16,128]{2,1,0:T(8,128)(2,1)S(1)} %conv_taps.1), channel_id=1, replica_groups=mesh['dp'=8,'tile'=64] {'tile'}, dimensions={0} | all-to-all | bytes 524288 | tf_op jit(solution)/shard_map/all_to_all | solution.py:235
  131.7 1.6 %join.1 = (bf16[256,256]{1,0:T(8,128)(2,1)}, bf16[256,256]{1,0:T(8,128)(2,1)}) custom-call(s32[2]{0:T(128)S(1)} %pad_add_fusion.place_ref, bf16[64,16,128]{2,1,0:T(8,128)(2,1)S(1)} %all_to_all.27.recv_ref, s32[1,64]{1,0:T(1,128)S(1)} %copy-done.3), custom_call_target="tpu_custom_call" | custom-call | tf_op jit(solution)/shard_map/join/pallas_call | solution.py:236
  133.3 0.3 copy.34
  133.7 0.3 copy.35
  134.0 0.1 pad_maximum_fusion
  134.1 1.5 %copy.36 = bf16[3,3,256,256]{3,2,1,0:T(8,128)(2,1)} copy(bf16[3,3,256,256]{2,3,1,0:T(8,128)(2,1)S(1)} %pad_maximum_fusion) | data formatting | bytes 2359296
  (22 shorter events, 0.5 us)
Async XLA Ops:
  0.6 16.6 %copy-start.3 = (s32[1,64]{1,0:T(1,128)S(1)}, s32[1,64]{1,0:T(1,128)}, u32[]{:S(2)}) copy-start(s32[1,64]{1,0:T(1,128)} %owner_ref.3) | copy-start | bytes 772
  0.6 16.5 %copy-start.4 = (s32[1,64,8]{1,2,0:T(8,128)S(1)}, s32[1,64,8]{1,2,0:T(8,128)}, u32[]{:S(2)}) copy-start(s32[1,64,8]{1,2,0:T(8,128)} %param.10) | copy-start | bytes 6148
  1.4 0.9 copy-start
  2.3 0.9 copy-start.1
  3.2 0.7 copy-start.2
  5.5 29.0 %all-to-all-start = ((bf16[64,16,256]{2,1,0:T(8,128)(2,1)}), bf16[64,16,256]{2,1,0:T(8,128)(2,1)S(1)}, u32[]{:S(2)}, u32[]{:S(2)}) async-start(bf16[64,16,256]{2,1,0:T(8,128)(2,1)} %split.1), calls=%async_computation | async-start | bytes 1048576 | tf_op jit(solution)/shard_map/all_to_all | solution.py:173
  77.1 23.3 %all-to-all-start.4 = ((bf16[32,72,128]{2,1,0:T(8,128)(2,1)}), bf16[32,72,128]{2,1,0:T(8,128)(2,1)S(1)}, u32[]{:S(2)}, u32[]{:S(2)}) async-start(bf16[32,72,128]{2,1,0:T(8,128)(2,1)} %broadcast_in_dim.46), calls=%async_computation.4 | async-start | bytes 1179648 | tf_op jit(solution)/shard_map/all_to_all | solution.py:202
  88.7 21.4 %collective-permute-start = (bf16[16,64,128]{2,1,0:T(8,128)(2,1)S(1)}, bf16[16,64,128]{2,1,0:T(8,128)(2,1)S(1)}, u32[]{:S(2)}, u32[]{:S(2)}) collective-permute-start(bf16[16,64,128]{2,1,0:T(8,128)(2,1)S(1)} %get-tuple-element.8.xa_ref), channel_id=1, source_target_pairs={{0,1},{1,0},{2,3},{3,2},{4,5},{5,4},{6,7},{7,6},{8,9},{9,8},{10,11... | collective-permute-start | bytes 786440 | tf_op jit(solution)/shard_map/ppermute | solution.py:215
  93.5 16.6 %collective-permute-start.1 = (bf16[16,64,128]{2,1,0:T(8,128)(2,1)S(1)}, bf16[16,64,128]{2,1,0:T(8,128)(2,1)S(1)}, u32[]{:S(2)}, u32[]{:S(2)}) collective-permute-start(bf16[16,64,128]{2,1,0:T(8,128)(2,1)S(1)} %get-tuple-element.9.ga_ref), channel_id=1, source_target_pairs={{0,2},{1,3},{2,0},{3,1},{4,6},{5,7},{6,4},{7,5},{8,10},{9,11},{10,... | collective-permute-start | bytes 786440 | tf_op jit(solution)/shard_map/ppermute | solution.py:216
  100.4 32.9 %collective-permute-start.2 = (bf16[32,72,128]{2,1,0:T(8,128)(2,1)S(1)}, bf16[32,72,128]{2,1,0:T(8,128)(2,1)S(1)}, u32[]{:S(2)}, u32[]{:S(2)}) collective-permute-start(bf16[32,72,128]{2,1,0:T(8,128)(2,1)S(1)} %all-to-all-done.4), channel_id=1, source_target_pairs={{0,1},{1,0},{2,3},{3,2},{4,5},{5,4},{6,7},{7,6},{8,9},{9,8},{10,11... | collective-permute-start | bytes 1769480 | tf_op jit(solution)/shard_map/ppermute | solution.py:206

commit v2 on v1

v2 whole, which is shorter than its diff:
```python
import functools
import math

import jax
import jax.numpy as jnp
from jax import lax
from jax.experimental import pallas as pl
from jax.experimental.pallas import tpu as pltpu
from jax.sharding import PartitionSpec as P

SPAN = 4
CELLS = SPAN * SPAN
CLASSES = SPAN * SPAN
PAD = SPAN + 2
HALF = 128
QUARTER = 64
ROWS = 8
COLUMNS = 4
BACK_ROWS = COLUMNS * 2 * CELLS
PIECE_ROWS = 80
bf16, f32 = jnp.bfloat16, jnp.float32


def device_of(m, hi, ho):
    return ho * 32 + m * 2 + hi


def vmem(n):
    return [pl.BlockSpec(memory_space=pltpu.VMEM)] * n


PARAMS = pltpu.CompilerParams(vmem_limit_bytes=24 * 1024 * 1024)


def live_mask(owner, device, count):
    positions = lax.broadcasted_iota(jnp.int32, owner.shape, 1)
    held = jnp.sum(jnp.where(owner == device, positions, 0).astype(f32), axis=1, keepdims=True)
    return held < count.astype(f32)


def class_order(transposed):
    n = CLASSES * CELLS
    o = lax.broadcasted_iota(jnp.int32, (n, n), 1 if transposed else 0)
    c = lax.broadcasted_iota(jnp.int32, (n, n), 0 if transposed else 1)
    mr, mc, r, k = o >> 6, (o >> 4) & 3, (o >> 2) & 3, o & 3
    return c == (r * SPAN + mr) * 16 + k * SPAN + mc


def swap16():
    o = lax.broadcasted_iota(jnp.int32, (256, 256), 0)
    c = lax.broadcasted_iota(jnp.int32, (256, 256), 1)
    return jnp.where(c == ((o & 15) << 4) + (o >> 4), 1.0, 0.0).astype(bf16)


def dot(a, b):
    return jnp.dot(a, b, preferred_element_type=f32)


def split_kernel(place_ref, owner_hbm, x_hbm, g_hbm, send_ref, owner_ref, x_ref, g_ref, sems):
    pairs = [(owner_hbm, owner_ref), (x_hbm, x_ref), (g_hbm, g_ref)]
    copies = [pltpu.make_async_copy(src, dst, sems.at[n]) for n, (src, dst) in enumerate(pairs)]
    for copy in copies:
        copy.start()
    order = class_order(False)
    for copy in copies:
        copy.wait()
    live = live_mask(owner_ref[...], place_ref[0], place_ref[1])
    order = jnp.where(order & live, 1.0, 0.0).astype(bf16)
    x = dot(order, x_ref[...]).astype(bf16)
    g = dot(order, g_ref[...]).astype(bf16)
    for m in range(CLASSES):
        rows = slice(m * CELLS, (m + 1) * CELLS)
        for ho in range(2):
            chip = device_of(m, 0, ho) // 2
            send_ref[chip, :, : 2 * HALF] = x[rows]
            send_ref[chip, :, 2 * HALF :] = g[rows]


def surround(padded, cells, sel_ref):
    def put(d, sources, targets):
        width = cells[0].shape[1]
        got = dot(sel_ref[d], jnp.concatenate([cells[s] for s in sources], axis=1)).astype(bf16)
        for n, (r, c) in enumerate(targets):
            padded[r * PAD + c] = got[:, n * width : (n + 1) * width]

    for r in range(SPAN):
        for c in range(SPAN):
            padded[(r + 1) * PAD + c + 1] = cells[r * SPAN + c]
    last, side = SPAN - 1, range(SPAN)
    put(0, [last * SPAN + last], [(0, 0)])
    put(1, [last * SPAN + c for c in side], [(0, c + 1) for c in side])
    put(2, [last * SPAN], [(0, PAD - 1)])
    put(3, [r * SPAN + last for r in side], [(r + 1, 0) for r in side])
    put(4, [r * SPAN for r in side], [(r + 1, PAD - 1) for r in side])
    put(5, [last], [(PAD - 1, 0)])
    put(6, [c for c in side], [(PAD - 1, c + 1) for c in side])
    put(7, [0], [(PAD - 1, PAD - 1)])


def window(padded, a, b):
    rows = [padded[(r + a) * PAD + c + b] for r in range(SPAN) for c in range(SPAN)]
    return jnp.concatenate(rows, axis=0)


def weight_kernel(place_ref, own_ref, other_ref, sel_ref, sum_ref, x_ref, g_ref, padded):
    swap = swap16()
    chips = own_ref.shape[0]
    for n, ref in enumerate((own_ref, other_ref)):
        for k in range(0, chips, 16):
            turned = dot(swap, ref[k : k + 16].reshape(256, 4 * HALF)).astype(bf16)
            tiles = slice(n * chips + k, n * chips + k + 16)
            for s in range(CELLS):
                x_ref[s, tiles, :] = turned[s * 16 : (s + 1) * 16, : 2 * HALF]
                g_ref[s, tiles, :] = turned[s * 16 : (s + 1) * 16, 2 * HALF :]
    device = place_ref[0]
    low_x, low_g = device % 2 == 0, device < chips
    x = [jnp.where(low_x, x_ref[s, :, :HALF], x_ref[s, :, HALF:]) for s in range(CELLS)]
    surround(padded, x, sel_ref)
    grad = jnp.where(low_g, g_ref[:, :, :HALF], g_ref[:, :, HALF:]).reshape(-1, HALF).T
    for a in range(3):
        for b in range(3):
            tap = a * 3 + b
            sum_ref[tap * HALF : (tap + 1) * HALF, :] = dot(grad, window(padded, a, b)).T


def conv_kernel(place_ref, x_ref, g_ref, sel_ref, wo_ref, wg_ref, own_ref, other_ref, padded):
    tiles = x_ref.shape[1]

    def taps(cells_ref, w_ref, flip):
        surround(padded, [cells_ref[s] for s in range(CELLS)], sel_ref)
        total = jnp.zeros((CELLS * tiles, QUARTER), f32)
        for a in range(3):
            for b in range(3):
                view = window(padded, 2 - a, 2 - b) if flip else window(padded, a, b)
                total = total + dot(view, w_ref[a * 3 + b])
        return total

    forward = taps(x_ref, wo_ref, False)
    backward = taps(g_ref, wg_ref, True)
    both = jnp.concatenate([forward, backward], axis=1).astype(bf16)
    swap = swap16()
    column = place_ref[0] // (2 * ROWS)
    chips = tiles // 2
    for n, ref in enumerate((own_ref, other_ref)):
        for k in range(0, chips, 16):
            begin = n * chips + k
            rows = [both[s * tiles + begin : s * tiles + begin + 16] for s in range(CELLS)]
            turned = dot(swap, jnp.concatenate(rows, axis=0)).astype(bf16).reshape(16, CELLS, 2 * QUARTER)
            for half in range(16 // ROWS):
                there = (k // ROWS + half) ^ column
                ref[pl.ds(there, 1)] = turned[half * ROWS : (half + 1) * ROWS][None]


def pack_kernel(scale, back_ref, parts_ref, out_ref):
    total = parts_ref[0]
    for s in range(1, parts_ref.shape[0]):
        total = total + parts_ref[s]
    piece = (total * scale).astype(bf16)
    piece = jnp.concatenate([piece, jnp.zeros((PIECE_ROWS - piece.shape[0], HALF), bf16)], axis=0)
    for y in range(ROWS):
        for n in range(back_ref.shape[0]):
            for i in range(2):
                begin = (n * 2 + i) * CELLS
                out_ref[y, begin : begin + CELLS, :] = back_ref[n, i, y]
        out_ref[y, BACK_ROWS:, :] = piece


def join_kernel(place_ref, recv_ref, owner_ref, out_ref, grad_ref):
    live = live_mask(owner_ref[...], place_ref[0], place_ref[1])
    order = jnp.where(class_order(True) & live, 1.0, 0.0).astype(bf16)

    column, core = place_ref[0] // (2 * ROWS), place_ref[0] % 2
    classes = []
    for m in range(CLASSES):
        quarters = []
        for hi in range(2):
            for ho in range(2):
                chip = device_of(m, 0, ho) // 2
                slot = ((chip // ROWS) ^ column) * 2 + (hi ^ core)
                begin = pl.multiple_of(slot * CELLS, CELLS)
                quarters.append(recv_ref[chip % ROWS, pl.ds(begin, CELLS), :])
        classes.append(quarters)

    def join(low):
        rows = [jnp.concatenate([part[:, low : low + QUARTER] for part in parts], axis=1) for parts in classes]
        return dot(order, jnp.concatenate(rows, axis=0)).astype(bf16)

    out_ref[...] = join(0)
    grad_ref[...] = join(QUARTER)


def rows_kernel(place_ref, mine_ref, other_ref, out_ref):
    low = place_ref[0] % 2 == 0
    for tap in range(mine_ref.shape[1]):
        mine = jnp.concatenate([mine_ref[0, tap], mine_ref[1, tap]], axis=1)
        other = jnp.concatenate([other_ref[0, tap], other_ref[1, tap]], axis=1)
        out_ref[tap, :HALF, :] = jnp.where(low, mine, other)
        out_ref[tap, HALF:, :] = jnp.where(low, other, mine)


def neighbour_table(owner, neighbors, names):
    positions = jnp.arange(owner.shape[0], dtype=jnp.int32)
    beside = jnp.sum(jnp.where(neighbors[:, :, None] == positions, owner + 1, 0), axis=2) - 1
    peer = jnp.sum(jnp.where((owner == names[:, None])[:, :, None], beside[None], 0), axis=1)
    return (peer.T[:, :, None] == names).astype(bf16)


def local(features, cotangent, weight, tile_owner, tile_neighbors, tile_counts):
    tiles = lax.axis_size("tile")
    slides = lax.axis_size("dp")
    device = lax.axis_index("tile")
    hi, ho = device % 2, device // (tiles // 2)
    width = features.shape[-1]
    cells = features.shape[2] * features.shape[3]
    place = jnp.stack([device, tile_counts[0]])
    smem = pl.BlockSpec(memory_space=pltpu.SMEM)
    hbm = pl.BlockSpec(memory_space=pltpu.HBM)

    chips = tiles // 2
    core = [(j, j ^ 1) for j in range(tiles)]
    same_core = [[2 * c + i for c in range(chips)] for i in range(2)]
    send = pl.pallas_call(
        split_kernel,
        out_shape=jax.ShapeDtypeStruct((chips, CELLS, 4 * HALF), bf16),
        in_specs=[smem, hbm, hbm, hbm],
        out_specs=vmem(1)[0],
        scratch_shapes=[
            pltpu.VMEM((1, tiles), jnp.int32),
            pltpu.VMEM((cells, width), bf16),
            pltpu.VMEM((cells, width), bf16),
            pltpu.SemaphoreType.DMA((3,)),
        ],
        name="split",
    )(place, tile_owner, features.reshape(cells, width), cotangent.reshape(cells, width))
    own = lax.all_to_all(send, "tile", 0, 0, tiled=True, axis_index_groups=same_core)

    side = jnp.arange(chips, dtype=jnp.int32) * 2
    names = jnp.concatenate([side + hi, side + 1 - hi])
    sel = neighbour_table(tile_owner[0], tile_neighbors[0], names)
    taps = weight.shape[0] * weight.shape[1]
    quarter = (2 * hi + ho) * QUARTER
    flat = weight.reshape(taps, width, width)
    w_out = lax.dynamic_slice_in_dim(flat, quarter, QUARTER, axis=2)
    w_grad = lax.dynamic_slice_in_dim(flat, quarter, QUARTER, axis=1).transpose(0, 2, 1)
    own, sel, w_out, w_grad = lax.optimization_barrier((own, sel, w_out, w_grad))
    other = lax.ppermute(own, "tile", core)

    block = (CELLS, tiles, width)
    partial, x, g = pl.pallas_call(
        weight_kernel,
        out_shape=[
            jax.ShapeDtypeStruct((taps * HALF, HALF), f32),
            jax.ShapeDtypeStruct(block, bf16),
            jax.ShapeDtypeStruct(block, bf16),
        ],
        in_specs=[smem, *vmem(3)],
        out_specs=vmem(3),
        scratch_shapes=[pltpu.VMEM((PAD * PAD, tiles, HALF), bf16)],
        compiler_params=PARAMS,
        name="weight_taps",
    )(place, own, other, sel)

    groups = [[device_of(m, i, o) for m in range(CLASSES)] for o in range(2) for i in range(2)]
    rows = taps * HALF // CLASSES
    parts = lax.all_to_all(
        partial.reshape(CLASSES, rows, HALF), "tile", 0, 0, tiled=True, axis_index_groups=groups
    )
    outgoing = jax.ShapeDtypeStruct((COLUMNS, ROWS, CELLS, 2 * QUARTER), bf16)
    back_own, back_other = pl.pallas_call(
        conv_kernel,
        out_shape=[outgoing, outgoing],
        in_specs=[smem, *vmem(5)],
        out_specs=vmem(2),
        scratch_shapes=[pltpu.VMEM((PAD * PAD, tiles, width), bf16)],
        compiler_params=PARAMS,
        name="conv_taps",
    )(place, x, g, sel, w_out, w_grad)
    back_other = lax.ppermute(back_other, "tile", core)
    back = jnp.stack([back_own, back_other], axis=1)
    turned = [back[0]]
    for n in range(1, COLUMNS):
        turned.append(lax.ppermute(back[n], "tile", [(j, j ^ (n * 2 * ROWS)) for j in range(tiles)]))
    back = jnp.stack(turned)
    parts, back = lax.optimization_barrier((parts, back))

    part = jnp.sum(parts, axis=0)
    parts = lax.all_to_all(jnp.broadcast_to(part, (slides, rows, HALF)), "dp", 0, 0, tiled=True)
    scale = 1.0 / math.sqrt(slides * tiles * cells)
    along_y = [[(x * ROWS + y) * 2 + i for y in range(ROWS)] for x in range(COLUMNS) for i in range(2)]
    along_x = [[(x * ROWS + y) * 2 + i for x in range(COLUMNS)] for y in range(ROWS) for i in range(2)]
    packed = pl.pallas_call(
        functools.partial(pack_kernel, scale),
        out_shape=jax.ShapeDtypeStruct((ROWS, BACK_ROWS + PIECE_ROWS, HALF), bf16),
        in_specs=vmem(2),
        out_specs=vmem(1)[0],
        compiler_params=PARAMS,
        name="pack",
    )(back, parts)
    packed = lax.all_to_all(packed, "tile", 0, 0, tiled=True, axis_index_groups=along_y)
    column = packed[:, BACK_ROWS : BACK_ROWS + rows]
    mine = lax.all_to_all(
        jnp.broadcast_to(column, (COLUMNS, ROWS, rows, HALF)), "tile", 0, 0, tiled=True, axis_index_groups=along_x
    )
    other = lax.ppermute(mine, "tile", core)
    halves = (2, taps, HALF, HALF)
    grad_weight = pl.pallas_call(
        rows_kernel,
        out_shape=jax.ShapeDtypeStruct((taps, width, width), bf16),
        in_specs=[smem, *vmem(2)],
        out_specs=vmem(1)[0],
        compiler_params=PARAMS,
        name="rows",
    )(place, mine.reshape(halves), other.reshape(halves)).reshape(weight.shape)

    out, grad = pl.pallas_call(
        join_kernel,
        out_shape=[jax.ShapeDtypeStruct((cells, width), bf16)] * 2,
        in_specs=[smem, *vmem(2)],
        out_specs=vmem(2),
        compiler_params=PARAMS,
        name="join",
    )(place, packed, tile_owner)
    return out.reshape(features.shape), grad.reshape(features.shape), grad_weight


def solution(mesh):
    return jax.shard_map(
        local,
        mesh=mesh,
        in_specs=(
            P("dp", "tile", None, None, None),
            P("dp", "tile", None, None, None),
            P(),
            P("dp", None),
            P("dp", None, None),
            P("dp"),
        ),
        out_specs=(P("dp", "tile", None, None, None), P("dp", "tile", None, None, None), P()),
        check_vma=False,
    )
```

time: 136 us -> 124 us (0.912)
  blocking collectives: 58.3 us -> 46.4 us
  local copies, waits for them, and re-layouts: 8.82 us -> 2.36 us
  Pallas kernels: 8.11 us -> 13.1 us
  starting transfers between devices: 37.4 us -> 41 us
  waiting for transfers between devices: 17.1 us -> 15.7 us
    all_to_all x2, blocking collectives: 38.8 us -> 26.8 us  [the longest x1 17.1 us: local(): lax.all_to_all(packed, 'tile', 0, 0, tiled=True, axis_index_groups=along_y)]
    ppermute x2 -> x5, starting transfers between devices: 8.21 us -> 17.7 us  [the longest x3 9.78 us: local(): lax.ppermute(back[n], 'tile', [(j, j ^ n * 2 * ROWS) for j in range(tiles)])]
    all_to_all x2, waiting for transfers between devices: 17.1 us -> 9.57 us  [the longest x1 9.57 us: local(): lax.all_to_all(send, 'tile', 0, 0, tiled=True, axis_index_groups=same_core)]
    all_to_all x2, starting transfers between devices: 20.9 us -> 14.8 us  [the longest x1 10.5 us: local(): lax.all_to_all(send, 'tile', 0, 0, tiled=True, axis_index_groups=same_core)]
    ppermute x2 -> x5, waiting for transfers between devices: 0.01 us -> 6.07 us  [the longest x3 3.59 us: local(): lax.ppermute(back[n], 'tile', [(j, j ^ n * 2 * ROWS) for j in range(tiles)])]
    unnamed x12 -> x11, local copies, waits for them, and re-layouts: 5.58 us -> 0.76 us
    pallas_call x2 -> x4, Pallas kernels: 5.14 us -> 8.53 us  [the longest x1 4.08 us: local(): pl.pallas_call(conv_kernel, out_shape=[outgoing, outgoing], in_specs=[sme...]
    pallas_call x1, Pallas kernels: 1.38 us -> 2.92 us  [local(): pl.pallas_call(weight_kernel, out_shape=[jax.ShapeDtypeStruct((taps * HAL...]
  transfers between devices with their start and end apart: 5 -> 8, of which waited for: 2 -> 5; matrix products, arithmetic and copies ran while one was open for 5% -> 4% of each run, Pallas kernels for 4% -> 5%
where the time goes in v2:
time: 124 us
  blocking collectives  46.4 us (37%)
  starting transfers between devices  41 us (33%)
  waiting for transfers between devices  15.7 us (13%)
  Pallas kernels  13.1 us (11%)
  other arithmetic  3.38 us (3%)
  local copies, waits for them, and re-layouts  2.36 us (2%)
  between operations  1.68 us (1%)
    all_to_all x1, blocking collectives, local(): lax.all_to_all(jnp.broadcast_to(part, (slides, rows, HALF)), 'dp', 0, 0,...  19.6 us
    all_to_all x1, blocking collectives, local(): lax.all_to_all(packed, 'tile', 0, 0, tiled=True, axis_index_groups=along_y)  17.1 us
    all_to_all x1, starting transfers between devices, local(): lax.all_to_all(send, 'tile', 0, 0, tiled=True, axis_index_groups=same_core)  10.5 us
    ppermute x3, starting transfers between devices, local(): lax.ppermute(back[n], 'tile', [(j, j ^ n * 2 * ROWS) for j in range(tiles)])  9.78 us
    all_to_all x1, blocking collectives, local(): lax.all_to_all(jnp.broadcast_to(column, (COLUMNS, ROWS, rows, HALF)), 'ti...  9.67 us
    all_to_all x1, waiting for transfers between devices, local(): lax.all_to_all(send, 'tile', 0, 0, tiled=True, axis_index_groups=same_core)  9.57 us
    ppermute x1, starting transfers between devices, local(): other = lax.ppermute(mine, 'tile', core)  8.52 us
    ppermute x1, starting transfers between devices, local(): other = lax.ppermute(own, 'tile', core)  5.39 us
  transfers between devices with their start and end apart: 8, of which 5 were waited for; matrix products, arithmetic and copies ran while one was open for 4% of the time, Pallas kernels for 5%

profile of v2, /device:TPU:1, one launch (start us, length us, event | category | flops | bytes accessed | tf_op | source)
XLA Modules:
  0.0 123.6 jit_solution(16674092958159111878)
XLA Ops:
  1.4 0.6 pad_add_fusion.place_ref
  2.0 2.7 %split.1 = bf16[32,16,512]{2,1,0:T(8,128)(2,1)} custom-call(s32[2]{0:T(128)} %pad_add_fusion.place_ref, s32[1,64]{1,0:T(1,128)} %owner_ref.1, bf16[256,256]{1,0:T(8,128)(2,1)} %bitcast.35, bf16[256,256]{1,0:T(8,128)(2,1)} %bitcast.36), custom_call_target="tpu_custom_call" | custom-call | tf_op jit(solution)/shard_map/split/pallas_call | solution.py:222
  4.7 10.5 %all-to-all-start = ((bf16[32,16,512]{2,1,0:T(8,128)(2,1)}), bf16[32,16,512]{2,1,0:T(8,128)(2,1)S(1)}, u32[]{:S(2)}, u32[]{:S(2)}) async-start(bf16[32,16,512]{2,1,0:T(8,128)(2,1)} %split.1), calls=%async_computation | async-start | bytes 1048576 | tf_op jit(solution)/shard_map/all_to_all | solution.py:235
  15.3 0.7 copy.20
  16.1 0.1 copy.17
  16.2 1.2 %select_reduce_fusion.1 = s32[64,8]{1,0:T(8,128)S(1)} fusion(s32[64]{0:T(128)S(1)} %broadcast_add_fusion.1, s32[64,8]{1,0:T(8,128)S(1)} %copy.17), kind=kLoop, calls=%fused_computation.9 | loop fusion | flops 97792 | bytes 4352 | tf_op jit(solution)/shard_map/reduce_sum | solution.py:203
  17.5 0.1 pad_add_fusion.1
  17.7 1.2 select_reduce_fusion
  18.9 0.7 constant_dynamic-slice_fusion
  19.6 0.2 dynamic-slice_bitcast_fusion.wg_ref
  19.9 0.1 compare_convert_fusion.sel_ref
  20.0 9.6 %all-to-all-done.own_ref = bf16[32,16,512]{2,1,0:T(8,128)(2,1)S(1)} async-done(((bf16[32,16,512]{2,1,0:T(8,128)(2,1)}), bf16[32,16,512]{2,1,0:T(8,128)(2,1)S(1)}, u32[]{:S(2)}, u32[]{:S(2)}) %all-to-all-start) | async-done | bytes 524320 | tf_op jit(solution)/shard_map/all_to_all | solution.py:235
  29.6 5.4 %collective-permute-start = (bf16[32,16,512]{2,1,0:T(8,128)(2,1)S(1)}, bf16[32,16,512]{2,1,0:T(8,128)(2,1)S(1)}, u32[]{:S(2)}, u32[]{:S(2)}) collective-permute-start(bf16[32,16,512]{2,1,0:T(8,128)(2,1)S(1)} %all-to-all-done.own_ref), channel_id=1, source_target_pairs={{0,1},{1,0},{2,3},{3,2},{4,5},{5,4},{6,7},{7,6},{8,9},{9,8},{10,11... | collective-permute-start | bytes 1572872 | tf_op jit(solution)/shard_map/ppermute | solution.py:246
  35.0 1.5 %collective-permute-done.other_ref = bf16[32,16,512]{2,1,0:T(8,128)(2,1)S(1)} collective-permute-done((bf16[32,16,512]{2,1,0:T(8,128)(2,1)S(1)}, bf16[32,16,512]{2,1,0:T(8,128)(2,1)S(1)}, u32[]{:S(2)}, u32[]{:S(2)}) %collective-permute-start) | collective-permute-done | bytes 524320 | tf_op jit(solution)/shard_map/ppermute | solution.py:246
  36.5 2.9 %weight_taps.1 = (f32[1152,128]{1,0:T(8,128)}, bf16[16,64,256]{2,1,0:T(8,128)(2,1)S(1)}, bf16[16,64,256]{2,1,0:T(8,128)(2,1)S(1)}) custom-call(s32[2]{0:T(128)S(1)} %copy-done, bf16[32,16,512]{2,1,0:T(8,128)(2,1)S(1)} %all-to-all-done.own_ref, bf16[32,16,512]{2,1,0:T(8,128)(2,1)S(1)} %collective-permute-done.other_ref, ...), custom_call_target="tpu_custom_call" | custom-call | tf_op jit(solution)/shard_map/weight_taps/pallas_call | solution.py:249
  39.4 4.3 %all-to-all-start.1 = ((f32[16,72,128]{2,1,0:T(8,128)}), f32[16,72,128]{2,1,0:T(8,128)S(1)}, u32[]{:S(2)}, u32[]{:S(2)}) async-start(f32[16,72,128]{2,1,0:T(8,128)} %bitcast.8), calls=%async_computation.1 | async-start | bytes 1179648 | tf_op jit(solution)/shard_map/all_to_all | solution.py:265
  43.7 0.3 copy.21.wo_ref
  44.0 4.1 %conv_taps.1 = (bf16[4,8,16,128]{3,2,1,0:T(8,128)(2,1)S(1)}, bf16[4,8,16,128]{3,2,1,0:T(8,128)(2,1)S(1)}) custom-call(s32[2]{0:T(128)S(1)} %copy-done, bf16[16,64,256]{2,1,0:T(8,128)(2,1)S(1)} %get-tuple-element.19.x_ref, bf16[16,64,256]{2,1,0:T(8,128)(2,1)S(1)} %get-tuple-element.20.g_ref, bf16[8,64,64]{2,1,0:T(8,128)(2,1)S(1)} %compare_convert_fusion.sel_ref, ...), custom_call_target="tpu_custom_call" | custom-call | tf_op jit(solution)/shard_map/conv_taps/pallas_call | solution.py:269
  48.1 2.6 %collective-permute-start.1 = (bf16[4,8,16,128]{3,2,1,0:T(8,128)(2,1)S(1)}, bf16[4,8,16,128]{3,2,1,0:T(8,128)(2,1)S(1)}, u32[]{:S(2)}, u32[]{:S(2)}) collective-permute-start(bf16[4,8,16,128]{3,2,1,0:T(8,128)(2,1)S(1)} %get-tuple-element.24), channel_id=1, source_target_pairs={{0,1},{1,0},{2,3},{3,2},{4,5},{5,4},{6,7},{7,6},{8,9},{9,8},{10,11... | collective-permute-start | bytes 393224 | tf_op jit(solution)/shard_map/ppermute | solution.py:278
  50.7 1.0 collective-permute-done.1
  51.7 3.6 %collective-permute-start.2 = (bf16[2,8,16,128]{3,2,1,0:T(8,128)(2,1)S(1)}, bf16[2,8,16,128]{3,2,1,0:T(8,128)(2,1)S(1)}, u32[]{:S(2)}, u32[]{:S(2)}) collective-permute-start(bf16[2,8,16,128]{3,2,1,0:T(8,128)(2,1)S(1)} %get-tuple-element.30), channel_id=1, source_target_pairs={{0,16},{1,17},{2,18},{3,19},{4,20},{5,21},{6,22},{7,23},{8,24},{9,... | collective-permute-start | bytes 196616 | tf_op jit(solution)/shard_map/ppermute | solution.py:282
  55.2 3.6 %collective-permute-start.3 = (bf16[2,8,16,128]{3,2,1,0:T(8,128)(2,1)S(1)}, bf16[2,8,16,128]{3,2,1,0:T(8,128)(2,1)S(1)}, u32[]{:S(2)}, u32[]{:S(2)}) collective-permute-start(bf16[2,8,16,128]{3,2,1,0:T(8,128)(2,1)S(1)} %get-tuple-element.32), channel_id=1, source_target_pairs={{0,32},{1,33},{2,34},{3,35},{4,36},{5,37},{6,38},{7,39},{8,40},{9,... | collective-permute-start | bytes 196616 | tf_op jit(solution)/shard_map/ppermute | solution.py:282
  58.9 2.6 %collective-permute-start.4 = (bf16[2,8,16,128]{3,2,1,0:T(8,128)(2,1)S(1)}, bf16[2,8,16,128]{3,2,1,0:T(8,128)(2,1)S(1)}, u32[]{:S(2)}, u32[]{:S(2)}) collective-permute-start(bf16[2,8,16,128]{3,2,1,0:T(8,128)(2,1)S(1)} %get-tuple-element.31), channel_id=1, source_target_pairs={{0,48},{1,49},{2,50},{3,51},{4,52},{5,53},{6,54},{7,55},{8,56},{9,... | collective-permute-start | bytes 196616 | tf_op jit(solution)/shard_map/ppermute | solution.py:282
  61.5 0.3 collective-permute-done.3
  61.8 3.3 %collective-permute-done.4 = bf16[2,8,16,128]{3,2,1,0:T(8,128)(2,1)S(1)} collective-permute-done((bf16[2,8,16,128]{3,2,1,0:T(8,128)(2,1)S(1)}, bf16[2,8,16,128]{3,2,1,0:T(8,128)(2,1)S(1)}, u32[]{:S(2)}, u32[]{:S(2)}) %collective-permute-start.4) | collective-permute-done | bytes 65568 | tf_op jit(solution)/shard_map/ppermute | solution.py:282
  65.2 19.6 %all_to_all.25.parts_ref = f32[8,72,128]{2,1,0:T(8,128)S(1)} all-to-all(f32[8,72,128]{2,1,0:T(8,128)S(1)} %broadcast_in_dim.45), channel_id=1, replica_groups=mesh['dp'=8,'tile'=64] {'dp'}, dimensions={0} | all-to-all | bytes 589824 | tf_op jit(solution)/shard_map/all_to_all | solution.py:287
  84.9 17.1 %all_to_all.26.recv_ref = bf16[8,208,128]{2,1,0:T(8,128)(2,1)S(1)} all-to-all(bf16[8,208,128]{2,1,0:T(8,128)(2,1)S(1)} %pack.1), channel_id=1, replica_groups={{0,2,4,6,8,10,12,14},{1,3,5,7,9,11,13,15},{16,18,20,22,24,26,28,30},{17..., dimensions={0} | all-to-all | bytes 851968 | tf_op jit(solution)/shard_map/all_to_all | solution.py:299
  102.0 0.1 broadcast_in_dim.46
  102.1 9.7 %all_to_all.27 = bf16[4,8,72,128]{3,2,1,0:T(8,128)(2,1)S(1)} all-to-all(bf16[4,8,72,128]{3,2,1,0:T(8,128)(2,1)S(1)} %broadcast_in_dim.46), channel_id=1, replica_groups={{0,16,32,48},{1,17,33,49},{2,18,34,50},{3,19,35,51},{4,20,36,52},{5,21,..., dimensions={0} | all-to-all | bytes 1179648 | tf_op jit(solution)/shard_map/all_to_all | solution.py:301
  111.8 8.5 %collective-permute-start.5 = (bf16[4,8,72,128]{3,2,1,0:T(8,128)(2,1)S(1)}, bf16[4,8,72,128]{3,2,1,0:T(8,128)(2,1)S(1)}, u32[]{:S(2)}, u32[]{:S(2)}) collective-permute-start(bf16[4,8,72,128]{3,2,1,0:T(8,128)(2,1)S(1)} %all_to_all.27), channel_id=1, source_target_pairs={{0,1},{1,0},{2,3},{3,2},{4,5},{5,4},{6,7},{7,6},{8,9},{9,8},{10,11... | collective-permute-start | bytes 1769480 | tf_op jit(solution)/shard_map/ppermute | solution.py:304
  120.3 1.6 %join.1 = (bf16[256,256]{1,0:T(8,128)(2,1)}, bf16[256,256]{1,0:T(8,128)(2,1)}) custom-call(s32[2]{0:T(128)S(1)} %copy-done, bf16[8,208,128]{2,1,0:T(8,128)(2,1)S(1)} %all_to_all.26.recv_ref, s32[1,64]{1,0:T(1,128)S(1)} %copy-done.1), custom_call_target="tpu_custom_call" | custom-call | tf_op jit(solution)/shard_map/join/pallas_call | solution.py:315
  121.9 1.7 %rows.1 = bf16[9,256,256]{2,1,0:T(8,128)(2,1)} custom-call(s32[2]{0:T(128)S(1)} %copy-done, bf16[2,9,128,128]{3,2,1,0:T(8,128)(2,1)S(1)} %bitcast.27, bf16[2,9,128,128]{3,2,1,0:T(8,128)(2,1)S(1)} %bitcast.28), custom_call_target="tpu_custom_call" | custom-call | tf_op jit(solution)/shard_map/rows/pallas_call | solution.py:306
  (25 shorter events, 0.4 us)
Async XLA Ops:
  0.6 14.7 %copy-start.1 = (s32[1,64]{1,0:T(1,128)S(1)}, s32[1,64]{1,0:T(1,128)}, u32[]{:S(2)}) copy-start(s32[1,64]{1,0:T(1,128)} %owner_ref.1) | copy-start | bytes 772
  0.6 14.7 %copy-start.3 = (bf16[3,3,256,256]{3,2,1,0:T(8,128)(2,1)S(1)}, bf16[3,3,256,256]{3,2,1,0:T(8,128)(2,1)}, u32[]{:S(2)}) copy-start(bf16[3,3,256,256]{3,2,1,0:T(8,128)(2,1)} %param.8) | copy-start | bytes 3538948
  4.7 24.8 %all-to-all-start = ((bf16[32,16,512]{2,1,0:T(8,128)(2,1)}), bf16[32,16,512]{2,1,0:T(8,128)(2,1)S(1)}, u32[]{:S(2)}, u32[]{:S(2)}) async-start(bf16[32,16,512]{2,1,0:T(8,128)(2,1)} %split.1), calls=%async_computation | async-start | bytes 1048576 | tf_op jit(solution)/shard_map/all_to_all | solution.py:235
  15.3 0.8 copy-start.4
  16.1 20.4 %copy-start = (s32[2]{0:T(128)S(1)}, s32[2]{0:T(128)}, u32[]{:S(2)}) copy-start(s32[2]{0:T(128)} %pad_add_fusion.place_ref) | copy-start | bytes 28
  20.0 23.7 %copy-start.2 = (bf16[9,256,64]{1,2,0:T(8,128)(2,1)S(1)}, bf16[9,256,64]{1,2,0:T(8,128)(2,1)}, u32[]{:S(2)}) copy-start(bf16[9,256,64]{1,2,0:T(8,128)(2,1)} %constant_dynamic-slice_fusion) | copy-start | bytes 884740
  29.6 6.9 %collective-permute-start = (bf16[32,16,512]{2,1,0:T(8,128)(2,1)S(1)}, bf16[32,16,512]{2,1,0:T(8,128)(2,1)S(1)}, u32[]{:S(2)}, u32[]{:S(2)}) collective-permute-start(bf16[32,16,512]{2,1,0:T(8,128)(2,1)S(1)} %all-to-all-done.own_ref), channel_id=1, source_target_pairs={{0,1},{1,0},{2,3},{3,2},{4,5},{5,4},{6,7},{7,6},{8,9},{9,8},{10,11... | collective-permute-start | bytes 1572872 | tf_op jit(solution)/shard_map/ppermute | solution.py:246
  39.4 25.7 %all-to-all-start.1 = ((f32[16,72,128]{2,1,0:T(8,128)}), f32[16,72,128]{2,1,0:T(8,128)S(1)}, u32[]{:S(2)}, u32[]{:S(2)}) async-start(f32[16,72,128]{2,1,0:T(8,128)} %bitcast.8), calls=%async_computation.1 | async-start | bytes 1179648 | tf_op jit(solution)/shard_map/all_to_all | solution.py:265
  48.1 3.5 %collective-permute-start.1 = (bf16[4,8,16,128]{3,2,1,0:T(8,128)(2,1)S(1)}, bf16[4,8,16,128]{3,2,1,0:T(8,128)(2,1)S(1)}, u32[]{:S(2)}, u32[]{:S(2)}) collective-permute-start(bf16[4,8,16,128]{3,2,1,0:T(8,128)(2,1)S(1)} %get-tuple-element.24), channel_id=1, source_target_pairs={{0,1},{1,0},{2,3},{3,2},{4,5},{5,4},{6,7},{7,6},{8,9},{9,8},{10,11... | collective-permute-start | bytes 393224 | tf_op jit(solution)/shard_map/ppermute | solution.py:278
  51.7 9.8 %collective-permute-start.2 = (bf16[2,8,16,128]{3,2,1,0:T(8,128)(2,1)S(1)}, bf16[2,8,16,128]{3,2,1,0:T(8,128)(2,1)S(1)}, u32[]{:S(2)}, u32[]{:S(2)}) collective-permute-start(bf16[2,8,16,128]{3,2,1,0:T(8,128)(2,1)S(1)} %get-tuple-element.30), channel_id=1, source_target_pairs={{0,16},{1,17},{2,18},{3,19},{4,20},{5,21},{6,22},{7,23},{8,24},{9,... | collective-permute-start | bytes 196616 | tf_op jit(solution)/shard_map/ppermute | solution.py:282
  55.2 6.5 %collective-permute-start.3 = (bf16[2,8,16,128]{3,2,1,0:T(8,128)(2,1)S(1)}, bf16[2,8,16,128]{3,2,1,0:T(8,128)(2,1)S(1)}, u32[]{:S(2)}, u32[]{:S(2)}) collective-permute-start(bf16[2,8,16,128]{3,2,1,0:T(8,128)(2,1)S(1)} %get-tuple-element.32), channel_id=1, source_target_pairs={{0,32},{1,33},{2,34},{3,35},{4,36},{5,37},{6,38},{7,39},{8,40},{9,... | collective-permute-start | bytes 196616 | tf_op jit(solution)/shard_map/ppermute | solution.py:282
  58.9 6.2 %collective-permute-start.4 = (bf16[2,8,16,128]{3,2,1,0:T(8,128)(2,1)S(1)}, bf16[2,8,16,128]{3,2,1,0:T(8,128)(2,1)S(1)}, u32[]{:S(2)}, u32[]{:S(2)}) collective-permute-start(bf16[2,8,16,128]{3,2,1,0:T(8,128)(2,1)S(1)} %get-tuple-element.31), channel_id=1, source_target_pairs={{0,48},{1,49},{2,50},{3,51},{4,52},{5,53},{6,54},{7,55},{8,56},{9,... | collective-permute-start | bytes 196616 | tf_op jit(solution)/shard_map/ppermute | solution.py:282
  111.8 10.1 %collective-permute-start.5 = (bf16[4,8,72,128]{3,2,1,0:T(8,128)(2,1)S(1)}, bf16[4,8,72,128]{3,2,1,0:T(8,128)(2,1)S(1)}, u32[]{:S(2)}, u32[]{:S(2)}) collective-permute-start(bf16[4,8,72,128]{3,2,1,0:T(8,128)(2,1)S(1)} %all_to_all.27), channel_id=1, source_target_pairs={{0,1},{1,0},{2,3},{3,2},{4,5},{5,4},{6,7},{7,6},{8,9},{9,8},{10,11... | collective-permute-start | bytes 1769480 | tf_op jit(solution)/shard_map/ppermute | solution.py:304

commit v3 on v2

v3 whole, which is shorter than its diff:
```python
import functools
import math

import jax
import jax.numpy as jnp
from jax import lax
from jax.experimental import pallas as pl
from jax.experimental.pallas import tpu as pltpu
from jax.sharding import PartitionSpec as P

SPAN = 4
CELLS = SPAN * SPAN
CLASSES = SPAN * SPAN
PAD = SPAN + 2
HALF = 128
QUARTER = 64
ROWS = 8
COLUMNS = 4
PIECE_ROWS = 80
bf16, f32 = jnp.bfloat16, jnp.float32


def device_of(m, hi, ho):
    return ho * 32 + m * 2 + hi


def vmem(n):
    return [pl.BlockSpec(memory_space=pltpu.VMEM)] * n


PARAMS = pltpu.CompilerParams(vmem_limit_bytes=24 * 1024 * 1024)


def live_mask(owner, count):
    device = lax.axis_index("tile")
    positions = lax.broadcasted_iota(jnp.int32, owner.shape, 1)
    held = jnp.sum(jnp.where(owner == device, positions, 0).astype(f32), axis=1, keepdims=True)
    return held < count.astype(f32)


def class_order(transposed):
    n = CLASSES * CELLS
    o = lax.broadcasted_iota(jnp.int32, (n, n), 1 if transposed else 0)
    c = lax.broadcasted_iota(jnp.int32, (n, n), 0 if transposed else 1)
    mr, mc, r, k = o >> 6, (o >> 4) & 3, (o >> 2) & 3, o & 3
    return c == (r * SPAN + mr) * 16 + k * SPAN + mc


def swap16():
    o = lax.broadcasted_iota(jnp.int32, (256, 256), 0)
    c = lax.broadcasted_iota(jnp.int32, (256, 256), 1)
    return jnp.where(c == ((o & 15) << 4) + (o >> 4), 1.0, 0.0).astype(bf16)


def dot(a, b):
    return jnp.dot(a, b, preferred_element_type=f32)


def split_kernel(count_ref, owner_hbm, x_hbm, g_hbm, send_ref, owner_ref, x_ref, g_ref, sems):
    pairs = [(owner_hbm, owner_ref), (x_hbm, x_ref), (g_hbm, g_ref)]
    copies = [pltpu.make_async_copy(src, dst, sems.at[n]) for n, (src, dst) in enumerate(pairs)]
    for copy in copies:
        copy.start()
    order = class_order(False)
    for copy in copies:
        copy.wait()
    live = live_mask(owner_ref[...], count_ref[0])
    order = jnp.where(order & live, 1.0, 0.0).astype(bf16)
    x = dot(order, x_ref[...]).astype(bf16)
    g = dot(order, g_ref[...]).astype(bf16)
    for m in range(CLASSES):
        rows = slice(m * CELLS, (m + 1) * CELLS)
        for ho in range(2):
            chip = device_of(m, 0, ho) // 2
            send_ref[chip, :, : 2 * HALF] = x[rows]
            send_ref[chip, :, 2 * HALF :] = g[rows]


def surround(padded, cells, sel_ref):
    def put(d, sources, targets):
        width = cells[0].shape[1]
        got = dot(sel_ref[d], jnp.concatenate([cells[s] for s in sources], axis=1)).astype(bf16)
        for n, (r, c) in enumerate(targets):
            padded[r * PAD + c] = got[:, n * width : (n + 1) * width]

    for r in range(SPAN):
        for c in range(SPAN):
            padded[(r + 1) * PAD + c + 1] = cells[r * SPAN + c]
    last, side = SPAN - 1, range(SPAN)
    put(0, [last * SPAN + last], [(0, 0)])
    put(1, [last * SPAN + c for c in side], [(0, c + 1) for c in side])
    put(2, [last * SPAN], [(0, PAD - 1)])
    put(3, [r * SPAN + last for r in side], [(r + 1, 0) for r in side])
    put(4, [r * SPAN for r in side], [(r + 1, PAD - 1) for r in side])
    put(5, [last], [(PAD - 1, 0)])
    put(6, [c for c in side], [(PAD - 1, c + 1) for c in side])
    put(7, [0], [(PAD - 1, PAD - 1)])


def window(padded, a, b):
    rows = [padded[(r + a) * PAD + c + b] for r in range(SPAN) for c in range(SPAN)]
    return jnp.concatenate(rows, axis=0)


def by_cell(refs, put, lanes):
    swap = swap16()
    chips = refs[0].shape[0]
    for n, ref in enumerate(refs):
        for k in range(0, chips, 16):
            turned = dot(swap, lanes(ref, k).reshape(256, -1)).astype(bf16)
            for s in range(CELLS):
                put(s, slice(n * chips + k, n * chips + k + 16), turned[s * 16 : (s + 1) * 16])


def weight_kernel(own_ref, other_ref, sel_ref, sum_ref, x_ref, g_ref, padded):
    device = lax.axis_index("tile")
    low_x, low_g = device % 2 == 0, device < own_ref.shape[0]

    def halves(ref, k):
        rows = ref[k : k + 16]
        x = jnp.where(low_x, rows[:, :, :HALF], rows[:, :, HALF : 2 * HALF])
        g = jnp.where(low_g, rows[:, :, 2 * HALF : 3 * HALF], rows[:, :, 3 * HALF :])
        return jnp.concatenate([x, g], axis=2)

    def put(s, tiles, value):
        x_ref[s, tiles, :] = value[:, :HALF]
        g_ref[s, tiles, :] = value[:, HALF:]

    by_cell((own_ref, other_ref), put, halves)
    surround(padded, [x_ref[s] for s in range(CELLS)], sel_ref)
    grad = g_ref[...].reshape(-1, HALF).T
    for a in range(3):
        for b in range(3):
            tap = a * 3 + b
            sum_ref[tap * HALF : (tap + 1) * HALF, :] = dot(grad, window(padded, a, b)).T


def conv_kernel(
    own_in_ref, other_in_ref, sel_ref, wo_ref, wg_ref, own_ref, other_ref, x_ref, g_ref, padded
):
    tiles = x_ref.shape[1]
    width = x_ref.shape[2]

    def put(s, where, value):
        x_ref[s, where, :] = value[:, :width]
        g_ref[s, where, :] = value[:, width:]

    by_cell((own_in_ref, other_in_ref), put, lambda ref, k: ref[k : k + 16])

    def taps(cells_ref, w_ref, flip):
        surround(padded, [cells_ref[s] for s in range(CELLS)], sel_ref)
        total = jnp.zeros((CELLS * tiles, QUARTER), f32)
        for a in range(3):
            for b in range(3):
                view = window(padded, 2 - a, 2 - b) if flip else window(padded, a, b)
                total = total + dot(view, w_ref[a * 3 + b])
        return total

    forward = taps(x_ref, wo_ref, False)
    backward = taps(g_ref, wg_ref, True)
    both = jnp.concatenate([forward, backward], axis=1).astype(bf16)
    swap = swap16()
    chips = tiles // 2
    for n, ref in enumerate((own_ref, other_ref)):
        for k in range(0, chips, 16):
            begin = n * chips + k
            rows = [both[s * tiles + begin : s * tiles + begin + 16] for s in range(CELLS)]
            turned = dot(swap, jnp.concatenate(rows, axis=0)).astype(bf16)
            ref[k : k + 16] = turned.reshape(16, CELLS, 2 * QUARTER)


def pack_y_kernel(scale, own_ref, other_ref, parts_ref, out_ref):
    total = parts_ref[0]
    for s in range(1, parts_ref.shape[0]):
        total = total + parts_ref[s]
    piece = (total * scale).astype(bf16)
    piece = jnp.concatenate([piece, jnp.zeros((PIECE_ROWS - piece.shape[0], HALF), bf16)], axis=0)
    for y in range(ROWS):
        for x in range(COLUMNS):
            for i, ref in enumerate((own_ref, other_ref)):
                begin = (x * 2 + i) * CELLS
                out_ref[y, begin : begin + CELLS, :] = ref[x * ROWS + y]
        out_ref[y, COLUMNS * 2 * CELLS :, :] = piece


def pack_x_kernel(size, in_ref, out_ref):
    pair = 2 * CELLS
    pieces = [in_ref[y, COLUMNS * pair :, :].astype(f32)[:size] for y in range(ROWS)]
    pieces = jnp.concatenate(pieces, axis=0).astype(bf16)
    for x in range(COLUMNS):
        for y in range(ROWS):
            out_ref[x, y * pair : (y + 1) * pair, :] = in_ref[y, x * pair : (x + 1) * pair, :]
        out_ref[x, ROWS * pair :, :] = pieces


def join_kernel(count_ref, recv_ref, owner_ref, out_ref, grad_ref):
    live = live_mask(owner_ref[...], count_ref[0])
    order = jnp.where(class_order(True) & live, 1.0, 0.0).astype(bf16)

    core = lax.axis_index("tile") % 2
    classes = []
    for m in range(CLASSES):
        quarters = []
        for hi in range(2):
            for ho in range(2):
                chip = device_of(m, 0, ho) // 2
                begin = pl.multiple_of((chip % ROWS * 2 + (hi ^ core)) * CELLS, CELLS)
                quarters.append(recv_ref[chip // ROWS, pl.ds(begin, CELLS), :])
        classes.append(quarters)

    def join(low):
        rows = [jnp.concatenate([part[:, low : low + QUARTER] for part in parts], axis=1) for parts in classes]
        return dot(order, jnp.concatenate(rows, axis=0)).astype(bf16)

    out_ref[...] = join(0)
    grad_ref[...] = join(QUARTER)


def rows_kernel(mine_ref, other_ref, out_ref):
    low = lax.axis_index("tile") % 2 == 0
    begin = ROWS * 2 * CELLS

    def half(ref, ho):
        return jnp.concatenate([ref[ho * 2, begin:, :], ref[ho * 2 + 1, begin:, :]], axis=0)

    for ho in range(2):
        mine, other = half(mine_ref, ho), half(other_ref, ho)
        columns = slice(ho * HALF, (ho + 1) * HALF)
        for tap in range(out_ref.shape[0]):
            rows = slice(tap * HALF, (tap + 1) * HALF)
            out_ref[tap, :HALF, columns] = jnp.where(low, mine[rows], other[rows])
            out_ref[tap, HALF:, columns] = jnp.where(low, other[rows], mine[rows])


def neighbour_table(owner, neighbors, names):
    positions = jnp.arange(owner.shape[0], dtype=jnp.int32)
    beside = jnp.sum(jnp.where(neighbors[:, :, None] == positions, owner + 1, 0), axis=2) - 1
    peer = jnp.sum(jnp.where((owner == names[:, None])[:, :, None], beside[None], 0), axis=1)
    return (peer.T[:, :, None] == names).astype(bf16)


def local(features, cotangent, weight, tile_owner, tile_neighbors, tile_counts):
    tiles = lax.axis_size("tile")
    slides = lax.axis_size("dp")
    device = lax.axis_index("tile")
    hi, ho = device % 2, device // (tiles // 2)
    width = features.shape[-1]
    cells = features.shape[2] * features.shape[3]
    smem = pl.BlockSpec(memory_space=pltpu.SMEM)
    hbm = pl.BlockSpec(memory_space=pltpu.HBM)

    chips = tiles // 2
    core = [(j, j ^ 1) for j in range(tiles)]
    same_core = [[2 * c + i for c in range(chips)] for i in range(2)]
    send = pl.pallas_call(
        split_kernel,
        out_shape=jax.ShapeDtypeStruct((chips, CELLS, 4 * HALF), bf16),
        in_specs=[smem, hbm, hbm, hbm],
        out_specs=vmem(1)[0],
        scratch_shapes=[
            pltpu.VMEM((1, tiles), jnp.int32),
            pltpu.VMEM((cells, width), bf16),
            pltpu.VMEM((cells, width), bf16),
            pltpu.SemaphoreType.DMA((3,)),
        ],
        name="split",
    )(tile_counts, tile_owner, features.reshape(cells, width), cotangent.reshape(cells, width))
    own = lax.all_to_all(send, "tile", 0, 0, tiled=True, axis_index_groups=same_core)

    side = jnp.arange(chips, dtype=jnp.int32) * 2
    names = jnp.concatenate([side + hi, side + 1 - hi])
    sel = neighbour_table(tile_owner[0], tile_neighbors[0], names)
    taps = weight.shape[0] * weight.shape[1]
    quarter = (2 * hi + ho) * QUARTER
    flat = weight.reshape(taps, width, width)
    w_out = lax.dynamic_slice_in_dim(flat, quarter, QUARTER, axis=2)
    w_grad = lax.dynamic_slice_in_dim(flat, quarter, QUARTER, axis=1).transpose(0, 2, 1)
    own, sel, w_out, w_grad = lax.optimization_barrier((own, sel, w_out, w_grad))
    other = lax.ppermute(own, "tile", core)

    partial = pl.pallas_call(
        weight_kernel,
        out_shape=jax.ShapeDtypeStruct((taps * HALF, HALF), f32),
        in_specs=vmem(3),
        out_specs=vmem(1)[0],
        scratch_shapes=[pltpu.VMEM((n, tiles, HALF), bf16) for n in (CELLS, CELLS, PAD * PAD)],
        compiler_params=PARAMS,
        name="weight_taps",
    )(own, other, sel)

    groups = [[device_of(m, i, o) for m in range(CLASSES)] for o in range(2) for i in range(2)]
    rows = taps * HALF // CLASSES
    parts = lax.all_to_all(
        partial.reshape(CLASSES, rows, HALF), "tile", 0, 0, tiled=True, axis_index_groups=groups
    )
    outgoing = jax.ShapeDtypeStruct((chips, CELLS, 2 * QUARTER), bf16)
    back_own, back_other = pl.pallas_call(
        conv_kernel,
        out_shape=[outgoing, outgoing],
        in_specs=vmem(5),
        out_specs=vmem(2),
        scratch_shapes=[pltpu.VMEM((n, tiles, width), bf16) for n in (CELLS, CELLS, PAD * PAD)],
        compiler_params=PARAMS,
        name="conv_taps",
    )(own, other, sel, w_out, w_grad)
    back_other = lax.ppermute(back_other, "tile", core)
    parts, back_own, back_other = lax.optimization_barrier((parts, back_own, back_other))

    part = jnp.sum(parts, axis=0)
    parts = lax.all_to_all(jnp.broadcast_to(part, (slides, rows, HALF)), "dp", 0, 0, tiled=True)
    scale = 1.0 / math.sqrt(slides * tiles * cells)
    along_y = [[(x * ROWS + y) * 2 + i for y in range(ROWS)] for x in range(COLUMNS) for i in range(2)]
    along_x = [[(x * ROWS + y) * 2 + i for x in range(COLUMNS)] for y in range(ROWS) for i in range(2)]
    packed = pl.pallas_call(
        functools.partial(pack_y_kernel, scale),
        out_shape=jax.ShapeDtypeStruct((ROWS, COLUMNS * 2 * CELLS + PIECE_ROWS, HALF), bf16),
        in_specs=vmem(3),
        out_specs=vmem(1)[0],
        compiler_params=PARAMS,
        name="pack_y",
    )(back_own, back_other, parts)
    packed = lax.all_to_all(packed, "tile", 0, 0, tiled=True, axis_index_groups=along_y)
    packed = pl.pallas_call(
        functools.partial(pack_x_kernel, rows),
        out_shape=jax.ShapeDtypeStruct((COLUMNS, ROWS * (2 * CELLS + rows), HALF), bf16),
        in_specs=vmem(1),
        out_specs=vmem(1)[0],
        compiler_params=PARAMS,
        name="pack_x",
    )(packed)
    mine = lax.all_to_all(packed, "tile", 0, 0, tiled=True, axis_index_groups=along_x)
    other = lax.ppermute(mine, "tile", core)
    grad_weight = pl.pallas_call(
        rows_kernel,
        out_shape=jax.ShapeDtypeStruct((taps, width, width), bf16),
        in_specs=vmem(2),
        out_specs=vmem(1)[0],
        compiler_params=PARAMS,
        name="rows",
    )(mine, other).reshape(weight.shape)

    out, grad = pl.pallas_call(
        join_kernel,
        out_shape=[jax.ShapeDtypeStruct((cells, width), bf16)] * 2,
        in_specs=[smem, *vmem(2)],
        out_specs=vmem(2),
        compiler_params=PARAMS,
        name="join",
    )(tile_counts, mine, tile_owner)
    return out.reshape(features.shape), grad.reshape(features.shape), grad_weight


def solution(mesh):
    return jax.shard_map(
        local,
        mesh=mesh,
        in_specs=(
            P("dp", "tile", None, None, None),
            P("dp", "tile", None, None, None),
            P(),
            P("dp", None),
            P("dp", None, None),
            P("dp"),
        ),
        out_specs=(P("dp", "tile", None, None, None), P("dp", "tile", None, None, None), P()),
        check_vma=False,
    )
```

time: 124 us -> 118 us (0.952)
  starting transfers between devices: 41 us -> 30.4 us
  waiting for transfers between devices: 15.7 us -> 20.8 us
  blocking collectives: 46.4 us -> 49.3 us
  Pallas kernels: 13.1 us -> 10.7 us
    ppermute x3 -> x0, starting transfers between devices: 9.78 us -> none  [local(): lax.ppermute(back[n], 'tile', [(j, j ^ n * 2 * ROWS) for j in range(tiles)])]
    all_to_all x1, waiting for transfers between devices: 0.01 us -> 7.83 us  [local(): lax.all_to_all(partial.reshape(CLASSES, rows, HALF), 'tile', 0, 0, tiled=...]
    ppermute x3 -> x0, waiting for transfers between devices: 3.59 us -> none  [local(): lax.ppermute(back[n], 'tile', [(j, j ^ n * 2 * ROWS) for j in range(tiles)])]
    all_to_all x1, blocking collectives: 9.67 us -> 12.1 us  [local(): lax.all_to_all(packed, 'tile', 0, 0, tiled=True, axis_index_groups=along_x)]
    pallas_call x3 -> x4, Pallas kernels: 7.05 us -> 6.4 us  [the longest x1 4.03 us: local(): pl.pallas_call(conv_kernel, out_shape=[outgoing, outgoing], in_specs=vmem...]
  transfers between devices with their start and end apart: 8 -> 5, of which waited for: 5 -> 5; matrix products, arithmetic and copies ran while one was open for 4% -> 4% of each run, Pallas kernels for 5% -> 4%
where the time goes in v3:
time: 118 us
  blocking collectives  49.3 us (42%)
  starting transfers between devices  30.4 us (26%)
  waiting for transfers between devices  20.8 us (18%)
  Pallas kernels  10.7 us (9%)
  other arithmetic  2.73 us (2%)
  local copies, waits for them, and re-layouts  2.26 us (2%)
  between operations  1.61 us (1%)
    all_to_all x1, blocking collectives, local(): lax.all_to_all(jnp.broadcast_to(part, (slides, rows, HALF)), 'dp', 0, 0,...  19.4 us
    all_to_all x1, blocking collectives, local(): lax.all_to_all(packed, 'tile', 0, 0, tiled=True, axis_index_groups=along_y)  17.9 us
    all_to_all x1, blocking collectives, local(): lax.all_to_all(packed, 'tile', 0, 0, tiled=True, axis_index_groups=along_x)  12.1 us
    all_to_all x1, starting transfers between devices, local(): lax.all_to_all(send, 'tile', 0, 0, tiled=True, axis_index_groups=same_core)  10.5 us
    all_to_all x1, waiting for transfers between devices, local(): lax.all_to_all(send, 'tile', 0, 0, tiled=True, axis_index_groups=same_core)  9.57 us
    all_to_all x1, waiting for transfers between devices, local(): lax.all_to_all(partial.reshape(CLASSES, rows, HALF), 'tile', 0, 0, tiled=...  7.83 us
    ppermute x1, starting transfers between devices, local(): other = lax.ppermute(mine, 'tile', core)  7.65 us
    ppermute x1, starting transfers between devices, local(): other = lax.ppermute(own, 'tile', core)  5.4 us
  transfers between devices with their start and end apart: 5, of which 5 were waited for; matrix products, arithmetic and copies ran while one was open for 4% of the time, Pallas kernels for 4%

profile of v3, /device:TPU:1, one launch (start us, length us, event | category | flops | bytes accessed | tf_op | source)
XLA Modules:
  0.0 117.9 jit_solution(10692208008027768986)
XLA Ops:
  1.4 2.1 %split.1 = bf16[32,16,512]{2,1,0:T(8,128)(2,1)} custom-call(s32[1]{0:T(128)S(6)} %copy.22.count_ref, s32[1,64]{1,0:T(1,128)} %owner_ref.1, bf16[256,256]{1,0:T(8,128)(2,1)} %bitcast.18, bf16[256,256]{1,0:T(8,128)(2,1)} %bitcast.19), custom_call_target="tpu_custom_call" | custom-call | tf_op jit(solution)/shard_map/split/pallas_call | solution.py:255
  3.5 10.5 %all-to-all-start = ((bf16[32,16,512]{2,1,0:T(8,128)(2,1)}), bf16[32,16,512]{2,1,0:T(8,128)(2,1)S(1)}, u32[]{:S(2)}, u32[]{:S(2)}) async-start(bf16[32,16,512]{2,1,0:T(8,128)(2,1)} %split.1), calls=%async_computation | async-start | bytes 1048576 | tf_op jit(solution)/shard_map/all_to_all | solution.py:268
  14.1 0.0 copy-start.3
  14.1 0.7 copy.20
  14.9 0.1 copy.17
  14.9 1.2 %select_reduce_fusion.1 = s32[64,8]{1,0:T(8,128)S(1)} fusion(s32[64]{0:T(128)S(1)} %broadcast_add_fusion.1, s32[64,8]{1,0:T(8,128)S(1)} %copy.17), kind=kLoop, calls=%fused_computation.2 | loop fusion | flops 97792 | bytes 4352 | tf_op jit(solution)/shard_map/reduce_sum | solution.py:237
  16.2 0.1 copy.18
  16.2 0.1 pad_add_fusion
  16.3 0.1 broadcast_compare_fusion
  16.4 1.2 select_reduce_fusion
  17.6 0.1 copy.19
  17.6 0.7 constant_dynamic-slice_fusion
  18.4 0.2 dynamic-slice_bitcast_fusion.wg_ref
  18.6 0.1 compare_convert_fusion.sel_ref
  18.8 9.6 %all-to-all-done.own_ref.own_in_ref = bf16[32,16,512]{2,1,0:T(8,128)(2,1)S(1)} async-done(((bf16[32,16,512]{2,1,0:T(8,128)(2,1)}), bf16[32,16,512]{2,1,0:T(8,128)(2,1)S(1)}, u32[]{:S(2)}, u32[]{:S(2)}) %all-to-all-start) | async-done | bytes 524320 | tf_op jit(solution)/shard_map/all_to_all | solution.py:268
  28.3 5.4 %collective-permute-start = (bf16[32,16,512]{2,1,0:T(8,128)(2,1)S(1)}, bf16[32,16,512]{2,1,0:T(8,128)(2,1)S(1)}, u32[]{:S(2)}, u32[]{:S(2)}) collective-permute-start(bf16[32,16,512]{2,1,0:T(8,128)(2,1)S(1)} %all-to-all-done.own_ref.own_in_ref), channel_id=1, source_target_pairs={{0,1},{1,0},{2,3},{3,2},{4,5},{5,4},{6,7},{7,6},{8,9},{9,8},{10,11... | collective-permute-start | bytes 1572872 | tf_op jit(solution)/shard_map/ppermute | solution.py:279
  33.7 1.5 %collective-permute-done.other_ref.other_in_ref = bf16[32,16,512]{2,1,0:T(8,128)(2,1)S(1)} collective-permute-done((bf16[32,16,512]{2,1,0:T(8,128)(2,1)S(1)}, bf16[32,16,512]{2,1,0:T(8,128)(2,1)S(1)}, u32[]{:S(2)}, u32[]{:S(2)}) %collective-permute-start) | collective-permute-done | bytes 524320 | tf_op jit(solution)/shard_map/ppermute | solution.py:279
  35.3 2.2 %weight_taps.1 = f32[1152,128]{1,0:T(8,128)} custom-call(bf16[32,16,512]{2,1,0:T(8,128)(2,1)S(1)} %all-to-all-done.own_ref.own_in_ref, bf16[32,16,512]{2,1,0:T(8,128)(2,1)S(1)} %collective-permute-done.other_ref.other_in_ref, bf16[8,64,64]{2,1,0:T(8,128)(2,1)S(1)} %compare_convert_fusion.sel_ref), custom_call_target="tpu_custom_call" | custom-call | tf_op jit(solution)/shard_map/weight_taps/pallas_call | solution.py:281
  37.5 4.3 %all-to-all-start.1 = ((f32[16,72,128]{2,1,0:T(8,128)}), f32[16,72,128]{2,1,0:T(8,128)S(1)}, u32[]{:S(2)}, u32[]{:S(2)}) async-start(f32[16,72,128]{2,1,0:T(8,128)} %bitcast.7), calls=%async_computation.1 | async-start | bytes 1179648 | tf_op jit(solution)/shard_map/all_to_all | solution.py:293
  41.8 0.3 copy.21.wo_ref
  42.1 4.0 %conv_taps.1 = (bf16[32,16,128]{2,1,0:T(8,128)(2,1)S(1)}, bf16[32,16,128]{2,1,0:T(8,128)(2,1)S(1)}) custom-call(bf16[32,16,512]{2,1,0:T(8,128)(2,1)S(1)} %all-to-all-done.own_ref.own_in_ref, bf16[32,16,512]{2,1,0:T(8,128)(2,1)S(1)} %collective-permute-done.other_ref.other_in_ref, bf16[8,64,64]{2,1,0:T(8,128)(2,1)S(1)} %compare_convert_fusion.sel_ref, ...), custom_call_target="tpu_custom_call" | custom-call | tf_op jit(solution)/shard_map/conv_taps/pallas_call | solution.py:297
  46.1 2.6 %collective-permute-start.1 = (bf16[32,16,128]{2,1,0:T(8,128)(2,1)S(1)}, bf16[32,16,128]{2,1,0:T(8,128)(2,1)S(1)}, u32[]{:S(2)}, u32[]{:S(2)}) collective-permute-start(bf16[32,16,128]{2,1,0:T(8,128)(2,1)S(1)} %get-tuple-element.19), channel_id=1, source_target_pairs={{0,1},{1,0},{2,3},{3,2},{4,5},{5,4},{6,7},{7,6},{8,9},{9,8},{10,11... | collective-permute-start | bytes 393224 | tf_op jit(solution)/shard_map/ppermute | solution.py:306
  48.7 1.0 collective-permute-done.1.other_ref
  49.7 7.8 %all-to-all-done.1 = f32[16,72,128]{2,1,0:T(8,128)S(1)} async-done(((f32[16,72,128]{2,1,0:T(8,128)}), f32[16,72,128]{2,1,0:T(8,128)S(1)}, u32[]{:S(2)}, u32[]{:S(2)}) %all-to-all-start.1) | async-done | bytes 589856 | tf_op jit(solution)/shard_map/all_to_all | solution.py:293
  57.6 19.4 %all_to_all.25.parts_ref = f32[8,72,128]{2,1,0:T(8,128)S(1)} all-to-all(f32[8,72,128]{2,1,0:T(8,128)S(1)} %broadcast_in_dim.42), channel_id=1, replica_groups=mesh['dp'=8,'tile'=64] {'dp'}, dimensions={0} | all-to-all | bytes 589824 | tf_op jit(solution)/shard_map/all_to_all | solution.py:310
  77.0 17.9 %all_to_all.26.in_ref = bf16[8,208,128]{2,1,0:T(8,128)(2,1)S(1)} all-to-all(bf16[8,208,128]{2,1,0:T(8,128)(2,1)S(1)} %pack_y.1), channel_id=1, replica_groups={{0,2,4,6,8,10,12,14},{1,3,5,7,9,11,13,15},{16,18,20,22,24,26,28,30},{17..., dimensions={0} | all-to-all | bytes 851968 | tf_op jit(solution)/shard_map/all_to_all | solution.py:322
  94.8 0.1 pack_x.1
  94.9 12.1 %all_to_all.27.recv_ref.mine_ref = bf16[4,832,128]{2,1,0:T(8,128)(2,1)S(1)} all-to-all(bf16[4,832,128]{2,1,0:T(8,128)(2,1)S(1)} %pack_x.1), channel_id=1, replica_groups={{0,16,32,48},{1,17,33,49},{2,18,34,50},{3,19,35,51},{4,20,36,52},{5,21,..., dimensions={0} | all-to-all | bytes 1703936 | tf_op jit(solution)/shard_map/all_to_all | solution.py:331
  107.1 7.7 %collective-permute-start.2 = (bf16[4,832,128]{2,1,0:T(8,128)(2,1)S(1)}, bf16[4,832,128]{2,1,0:T(8,128)(2,1)S(1)}, u32[]{:S(2)}, u32[]{:S(2)}) collective-permute-start(bf16[4,832,128]{2,1,0:T(8,128)(2,1)S(1)} %all_to_all.27.recv_ref.mine_ref), channel_id=1, source_target_pairs={{0,1},{1,0},{2,3},{3,2},{4,5},{5,4},{6,7},{7,6},{8,9},{9,8},{10,11... | collective-permute-start | bytes 2555912 | tf_op jit(solution)/shard_map/ppermute | solution.py:332
  114.7 1.1 join.1
  115.8 0.9 collective-permute-done.2.other_ref
  116.7 1.2 rows.1
  (13 shorter events, 0.1 us)
Async XLA Ops:
  0.6 13.4 %copy-start = (s32[1,64]{1,0:T(1,128)S(1)}, s32[1,64]{1,0:T(1,128)}, u32[]{:S(2)}) copy-start(s32[1,64]{1,0:T(1,128)} %owner_ref.1) | copy-start | bytes 772
  0.6 13.4 %copy-start.2 = (bf16[3,3,256,256]{3,2,1,0:T(8,128)(2,1)S(1)}, bf16[3,3,256,256]{3,2,1,0:T(8,128)(2,1)}, u32[]{:S(2)}) copy-start(bf16[3,3,256,256]{3,2,1,0:T(8,128)(2,1)} %param.8) | copy-start | bytes 3538948
  3.5 24.8 %all-to-all-start = ((bf16[32,16,512]{2,1,0:T(8,128)(2,1)}), bf16[32,16,512]{2,1,0:T(8,128)(2,1)S(1)}, u32[]{:S(2)}, u32[]{:S(2)}) async-start(bf16[32,16,512]{2,1,0:T(8,128)(2,1)} %split.1), calls=%async_computation | async-start | bytes 1048576 | tf_op jit(solution)/shard_map/all_to_all | solution.py:268
  14.1 0.8 copy-start.3
  18.7 23.0 %copy-start.1 = (bf16[9,256,64]{1,2,0:T(8,128)(2,1)S(1)}, bf16[9,256,64]{1,2,0:T(8,128)(2,1)}, u32[]{:S(2)}) copy-start(bf16[9,256,64]{1,2,0:T(8,128)(2,1)} %constant_dynamic-slice_fusion) | copy-start | bytes 884740
  28.3 6.9 %collective-permute-start = (bf16[32,16,512]{2,1,0:T(8,128)(2,1)S(1)}, bf16[32,16,512]{2,1,0:T(8,128)(2,1)S(1)}, u32[]{:S(2)}, u32[]{:S(2)}) collective-permute-start(bf16[32,16,512]{2,1,0:T(8,128)(2,1)S(1)} %all-to-all-done.own_ref.own_in_ref), channel_id=1, source_target_pairs={{0,1},{1,0},{2,3},{3,2},{4,5},{5,4},{6,7},{7,6},{8,9},{9,8},{10,11... | collective-permute-start | bytes 1572872 | tf_op jit(solution)/shard_map/ppermute | solution.py:279
  37.5 20.0 %all-to-all-start.1 = ((f32[16,72,128]{2,1,0:T(8,128)}), f32[16,72,128]{2,1,0:T(8,128)S(1)}, u32[]{:S(2)}, u32[]{:S(2)}) async-start(f32[16,72,128]{2,1,0:T(8,128)} %bitcast.7), calls=%async_computation.1 | async-start | bytes 1179648 | tf_op jit(solution)/shard_map/all_to_all | solution.py:293
  46.1 3.5 %collective-permute-start.1 = (bf16[32,16,128]{2,1,0:T(8,128)(2,1)S(1)}, bf16[32,16,128]{2,1,0:T(8,128)(2,1)S(1)}, u32[]{:S(2)}, u32[]{:S(2)}) collective-permute-start(bf16[32,16,128]{2,1,0:T(8,128)(2,1)S(1)} %get-tuple-element.19), channel_id=1, source_target_pairs={{0,1},{1,0},{2,3},{3,2},{4,5},{5,4},{6,7},{7,6},{8,9},{9,8},{10,11... | collective-permute-start | bytes 393224 | tf_op jit(solution)/shard_map/ppermute | solution.py:306
  107.1 9.6 %collective-permute-start.2 = (bf16[4,832,128]{2,1,0:T(8,128)(2,1)S(1)}, bf16[4,832,128]{2,1,0:T(8,128)(2,1)S(1)}, u32[]{:S(2)}, u32[]{:S(2)}) collective-permute-start(bf16[4,832,128]{2,1,0:T(8,128)(2,1)S(1)} %all_to_all.27.recv_ref.mine_ref), channel_id=1, source_target_pairs={{0,1},{1,0},{2,3},{3,2},{4,5},{5,4},{6,7},{7,6},{8,9},{9,8},{10,11... | collective-permute-start | bytes 2555912 | tf_op jit(solution)/shard_map/ppermute | solution.py:332

commit v4 on v3

--- a/solution.py
+++ b/solution.py
@@ -14,9 +14,6 @@
 PAD = SPAN + 2
 HALF = 128
 QUARTER = 64
-ROWS = 8
-COLUMNS = 4
-PIECE_ROWS = 80
 bf16, f32 = jnp.bfloat16, jnp.float32
 
 
@@ -169,28 +166,15 @@
             ref[k : k + 16] = turned.reshape(16, CELLS, 2 * QUARTER)
 
 
-def pack_y_kernel(scale, own_ref, other_ref, parts_ref, out_ref):
+def pack_kernel(scale, own_ref, other_ref, parts_ref, out_ref):
     total = parts_ref[0]
     for s in range(1, parts_ref.shape[0]):
         total = total + parts_ref[s]
     piece = (total * scale).astype(bf16)
-    piece = jnp.concatenate([piece, jnp.zeros((PIECE_ROWS - piece.shape[0], HALF), bf16)], axis=0)
-    for y in range(ROWS):
-        for x in range(COLUMNS):
-            for i, ref in enumerate((own_ref, other_ref)):
-                begin = (x * 2 + i) * CELLS
-                out_ref[y, begin : begin + CELLS, :] = ref[x * ROWS + y]
-        out_ref[y, COLUMNS * 2 * CELLS :, :] = piece
-
-
-def pack_x_kernel(size, in_ref, out_ref):
-    pair = 2 * CELLS
-    pieces = [in_ref[y, COLUMNS * pair :, :].astype(f32)[:size] for y in range(ROWS)]
-    pieces = jnp.concatenate(pieces, axis=0).astype(bf16)
-    for x in range(COLUMNS):
-        for y in range(ROWS):
-            out_ref[x, y * pair : (y + 1) * pair, :] = in_ref[y, x * pair : (x + 1) * pair, :]
-        out_ref[x, ROWS * pair :, :] = pieces
+    for chip in range(out_ref.shape[0]):
+        out_ref[chip, :CELLS, :] = own_ref[chip]
+        out_ref[chip, CELLS : 2 * CELLS, :] = other_ref[chip]
+        out_ref[chip, 2 * CELLS :, :] = piece
 
 
 def join_kernel(count_ref, recv_ref, owner_ref, out_ref, grad_ref):
@@ -204,8 +188,8 @@
         for hi in range(2):
             for ho in range(2):
                 chip = device_of(m, 0, ho) // 2
-                begin = pl.multiple_of((chip % ROWS * 2 + (hi ^ core)) * CELLS, CELLS)
-                quarters.append(recv_ref[chip // ROWS, pl.ds(begin, CELLS), :])
+                begin = pl.multiple_of((hi ^ core) * CELLS, CELLS)
+                quarters.append(recv_ref[chip, pl.ds(begin, CELLS), :])
         classes.append(quarters)
 
     def join(low):
@@ -218,18 +202,19 @@
 
 def rows_kernel(mine_ref, other_ref, out_ref):
     low = lax.axis_index("tile") % 2 == 0
-    begin = ROWS * 2 * CELLS
+    taps = out_ref.shape[0]
 
     def half(ref, ho):
-        return jnp.concatenate([ref[ho * 2, begin:, :], ref[ho * 2 + 1, begin:, :]], axis=0)
+        chips = [device_of(m, 0, ho) // 2 for m in range(CLASSES)]
+        return jnp.concatenate([ref[c, 2 * CELLS :, :].astype(f32) for c in chips], axis=0)
 
     for ho in range(2):
         mine, other = half(mine_ref, ho), half(other_ref, ho)
         columns = slice(ho * HALF, (ho + 1) * HALF)
-        for tap in range(out_ref.shape[0]):
+        for tap in range(taps):
             rows = slice(tap * HALF, (tap + 1) * HALF)
-            out_ref[tap, :HALF, columns] = jnp.where(low, mine[rows], other[rows])
-            out_ref[tap, HALF:, columns] = jnp.where(low, other[rows], mine[rows])
+            out_ref[tap, :HALF, columns] = jnp.where(low, mine[rows], other[rows]).astype(bf16)
+            out_ref[tap, HALF:, columns] = jnp.where(low, other[rows], mine[rows]).astype(bf16)
 
 
 def neighbour_table(owner, neighbors, names):
@@ -309,26 +294,15 @@
     part = jnp.sum(parts, axis=0)
     parts = lax.all_to_all(jnp.broadcast_to(part, (slides, rows, HALF)), "dp", 0, 0, tiled=True)
     scale = 1.0 / math.sqrt(slides * tiles * cells)
-    along_y = [[(x * ROWS + y) * 2 + i for y in range(ROWS)] for x in range(COLUMNS) for i in range(2)]
-    along_x = [[(x * ROWS + y) * 2 + i for x in range(COLUMNS)] for y in range(ROWS) for i in range(2)]
     packed = pl.pallas_call(
-        functools.partial(pack_y_kernel, scale),
-        out_shape=jax.ShapeDtypeStruct((ROWS, COLUMNS * 2 * CELLS + PIECE_ROWS, HALF), bf16),
+        functools.partial(pack_kernel, scale),
+        out_shape=jax.ShapeDtypeStruct((chips, 2 * CELLS + rows, HALF), bf16),
         in_specs=vmem(3),
         out_specs=vmem(1)[0],
         compiler_params=PARAMS,
-        name="pack_y",
+        name="pack",
     )(back_own, back_other, parts)
-    packed = lax.all_to_all(packed, "tile", 0, 0, tiled=True, axis_index_groups=along_y)
-    packed = pl.pallas_call(
-        functools.partial(pack_x_kernel, rows),
-        out_shape=jax.ShapeDtypeStruct((COLUMNS, ROWS * (2 * CELLS + rows), HALF), bf16),
-        in_specs=vmem(1),
-        out_specs=vmem(1)[0],
-        compiler_params=PARAMS,
-        name="pack_x",
-    )(packed)
-    mine = lax.all_to_all(packed, "tile", 0, 0, tiled=True, axis_index_groups=along_x)
+    mine = lax.all_to_all(packed, "tile", 0, 0, tiled=True, axis_index_groups=same_core)
     other = lax.ppermute(mine, "tile", core)
     grad_weight = pl.pallas_call(
         rows_kernel,

time: 118 us -> 116 us (0.983)
  blocking collectives: 49.3 us -> 46.7 us
    all_to_all x2 -> x1, blocking collectives: 30 us -> 27.4 us  [local(): lax.all_to_all(packed, 'tile', 0, 0, tiled=True, axis_index_groups=same_c...]
where the time goes in v4:
time: 116 us
  blocking collectives  46.7 us (40%)
  starting transfers between devices  31 us (27%)
  waiting for transfers between devices  20.8 us (18%)
  Pallas kernels  10.8 us (9%)
  other arithmetic  2.73 us (2%)
  local copies, waits for them, and re-layouts  2.26 us (2%)
  between operations  1.61 us (1%)
    all_to_all x1, blocking collectives, local(): lax.all_to_all(packed, 'tile', 0, 0, tiled=True, axis_index_groups=same_c...  27.4 us
    all_to_all x1, blocking collectives, local(): lax.all_to_all(jnp.broadcast_to(part, (slides, rows, HALF)), 'dp', 0, 0,...  19.4 us
    all_to_all x1, starting transfers between devices, local(): lax.all_to_all(send, 'tile', 0, 0, tiled=True, axis_index_groups=same_core)  10.5 us
    all_to_all x1, waiting for transfers between devices, local(): lax.all_to_all(send, 'tile', 0, 0, tiled=True, axis_index_groups=same_core)  9.57 us
    ppermute x1, starting transfers between devices, local(): other = lax.ppermute(mine, 'tile', core)  8.23 us
    all_to_all x1, waiting for transfers between devices, local(): lax.all_to_all(partial.reshape(CLASSES, rows, HALF), 'tile', 0, 0, tiled=...  7.83 us
    ppermute x1, starting transfers between devices, local(): other = lax.ppermute(own, 'tile', core)  5.4 us
    all_to_all x1, starting transfers between devices, local(): lax.all_to_all(partial.reshape(CLASSES, rows, HALF), 'tile', 0, 0, tiled=...  4.27 us
  transfers between devices with their start and end apart: 5, of which 5 were waited for; matrix products, arithmetic and copies ran while one was open for 4% of the time, Pallas kernels for 4%

profile of v4, /device:TPU:1, one launch (start us, length us, event | category | flops | bytes accessed | tf_op | source)
XLA Modules:
  0.0 115.9 jit_solution(12724276522591729462)
XLA Ops:
  1.4 2.1 %split.1 = bf16[32,16,512]{2,1,0:T(8,128)(2,1)} custom-call(s32[1]{0:T(128)S(6)} %copy.22.count_ref, s32[1,64]{1,0:T(1,128)} %owner_ref.1, bf16[256,256]{1,0:T(8,128)(2,1)} %bitcast.18, bf16[256,256]{1,0:T(8,128)(2,1)} %bitcast.19), custom_call_target="tpu_custom_call" | custom-call | tf_op jit(solution)/shard_map/split/pallas_call | solution.py:240
  3.5 10.5 %all-to-all-start = ((bf16[32,16,512]{2,1,0:T(8,128)(2,1)}), bf16[32,16,512]{2,1,0:T(8,128)(2,1)S(1)}, u32[]{:S(2)}, u32[]{:S(2)}) async-start(bf16[32,16,512]{2,1,0:T(8,128)(2,1)} %split.1), calls=%async_computation | async-start | bytes 1048576 | tf_op jit(solution)/shard_map/all_to_all | solution.py:253
  14.1 0.0 copy-done.2
  14.1 0.0 copy-start.3
  14.1 0.7 copy.20
  14.9 0.1 copy.17
  14.9 1.2 %select_reduce_fusion.1 = s32[64,8]{1,0:T(8,128)S(1)} fusion(s32[64]{0:T(128)S(1)} %broadcast_add_fusion.1, s32[64,8]{1,0:T(8,128)S(1)} %copy.17), kind=kLoop, calls=%fused_computation.2 | loop fusion | flops 97792 | bytes 4352 | tf_op jit(solution)/shard_map/reduce_sum | solution.py:222
  16.2 0.1 copy.18
  16.2 0.1 pad_add_fusion
  16.3 0.1 broadcast_compare_fusion
  16.4 1.2 %select_reduce_fusion = s32[64,8]{1,0:T(8,128)S(1)} fusion(s32[64,8]{0,1:T(8,128)S(1)} %broadcast_add_fusion, pred[64,64]{1,0:T(8,128)(4,1)S(1)} %broadcast_compare_fusion), kind=kLoop, calls=%fused_computation.1 | loop fusion | flops 65024 | bytes 8192 | tf_op jit(solution)/shard_map/reduce_sum | solution.py:223
  17.6 0.1 copy.19
  17.6 0.7 constant_dynamic-slice_fusion
  18.4 0.2 dynamic-slice_bitcast_fusion.wg_ref
  18.6 0.1 compare_convert_fusion.sel_ref
  18.8 9.6 %all-to-all-done.own_ref.own_in_ref = bf16[32,16,512]{2,1,0:T(8,128)(2,1)S(1)} async-done(((bf16[32,16,512]{2,1,0:T(8,128)(2,1)}), bf16[32,16,512]{2,1,0:T(8,128)(2,1)S(1)}, u32[]{:S(2)}, u32[]{:S(2)}) %all-to-all-start) | async-done | bytes 524320 | tf_op jit(solution)/shard_map/all_to_all | solution.py:253
  28.3 5.4 %collective-permute-start = (bf16[32,16,512]{2,1,0:T(8,128)(2,1)S(1)}, bf16[32,16,512]{2,1,0:T(8,128)(2,1)S(1)}, u32[]{:S(2)}, u32[]{:S(2)}) collective-permute-start(bf16[32,16,512]{2,1,0:T(8,128)(2,1)S(1)} %all-to-all-done.own_ref.own_in_ref), channel_id=1, source_target_pairs={{0,1},{1,0},{2,3},{3,2},{4,5},{5,4},{6,7},{7,6},{8,9},{9,8},{10,11... | collective-permute-start | bytes 1572872 | tf_op jit(solution)/shard_map/ppermute | solution.py:264
  33.7 1.5 %collective-permute-done.other_ref.other_in_ref = bf16[32,16,512]{2,1,0:T(8,128)(2,1)S(1)} collective-permute-done((bf16[32,16,512]{2,1,0:T(8,128)(2,1)S(1)}, bf16[32,16,512]{2,1,0:T(8,128)(2,1)S(1)}, u32[]{:S(2)}, u32[]{:S(2)}) %collective-permute-start) | collective-permute-done | bytes 524320 | tf_op jit(solution)/shard_map/ppermute | solution.py:264
  35.3 2.2 %weight_taps.1 = f32[1152,128]{1,0:T(8,128)} custom-call(bf16[32,16,512]{2,1,0:T(8,128)(2,1)S(1)} %all-to-all-done.own_ref.own_in_ref, bf16[32,16,512]{2,1,0:T(8,128)(2,1)S(1)} %collective-permute-done.other_ref.other_in_ref, bf16[8,64,64]{2,1,0:T(8,128)(2,1)S(1)} %compare_convert_fusion.sel_ref), custom_call_target="tpu_custom_call" | custom-call | tf_op jit(solution)/shard_map/weight_taps/pallas_call | solution.py:266
  37.5 4.3 %all-to-all-start.1 = ((f32[16,72,128]{2,1,0:T(8,128)}), f32[16,72,128]{2,1,0:T(8,128)S(1)}, u32[]{:S(2)}, u32[]{:S(2)}) async-start(f32[16,72,128]{2,1,0:T(8,128)} %bitcast.7), calls=%async_computation.1 | async-start | bytes 1179648 | tf_op jit(solution)/shard_map/all_to_all | solution.py:278
  41.8 0.3 copy.21.wo_ref
  42.1 4.0 %conv_taps.1 = (bf16[32,16,128]{2,1,0:T(8,128)(2,1)S(1)}, bf16[32,16,128]{2,1,0:T(8,128)(2,1)S(1)}) custom-call(bf16[32,16,512]{2,1,0:T(8,128)(2,1)S(1)} %all-to-all-done.own_ref.own_in_ref, bf16[32,16,512]{2,1,0:T(8,128)(2,1)S(1)} %collective-permute-done.other_ref.other_in_ref, bf16[8,64,64]{2,1,0:T(8,128)(2,1)S(1)} %compare_convert_fusion.sel_ref, ...), custom_call_target="tpu_custom_call" | custom-call | tf_op jit(solution)/shard_map/conv_taps/pallas_call | solution.py:282
  46.1 2.6 %collective-permute-start.1 = (bf16[32,16,128]{2,1,0:T(8,128)(2,1)S(1)}, bf16[32,16,128]{2,1,0:T(8,128)(2,1)S(1)}, u32[]{:S(2)}, u32[]{:S(2)}) collective-permute-start(bf16[32,16,128]{2,1,0:T(8,128)(2,1)S(1)} %get-tuple-element.19), channel_id=1, source_target_pairs={{0,1},{1,0},{2,3},{3,2},{4,5},{5,4},{6,7},{7,6},{8,9},{9,8},{10,11... | collective-permute-start | bytes 393224 | tf_op jit(solution)/shard_map/ppermute | solution.py:291
  48.7 1.0 collective-permute-done.1.other_ref
  49.7 7.8 %all-to-all-done.1 = f32[16,72,128]{2,1,0:T(8,128)S(1)} async-done(((f32[16,72,128]{2,1,0:T(8,128)}), f32[16,72,128]{2,1,0:T(8,128)S(1)}, u32[]{:S(2)}, u32[]{:S(2)}) %all-to-all-start.1) | async-done | bytes 589856 | tf_op jit(solution)/shard_map/all_to_all | solution.py:278
  57.6 19.4 %all_to_all.20.parts_ref = f32[8,72,128]{2,1,0:T(8,128)S(1)} all-to-all(f32[8,72,128]{2,1,0:T(8,128)S(1)} %broadcast_in_dim.42), channel_id=1, replica_groups=mesh['dp'=8,'tile'=64] {'dp'}, dimensions={0} | all-to-all | bytes 589824 | tf_op jit(solution)/shard_map/all_to_all | solution.py:295
  76.9 0.1 pack.1
  77.0 27.4 %all_to_all.21.recv_ref.mine_ref = bf16[32,104,128]{2,1,0:T(8,128)(2,1)S(1)} all-to-all(bf16[32,104,128]{2,1,0:T(8,128)(2,1)S(1)} %pack.1), channel_id=1, replica_groups={{0,2,4,6,8,10,12,14,16,18,20,22,24,26,28,30,32,34,36,38,40,42,44,46,48,..., dimensions={0} | all-to-all | bytes 1703936 | tf_op jit(solution)/shard_map/all_to_all | solution.py:305
  104.4 8.2 %collective-permute-start.2 = (bf16[32,104,128]{2,1,0:T(8,128)(2,1)S(1)}, bf16[32,104,128]{2,1,0:T(8,128)(2,1)S(1)}, u32[]{:S(2)}, u32[]{:S(2)}) collective-permute-start(bf16[32,104,128]{2,1,0:T(8,128)(2,1)S(1)} %all_to_all.21.recv_ref.mine_ref), channel_id=1, source_target_pairs={{0,1},{1,0},{2,3},{3,2},{4,5},{5,4},{6,7},{7,6},{8,9},{9,8},{10,11... | collective-permute-start | bytes 2555912 | tf_op jit(solution)/shard_map/ppermute | solution.py:306
  112.6 1.1 join.1
  113.7 0.9 collective-permute-done.2.other_ref
  114.6 1.3 %rows.1 = bf16[9,256,256]{2,1,0:T(8,128)(2,1)} custom-call(bf16[32,104,128]{2,1,0:T(8,128)(2,1)S(1)} %all_to_all.21.recv_ref.mine_ref, bf16[32,104,128]{2,1,0:T(8,128)(2,1)S(1)} %collective-permute-done.2.other_ref), custom_call_target="tpu_custom_call" | custom-call | tf_op jit(solution)/shard_map/rows/pallas_call | solution.py:307
  (11 shorter events, 0.1 us)
Async XLA Ops:
  0.6 13.4 %copy-start = (s32[1,64]{1,0:T(1,128)S(1)}, s32[1,64]{1,0:T(1,128)}, u32[]{:S(2)}) copy-start(s32[1,64]{1,0:T(1,128)} %owner_ref.1) | copy-start | bytes 772
  0.6 13.4 %copy-start.2 = (bf16[3,3,256,256]{3,2,1,0:T(8,128)(2,1)S(1)}, bf16[3,3,256,256]{3,2,1,0:T(8,128)(2,1)}, u32[]{:S(2)}) copy-start(bf16[3,3,256,256]{3,2,1,0:T(8,128)(2,1)} %param.8) | copy-start | bytes 3538948
  3.5 24.8 %all-to-all-start = ((bf16[32,16,512]{2,1,0:T(8,128)(2,1)}), bf16[32,16,512]{2,1,0:T(8,128)(2,1)S(1)}, u32[]{:S(2)}, u32[]{:S(2)}) async-start(bf16[32,16,512]{2,1,0:T(8,128)(2,1)} %split.1), calls=%async_computation | async-start | bytes 1048576 | tf_op jit(solution)/shard_map/all_to_all | solution.py:253
  14.1 0.8 copy-start.3
  18.7 23.0 %copy-start.1 = (bf16[9,256,64]{1,2,0:T(8,128)(2,1)S(1)}, bf16[9,256,64]{1,2,0:T(8,128)(2,1)}, u32[]{:S(2)}) copy-start(bf16[9,256,64]{1,2,0:T(8,128)(2,1)} %constant_dynamic-slice_fusion) | copy-start | bytes 884740
  28.3 6.9 %collective-permute-start = (bf16[32,16,512]{2,1,0:T(8,128)(2,1)S(1)}, bf16[32,16,512]{2,1,0:T(8,128)(2,1)S(1)}, u32[]{:S(2)}, u32[]{:S(2)}) collective-permute-start(bf16[32,16,512]{2,1,0:T(8,128)(2,1)S(1)} %all-to-all-done.own_ref.own_in_ref), channel_id=1, source_target_pairs={{0,1},{1,0},{2,3},{3,2},{4,5},{5,4},{6,7},{7,6},{8,9},{9,8},{10,11... | collective-permute-start | bytes 1572872 | tf_op jit(solution)/shard_map/ppermute | solution.py:264
  37.5 20.0 %all-to-all-start.1 = ((f32[16,72,128]{2,1,0:T(8,128)}), f32[16,72,128]{2,1,0:T(8,128)S(1)}, u32[]{:S(2)}, u32[]{:S(2)}) async-start(f32[16,72,128]{2,1,0:T(8,128)} %bitcast.7), calls=%async_computation.1 | async-start | bytes 1179648 | tf_op jit(solution)/shard_map/all_to_all | solution.py:278
  46.1 3.5 %collective-permute-start.1 = (bf16[32,16,128]{2,1,0:T(8,128)(2,1)S(1)}, bf16[32,16,128]{2,1,0:T(8,128)(2,1)S(1)}, u32[]{:S(2)}, u32[]{:S(2)}) collective-permute-start(bf16[32,16,128]{2,1,0:T(8,128)(2,1)S(1)} %get-tuple-element.19), channel_id=1, source_target_pairs={{0,1},{1,0},{2,3},{3,2},{4,5},{5,4},{6,7},{7,6},{8,9},{9,8},{10,11... | collective-permute-start | bytes 393224 | tf_op jit(solution)/shard_map/ppermute | solution.py:291
  104.4 10.2 %collective-permute-start.2 = (bf16[32,104,128]{2,1,0:T(8,128)(2,1)S(1)}, bf16[32,104,128]{2,1,0:T(8,128)(2,1)S(1)}, u32[]{:S(2)}, u32[]{:S(2)}) collective-permute-start(bf16[32,104,128]{2,1,0:T(8,128)(2,1)S(1)} %all_to_all.21.recv_ref.mine_ref), channel_id=1, source_target_pairs={{0,1},{1,0},{2,3},{3,2},{4,5},{5,4},{6,7},{7,6},{8,9},{9,8},{10,11... | collective-permute-start | bytes 2555912 | tf_op jit(solution)/shard_map/ppermute | solution.py:306

commit v5 on v4

--- a/solution.py
+++ b/solution.py
@@ -14,11 +14,13 @@
 PAD = SPAN + 2
 HALF = 128
 QUARTER = 64
+SHARE = 36
+SHARE_ROWS = 40
 bf16, f32 = jnp.bfloat16, jnp.float32
 
 
 def device_of(m, hi, ho):
-    return ho * 32 + m * 2 + hi
+    return m // 4 * 16 + ho * 8 + m % 4 * 2 + hi
 
 
 def vmem(n):
@@ -109,9 +111,13 @@
                 put(s, slice(n * chips + k, n * chips + k + 16), turned[s * 16 : (s + 1) * 16])
 
 
-def weight_kernel(own_ref, other_ref, sel_ref, sum_ref, x_ref, g_ref, padded):
+def share_of(m, parity):
+    return m // 4 * 4 + m % 2 * 2 + parity, m // 2 % 2
+
+
+def weight_kernel(own_ref, other_ref, sel_ref, out_ref, x_ref, g_ref, padded, sum_ref):
     device = lax.axis_index("tile")
-    low_x, low_g = device % 2 == 0, device < own_ref.shape[0]
+    low_x, low_g = device % 2 == 0, device // 8 % 2 == 0
 
     def halves(ref, k):
         rows = ref[k : k + 16]
@@ -130,6 +136,13 @@
         for b in range(3):
             tap = a * 3 + b
             sum_ref[tap * HALF : (tap + 1) * HALF, :] = dot(grad, window(padded, a, b)).T
+    fill = jnp.zeros((SHARE_ROWS - SHARE, HALF), f32)
+    for m in range(CLASSES):
+        for parity in range(2):
+            piece, half = share_of(m, parity)
+            begin = (m * 2 + parity) * SHARE
+            out_ref[piece, half, :SHARE, :] = sum_ref[begin : begin + SHARE, :]
+            out_ref[piece, half, SHARE:, :] = fill
 
 
 def conv_kernel(
@@ -166,11 +179,13 @@
             ref[k : k + 16] = turned.reshape(16, CELLS, 2 * QUARTER)
 
 
-def pack_kernel(scale, own_ref, other_ref, parts_ref, out_ref):
-    total = parts_ref[0]
-    for s in range(1, parts_ref.shape[0]):
-        total = total + parts_ref[s]
-    piece = (total * scale).astype(bf16)
+def pack_kernel(scale, own_ref, other_ref, parts_ref, out_ref, piece_ref):
+    for parity in range(2):
+        total = parts_ref[parity]
+        for s in range(parity + 2, parts_ref.shape[0], 2):
+            total = total + parts_ref[s]
+        piece_ref[parity * SHARE : parity * SHARE + SHARE_ROWS, :] = total
+    piece = (piece_ref[: 2 * SHARE, :] * scale).astype(bf16)
     for chip in range(out_ref.shape[0]):
         out_ref[chip, :CELLS, :] = own_ref[chip]
         out_ref[chip, CELLS : 2 * CELLS, :] = other_ref[chip]
@@ -228,7 +243,7 @@
     tiles = lax.axis_size("tile")
     slides = lax.axis_size("dp")
     device = lax.axis_index("tile")
-    hi, ho = device % 2, device // (tiles // 2)
+    hi, ho = device % 2, device // 8 % 2
     width = features.shape[-1]
     cells = features.shape[2] * features.shape[3]
     smem = pl.BlockSpec(memory_space=pltpu.SMEM)
@@ -265,19 +280,30 @@
 
     partial = pl.pallas_call(
         weight_kernel,
-        out_shape=jax.ShapeDtypeStruct((taps * HALF, HALF), f32),
+        out_shape=jax.ShapeDtypeStruct((CLASSES, 2, SHARE_ROWS, HALF), f32),
         in_specs=vmem(3),
         out_specs=vmem(1)[0],
-        scratch_shapes=[pltpu.VMEM((n, tiles, HALF), bf16) for n in (CELLS, CELLS, PAD * PAD)],
+        scratch_shapes=[
+            *(pltpu.VMEM((n, tiles, HALF), bf16) for n in (CELLS, CELLS, PAD * PAD)),
+            pltpu.VMEM((taps * HALF, HALF), f32),
+        ],
         compiler_params=PARAMS,
         name="weight_taps",
     )(own, other, sel)
 
-    groups = [[device_of(m, i, o) for m in range(CLASSES)] for o in range(2) for i in range(2)]
-    rows = taps * HALF // CLASSES
-    parts = lax.all_to_all(
-        partial.reshape(CLASSES, rows, HALF), "tile", 0, 0, tiled=True, axis_index_groups=groups
-    )
+    rows = 2 * SHARE
+
+    def at(slide, x, o, y, i):
+        return slide * tiles + device_of(x * 4 + y, i, o)
+
+    groups = [
+        [at(s + parity, x, o, y + low, i) for x in range(4) for low in range(2) for parity in range(2)]
+        for s in range(0, slides, 2)
+        for o in range(2)
+        for y in range(0, 4, 2)
+        for i in range(2)
+    ]
+    parts = lax.all_to_all(partial, ("dp", "tile"), 0, 0, tiled=True, axis_index_groups=groups)
     outgoing = jax.ShapeDtypeStruct((chips, CELLS, 2 * QUARTER), bf16)
     back_own, back_other = pl.pallas_call(
         conv_kernel,
@@ -292,13 +318,22 @@
     parts, back_own, back_other = lax.optimization_barrier((parts, back_own, back_other))
 
     part = jnp.sum(parts, axis=0)
-    parts = lax.all_to_all(jnp.broadcast_to(part, (slides, rows, HALF)), "dp", 0, 0, tiled=True)
+    groups = [
+        [at(s, x, o, y + low, i) for y in range(0, 4, 2) for s in range(slides)]
+        for x in range(4)
+        for o in range(2)
+        for low in range(2)
+        for i in range(2)
+    ]
+    shares = jnp.broadcast_to(part[:, None], (2, slides, SHARE_ROWS, HALF)).reshape(-1, SHARE_ROWS, HALF)
+    parts = lax.all_to_all(shares, ("dp", "tile"), 0, 0, tiled=True, axis_index_groups=groups)
     scale = 1.0 / math.sqrt(slides * tiles * cells)
     packed = pl.pallas_call(
         functools.partial(pack_kernel, scale),
         out_shape=jax.ShapeDtypeStruct((chips, 2 * CELLS + rows, HALF), bf16),
         in_specs=vmem(3),
         out_specs=vmem(1)[0],
+        scratch_shapes=[pltpu.VMEM((2 * SHARE_ROWS, HALF), f32)],
         compiler_params=PARAMS,
         name="pack",
     )(back_own, back_other, parts)

time: 116 us -> 113 us (0.974)
  waiting for transfers between devices: 20.8 us -> 15 us
    all_to_all x1, waiting for transfers between devices: 7.83 us -> 2.04 us  [local(): lax.all_to_all(partial, ('dp', 'tile'), 0, 0, tiled=True, axis_index_grou...]
    all_to_all x1, blocking collectives: 19.4 us -> 21.9 us  [local(): lax.all_to_all(shares, ('dp', 'tile'), 0, 0, tiled=True, axis_index_group...]
    all_to_all x1, blocking collectives: 27.4 us -> 25.3 us  [local(): lax.all_to_all(packed, 'tile', 0, 0, tiled=True, axis_index_groups=same_c...]
    all_to_all x1, starting transfers between devices: 4.27 us -> 6.27 us  [local(): lax.all_to_all(partial, ('dp', 'tile'), 0, 0, tiled=True, axis_index_grou...]
    ppermute x1, starting transfers between devices: 8.23 us -> 6.91 us  [local(): other = lax.ppermute(mine, 'tile', core)]
  transfers between devices with their start and end apart: 5 -> 5, of which waited for: 5 -> 5; matrix products, arithmetic and copies ran while one was open for 4% -> 5% of each run, Pallas kernels for 4% -> 5%
where the time goes in v5:
time: 113 us; the launch traced here: 112 us
  blocking collectives  47.2 us (42%)
  starting transfers between devices  31.7 us (28%)
  waiting for transfers between devices  15 us (13%)
  Pallas kernels  10.9 us (10%)
  local copies, waits for them, and re-layouts  3.22 us (3%)
  other arithmetic  2.74 us (2%)
  between operations  1.61 us (1%)
    all_to_all x1, blocking collectives, local(): lax.all_to_all(packed, 'tile', 0, 0, tiled=True, axis_index_groups=same_c...  25.3 us
    all_to_all x1, blocking collectives, local(): lax.all_to_all(shares, ('dp', 'tile'), 0, 0, tiled=True, axis_index_group...  21.9 us
    all_to_all x1, starting transfers between devices, local(): lax.all_to_all(send, 'tile', 0, 0, tiled=True, axis_index_groups=same_core)  10.5 us
    all_to_all x1, waiting for transfers between devices, local(): lax.all_to_all(send, 'tile', 0, 0, tiled=True, axis_index_groups=same_core)  9.56 us
    ppermute x1, starting transfers between devices, local(): other = lax.ppermute(mine, 'tile', core)  6.91 us
    all_to_all x1, starting transfers between devices, local(): lax.all_to_all(partial, ('dp', 'tile'), 0, 0, tiled=True, axis_index_grou...  6.27 us
    ppermute x1, starting transfers between devices, local(): other = lax.ppermute(own, 'tile', core)  5.4 us
    pallas_call x1, Pallas kernels, local(): pl.pallas_call(conv_kernel, out_shape=[outgoing, outgoing], in_specs=vmem...  4.04 us
  transfers between devices with their start and end apart: 5, of which 5 were waited for; matrix products, arithmetic and copies ran while one was open for 5% of the time, Pallas kernels for 5%

profile of v5, /device:TPU:1, one launch (start us, length us, event | category | flops | bytes accessed | tf_op | source)
XLA Modules:
  0.0 112.2 jit_solution(9215010525939721883)
XLA Ops:
  1.4 2.1 %split.1 = bf16[32,16,512]{2,1,0:T(8,128)(2,1)} custom-call(s32[1]{0:T(128)S(6)} %copy.22.count_ref, s32[1,64]{1,0:T(1,128)} %owner_ref.1, bf16[256,256]{1,0:T(8,128)(2,1)} %bitcast.19, bf16[256,256]{1,0:T(8,128)(2,1)} %bitcast.20), custom_call_target="tpu_custom_call" | custom-call | tf_op jit(solution)/shard_map/split/pallas_call | solution.py:255
  3.5 10.5 %all-to-all-start = ((bf16[32,16,512]{2,1,0:T(8,128)(2,1)}), bf16[32,16,512]{2,1,0:T(8,128)(2,1)S(1)}, u32[]{:S(2)}, u32[]{:S(2)}) async-start(bf16[32,16,512]{2,1,0:T(8,128)(2,1)} %split.1), calls=%async_computation | async-start | bytes 1048576 | tf_op jit(solution)/shard_map/all_to_all | solution.py:268
  14.1 0.0 copy-start.2
  14.1 0.7 copy.20
  14.9 0.0 copy-done.2
  14.9 0.1 copy.17
  15.0 1.2 %select_reduce_fusion.1 = s32[64,8]{1,0:T(8,128)S(1)} fusion(s32[64]{0:T(128)S(1)} %broadcast_add_fusion.1, s32[64,8]{1,0:T(8,128)S(1)} %copy.17), kind=kLoop, calls=%fused_computation.2 | loop fusion | flops 97792 | bytes 4352 | tf_op jit(solution)/shard_map/reduce_sum | solution.py:237
  16.2 0.1 copy.18
  16.3 0.1 pad_add_fusion
  16.3 0.1 broadcast_compare_fusion
  16.4 1.2 %select_reduce_fusion = s32[64,8]{1,0:T(8,128)S(1)} fusion(s32[64,8]{0,1:T(8,128)S(1)} %broadcast_add_fusion, pred[64,64]{1,0:T(8,128)(4,1)S(1)} %broadcast_compare_fusion), kind=kLoop, calls=%fused_computation.1 | loop fusion | flops 65024 | bytes 8192 | tf_op jit(solution)/shard_map/reduce_sum | solution.py:238
  17.6 0.1 copy.19
  17.6 0.7 constant_dynamic-slice_fusion
  18.4 0.2 dynamic-slice_bitcast_fusion.wg_ref
  18.6 0.1 compare_convert_fusion.sel_ref
  18.8 9.6 %all-to-all-done.own_ref.own_in_ref = bf16[32,16,512]{2,1,0:T(8,128)(2,1)S(1)} async-done(((bf16[32,16,512]{2,1,0:T(8,128)(2,1)}), bf16[32,16,512]{2,1,0:T(8,128)(2,1)S(1)}, u32[]{:S(2)}, u32[]{:S(2)}) %all-to-all-start) | async-done | bytes 524320 | tf_op jit(solution)/shard_map/all_to_all | solution.py:268
  28.3 5.4 %collective-permute-start = (bf16[32,16,512]{2,1,0:T(8,128)(2,1)S(1)}, bf16[32,16,512]{2,1,0:T(8,128)(2,1)S(1)}, u32[]{:S(2)}, u32[]{:S(2)}) collective-permute-start(bf16[32,16,512]{2,1,0:T(8,128)(2,1)S(1)} %all-to-all-done.own_ref.own_in_ref), channel_id=1, source_target_pairs={{0,1},{1,0},{2,3},{3,2},{4,5},{5,4},{6,7},{7,6},{8,9},{9,8},{10,11... | collective-permute-start | bytes 1572872 | tf_op jit(solution)/shard_map/ppermute | solution.py:279
  33.7 1.5 %collective-permute-done.other_ref.other_in_ref = bf16[32,16,512]{2,1,0:T(8,128)(2,1)S(1)} collective-permute-done((bf16[32,16,512]{2,1,0:T(8,128)(2,1)S(1)}, bf16[32,16,512]{2,1,0:T(8,128)(2,1)S(1)}, u32[]{:S(2)}, u32[]{:S(2)}) %collective-permute-start) | collective-permute-done | bytes 524320 | tf_op jit(solution)/shard_map/ppermute | solution.py:279
  35.3 2.3 %weight_taps.1 = f32[16,2,40,128]{3,2,1,0:T(8,128)} custom-call(bf16[32,16,512]{2,1,0:T(8,128)(2,1)S(1)} %all-to-all-done.own_ref.own_in_ref, bf16[32,16,512]{2,1,0:T(8,128)(2,1)S(1)} %collective-permute-done.other_ref.other_in_ref, bf16[8,64,64]{2,1,0:T(8,128)(2,1)S(1)} %compare_convert_fusion.sel_ref), custom_call_target="tpu_custom_call" | custom-call | tf_op jit(solution)/shard_map/weight_taps/pallas_call | solution.py:281
  37.6 6.3 %all-to-all-start.1 = ((f32[16,2,40,128]{3,2,1,0:T(8,128)}), f32[16,2,40,128]{3,2,1,0:T(8,128)S(1)}, u32[]{:S(2)}, u32[]{:S(2)}) async-start(f32[16,2,40,128]{3,2,1,0:T(8,128)} %weight_taps.1), calls=%async_computation.1 | async-start | bytes 1310720 | tf_op jit(solution)/shard_map/all_to_all | solution.py:306
  43.9 1.3 %copy.21.wo_ref = bf16[9,256,64]{2,1,0:T(8,128)(2,1)S(1)} copy(bf16[9,256,64]{1,2,0:T(8,128)(2,1)} %constant_dynamic-slice_fusion) | data formatting | bytes 589824 | tf_op jit(solution)/shard_map/optimization_barrier | solution.py:278
  45.2 4.0 %conv_taps.1 = (bf16[32,16,128]{2,1,0:T(8,128)(2,1)S(1)}, bf16[32,16,128]{2,1,0:T(8,128)(2,1)S(1)}) custom-call(bf16[32,16,512]{2,1,0:T(8,128)(2,1)S(1)} %all-to-all-done.own_ref.own_in_ref, bf16[32,16,512]{2,1,0:T(8,128)(2,1)S(1)} %collective-permute-done.other_ref.other_in_ref, bf16[8,64,64]{2,1,0:T(8,128)(2,1)S(1)} %compare_convert_fusion.sel_ref, ...), custom_call_target="tpu_custom_call" | custom-call | tf_op jit(solution)/shard_map/conv_taps/pallas_call | solution.py:308
  49.2 2.6 %collective-permute-start.1 = (bf16[32,16,128]{2,1,0:T(8,128)(2,1)S(1)}, bf16[32,16,128]{2,1,0:T(8,128)(2,1)S(1)}, u32[]{:S(2)}, u32[]{:S(2)}) collective-permute-start(bf16[32,16,128]{2,1,0:T(8,128)(2,1)S(1)} %get-tuple-element.19), channel_id=1, source_target_pairs={{0,1},{1,0},{2,3},{3,2},{4,5},{5,4},{6,7},{7,6},{8,9},{9,8},{10,11... | collective-permute-start | bytes 393224 | tf_op jit(solution)/shard_map/ppermute | solution.py:317
  51.8 1.0 collective-permute-done.1.other_ref
  52.7 2.0 %all-to-all-done.1 = f32[16,2,40,128]{3,2,1,0:T(8,128)S(1)} async-done(((f32[16,2,40,128]{3,2,1,0:T(8,128)}), f32[16,2,40,128]{3,2,1,0:T(8,128)S(1)}, u32[]{:S(2)}, u32[]{:S(2)}) %all-to-all-start.1) | async-done | bytes 655392 | tf_op jit(solution)/shard_map/all_to_all | solution.py:306
  54.8 21.9 %all_to_all.20.parts_ref = f32[16,40,128]{2,1,0:T(8,128)S(1)} all-to-all(f32[16,40,128]{2,1,0:T(8,128)S(1)} %bitcast.16), channel_id=1, replica_groups={{0,64,128,192,256,320,384,448,4,68,132,196,260,324,388,452},{1,65,129,1..., dimensions={0} | all-to-all | bytes 655360 | tf_op jit(solution)/shard_map/all_to_all | solution.py:329
  76.7 0.1 pack.1
  76.8 25.3 %all_to_all.21.recv_ref.mine_ref = bf16[32,104,128]{2,1,0:T(8,128)(2,1)S(1)} all-to-all(bf16[32,104,128]{2,1,0:T(8,128)(2,1)S(1)} %pack.1), channel_id=1, replica_groups={{0,2,4,6,8,10,12,14,16,18,20,22,24,26,28,30,32,34,36,38,40,42,44,46,48,..., dimensions={0} | all-to-all | bytes 1703936 | tf_op jit(solution)/shard_map/all_to_all | solution.py:340
  102.1 6.9 %collective-permute-start.2 = (bf16[32,104,128]{2,1,0:T(8,128)(2,1)S(1)}, bf16[32,104,128]{2,1,0:T(8,128)(2,1)S(1)}, u32[]{:S(2)}, u32[]{:S(2)}) collective-permute-start(bf16[32,104,128]{2,1,0:T(8,128)(2,1)S(1)} %all_to_all.21.recv_ref.mine_ref), channel_id=1, source_target_pairs={{0,1},{1,0},{2,3},{3,2},{4,5},{5,4},{6,7},{7,6},{8,9},{9,8},{10,11... | collective-permute-start | bytes 2555912 | tf_op jit(solution)/shard_map/ppermute | solution.py:341
  109.0 1.1 join.1
  110.1 0.9 collective-permute-done.2.other_ref
  111.0 1.3 %rows.1 = bf16[9,256,256]{2,1,0:T(8,128)(2,1)} custom-call(bf16[32,104,128]{2,1,0:T(8,128)(2,1)S(1)} %all_to_all.21.recv_ref.mine_ref, bf16[32,104,128]{2,1,0:T(8,128)(2,1)S(1)} %collective-permute-done.2.other_ref), custom_call_target="tpu_custom_call" | custom-call | tf_op jit(solution)/shard_map/rows/pallas_call | solution.py:342
  (9 shorter events, 0.1 us)
Async XLA Ops:
  0.6 13.4 %copy-start = (s32[1,64]{1,0:T(1,128)S(1)}, s32[1,64]{1,0:T(1,128)}, u32[]{:S(2)}) copy-start(s32[1,64]{1,0:T(1,128)} %owner_ref.1) | copy-start | bytes 772
  0.6 13.5 %copy-start.1 = (bf16[3,3,256,256]{3,2,1,0:T(8,128)(2,1)S(1)}, bf16[3,3,256,256]{3,2,1,0:T(8,128)(2,1)}, u32[]{:S(2)}) copy-start(bf16[3,3,256,256]{3,2,1,0:T(8,128)(2,1)} %param.8) | copy-start | bytes 3538948
  3.5 24.8 %all-to-all-start = ((bf16[32,16,512]{2,1,0:T(8,128)(2,1)}), bf16[32,16,512]{2,1,0:T(8,128)(2,1)S(1)}, u32[]{:S(2)}, u32[]{:S(2)}) async-start(bf16[32,16,512]{2,1,0:T(8,128)(2,1)} %split.1), calls=%async_computation | async-start | bytes 1048576 | tf_op jit(solution)/shard_map/all_to_all | solution.py:268
  14.1 0.8 copy-start.2
  28.3 6.9 %collective-permute-start = (bf16[32,16,512]{2,1,0:T(8,128)(2,1)S(1)}, bf16[32,16,512]{2,1,0:T(8,128)(2,1)S(1)}, u32[]{:S(2)}, u32[]{:S(2)}) collective-permute-start(bf16[32,16,512]{2,1,0:T(8,128)(2,1)S(1)} %all-to-all-done.own_ref.own_in_ref), channel_id=1, source_target_pairs={{0,1},{1,0},{2,3},{3,2},{4,5},{5,4},{6,7},{7,6},{8,9},{9,8},{10,11... | collective-permute-start | bytes 1572872 | tf_op jit(solution)/shard_map/ppermute | solution.py:279
  37.6 17.2 %all-to-all-start.1 = ((f32[16,2,40,128]{3,2,1,0:T(8,128)}), f32[16,2,40,128]{3,2,1,0:T(8,128)S(1)}, u32[]{:S(2)}, u32[]{:S(2)}) async-start(f32[16,2,40,128]{3,2,1,0:T(8,128)} %weight_taps.1), calls=%async_computation.1 | async-start | bytes 1310720 | tf_op jit(solution)/shard_map/all_to_all | solution.py:306
  49.2 3.5 %collective-permute-start.1 = (bf16[32,16,128]{2,1,0:T(8,128)(2,1)S(1)}, bf16[32,16,128]{2,1,0:T(8,128)(2,1)S(1)}, u32[]{:S(2)}, u32[]{:S(2)}) collective-permute-start(bf16[32,16,128]{2,1,0:T(8,128)(2,1)S(1)} %get-tuple-element.19), channel_id=1, source_target_pairs={{0,1},{1,0},{2,3},{3,2},{4,5},{5,4},{6,7},{7,6},{8,9},{9,8},{10,11... | collective-permute-start | bytes 393224 | tf_op jit(solution)/shard_map/ppermute | solution.py:317
  102.1 8.9 %collective-permute-start.2 = (bf16[32,104,128]{2,1,0:T(8,128)(2,1)S(1)}, bf16[32,104,128]{2,1,0:T(8,128)(2,1)S(1)}, u32[]{:S(2)}, u32[]{:S(2)}) collective-permute-start(bf16[32,104,128]{2,1,0:T(8,128)(2,1)S(1)} %all_to_all.21.recv_ref.mine_ref), channel_id=1, source_target_pairs={{0,1},{1,0},{2,3},{3,2},{4,5},{5,4},{6,7},{7,6},{8,9},{9,8},{10,11... | collective-permute-start | bytes 2555912 | tf_op jit(solution)/shard_map/ppermute | solution.py:341

commit v6 on v5

--- a/solution.py
+++ b/solution.py
@@ -15,7 +15,7 @@
 HALF = 128
 QUARTER = 64
 SHARE = 36
-SHARE_ROWS = 40
+LOW = 4
 bf16, f32 = jnp.bfloat16, jnp.float32
 
 
@@ -132,17 +132,18 @@
     by_cell((own_ref, other_ref), put, halves)
     surround(padded, [x_ref[s] for s in range(CELLS)], sel_ref)
     grad = g_ref[...].reshape(-1, HALF).T
-    for a in range(3):
-        for b in range(3):
-            tap = a * 3 + b
-            sum_ref[tap * HALF : (tap + 1) * HALF, :] = dot(grad, window(padded, a, b)).T
-    fill = jnp.zeros((SHARE_ROWS - SHARE, HALF), f32)
+    taps = [(a, b) for a in range(3) for b in range(3)]
+    for n in range(0, len(taps), 2):
+        views = [window(padded, a, b) for a, b in taps[n : n + 2]]
+        sums = dot(grad, jnp.concatenate(views, axis=1))
+        for k in range(len(views)):
+            sum_ref[(n + k) * HALF : (n + k + 1) * HALF, :] = sums[:, k * HALF : (k + 1) * HALF].T
     for m in range(CLASSES):
         for parity in range(2):
             piece, half = share_of(m, parity)
-            begin = (m * 2 + parity) * SHARE
-            out_ref[piece, half, :SHARE, :] = sum_ref[begin : begin + SHARE, :]
-            out_ref[piece, half, SHARE:, :] = fill
+            for k in range(SHARE // LOW):
+                begin = (m * 2 + parity) * SHARE + k * LOW
+                out_ref[piece, half, :, k * HALF : (k + 1) * HALF] = sum_ref[begin : begin + LOW, :]
 
 
 def conv_kernel(
@@ -184,8 +185,10 @@
         total = parts_ref[parity]
         for s in range(parity + 2, parts_ref.shape[0], 2):
             total = total + parts_ref[s]
-        piece_ref[parity * SHARE : parity * SHARE + SHARE_ROWS, :] = total
-    piece = (piece_ref[: 2 * SHARE, :] * scale).astype(bf16)
+        for k in range(SHARE // LOW):
+            begin = parity * SHARE + k * LOW
+            piece_ref[begin : begin + LOW, :] = total[:, k * HALF : (k + 1) * HALF]
+    piece = (piece_ref[...] * scale).astype(bf16)
     for chip in range(out_ref.shape[0]):
         out_ref[chip, :CELLS, :] = own_ref[chip]
         out_ref[chip, CELLS : 2 * CELLS, :] = other_ref[chip]
@@ -280,7 +283,7 @@
 
     partial = pl.pallas_call(
         weight_kernel,
-        out_shape=jax.ShapeDtypeStruct((CLASSES, 2, SHARE_ROWS, HALF), f32),
+        out_shape=jax.ShapeDtypeStruct((CLASSES, 2, LOW, SHARE // LOW * HALF), f32),
         in_specs=vmem(3),
         out_specs=vmem(1)[0],
         scratch_shapes=[
@@ -325,7 +328,7 @@
         for low in range(2)
         for i in range(2)
     ]
-    shares = jnp.broadcast_to(part[:, None], (2, slides, SHARE_ROWS, HALF)).reshape(-1, SHARE_ROWS, HALF)
+    shares = jnp.broadcast_to(part[:, None], (2, slides, *part.shape[1:])).reshape(-1, *part.shape[1:])
     parts = lax.all_to_all(shares, ("dp", "tile"), 0, 0, tiled=True, axis_index_groups=groups)
     scale = 1.0 / math.sqrt(slides * tiles * cells)
     packed = pl.pallas_call(
@@ -333,7 +336,7 @@
         out_shape=jax.ShapeDtypeStruct((chips, 2 * CELLS + rows, HALF), bf16),
         in_specs=vmem(3),
         out_specs=vmem(1)[0],
-        scratch_shapes=[pltpu.VMEM((2 * SHARE_ROWS, HALF), f32)],
+        scratch_shapes=[pltpu.VMEM((2 * SHARE, HALF), f32)],
         compiler_params=PARAMS,
         name="pack",
     )(back_own, back_other, parts)

time: 113 us -> 110 us (0.973)
  blocking collectives: 47.2 us -> 45 us
    all_to_all x1, blocking collectives: 25.3 us -> 23.9 us  [local(): lax.all_to_all(packed, 'tile', 0, 0, tiled=True, axis_index_groups=same_c...]
  transfers between devices with their start and end apart: 5 -> 5, of which waited for: 5 -> 5; matrix products, arithmetic and copies ran while one was open for 5% -> 4% of each run, Pallas kernels for 5% -> 5%
where the time goes in v6:
time: 110 us
  blocking collectives  45 us (41%)
  starting transfers between devices  32.5 us (30%)
  waiting for transfers between devices  15.2 us (14%)
  Pallas kernels  10.6 us (10%)
  other arithmetic  2.79 us (3%)
  local copies, waits for them, and re-layouts  2.28 us (2%)
  between operations  1.61 us (1%)
    all_to_all x1, blocking collectives, local(): lax.all_to_all(packed, 'tile', 0, 0, tiled=True, axis_index_groups=same_c...  23.9 us
    all_to_all x1, blocking collectives, local(): lax.all_to_all(shares, ('dp', 'tile'), 0, 0, tiled=True, axis_index_group...  21.1 us
    all_to_all x1, starting transfers between devices, local(): lax.all_to_all(send, 'tile', 0, 0, tiled=True, axis_index_groups=same_core)  10.5 us
    all_to_all x1, waiting for transfers between devices, local(): lax.all_to_all(send, 'tile', 0, 0, tiled=True, axis_index_groups=same_core)  9.55 us
    ppermute x1, starting transfers between devices, local(): other = lax.ppermute(mine, 'tile', core)  7.7 us
    all_to_all x1, starting transfers between devices, local(): lax.all_to_all(partial, ('dp', 'tile'), 0, 0, tiled=True, axis_index_grou...  6.28 us
    ppermute x1, starting transfers between devices, local(): other = lax.ppermute(own, 'tile', core)  5.4 us
    pallas_call x1, Pallas kernels, local(): pl.pallas_call(conv_kernel, out_shape=[outgoing, outgoing], in_specs=vmem...  4.04 us
  transfers between devices with their start and end apart: 5, of which 5 were waited for; matrix products, arithmetic and copies ran while one was open for 4% of the time, Pallas kernels for 5%

profile of v6, /device:TPU:1, one launch (start us, length us, event | category | flops | bytes accessed | tf_op | source)
XLA Modules:
  0.0 109.9 jit_solution(9016339711192729829)
XLA Ops:
  1.4 2.1 %split.1 = bf16[32,16,512]{2,1,0:T(8,128)(2,1)} custom-call(s32[1]{0:T(128)S(6)} %copy.22.count_ref, s32[1,64]{1,0:T(1,128)} %owner_ref.1, bf16[256,256]{1,0:T(8,128)(2,1)} %bitcast.19, bf16[256,256]{1,0:T(8,128)(2,1)} %bitcast.20), custom_call_target="tpu_custom_call" | custom-call | tf_op jit(solution)/shard_map/split/pallas_call | solution.py:258
  3.5 10.5 %all-to-all-start = ((bf16[32,16,512]{2,1,0:T(8,128)(2,1)}), bf16[32,16,512]{2,1,0:T(8,128)(2,1)S(1)}, u32[]{:S(2)}, u32[]{:S(2)}) async-start(bf16[32,16,512]{2,1,0:T(8,128)(2,1)} %split.1), calls=%async_computation | async-start | bytes 1048576 | tf_op jit(solution)/shard_map/all_to_all | solution.py:271
  14.1 0.0 copy-start.3
  14.1 0.7 copy.20
  14.9 0.1 copy.17
  15.0 1.2 %select_reduce_fusion.1 = s32[64,8]{1,0:T(8,128)S(1)} fusion(s32[64]{0:T(128)S(1)} %broadcast_add_fusion.1, s32[64,8]{1,0:T(8,128)S(1)} %copy.17), kind=kLoop, calls=%fused_computation.2 | loop fusion | flops 97792 | bytes 4352 | tf_op jit(solution)/shard_map/reduce_sum | solution.py:240
  16.2 0.1 copy.18
  16.3 0.1 pad_add_fusion
  16.3 0.1 broadcast_compare_fusion
  16.4 1.2 %select_reduce_fusion = s32[64,8]{1,0:T(8,128)S(1)} fusion(s32[64,8]{0,1:T(8,128)S(1)} %broadcast_add_fusion, pred[64,64]{1,0:T(8,128)(4,1)S(1)} %broadcast_compare_fusion), kind=kLoop, calls=%fused_computation.1 | loop fusion | flops 65024 | bytes 8192 | tf_op jit(solution)/shard_map/reduce_sum | solution.py:241
  17.6 0.1 copy.19
  17.6 0.7 constant_dynamic-slice_fusion
  18.4 0.2 dynamic-slice_bitcast_fusion.wg_ref
  18.6 0.1 compare_convert_fusion.sel_ref
  18.8 9.6 %all-to-all-done.own_ref.own_in_ref = bf16[32,16,512]{2,1,0:T(8,128)(2,1)S(1)} async-done(((bf16[32,16,512]{2,1,0:T(8,128)(2,1)}), bf16[32,16,512]{2,1,0:T(8,128)(2,1)S(1)}, u32[]{:S(2)}, u32[]{:S(2)}) %all-to-all-start) | async-done | bytes 524320 | tf_op jit(solution)/shard_map/all_to_all | solution.py:271
  28.3 5.4 %collective-permute-start = (bf16[32,16,512]{2,1,0:T(8,128)(2,1)S(1)}, bf16[32,16,512]{2,1,0:T(8,128)(2,1)S(1)}, u32[]{:S(2)}, u32[]{:S(2)}) collective-permute-start(bf16[32,16,512]{2,1,0:T(8,128)(2,1)S(1)} %all-to-all-done.own_ref.own_in_ref), channel_id=1, source_target_pairs={{0,1},{1,0},{2,3},{3,2},{4,5},{5,4},{6,7},{7,6},{8,9},{9,8},{10,11... | collective-permute-start | bytes 1572872 | tf_op jit(solution)/shard_map/ppermute | solution.py:282
  33.7 1.5 %collective-permute-done.other_ref.other_in_ref = bf16[32,16,512]{2,1,0:T(8,128)(2,1)S(1)} collective-permute-done((bf16[32,16,512]{2,1,0:T(8,128)(2,1)S(1)}, bf16[32,16,512]{2,1,0:T(8,128)(2,1)S(1)}, u32[]{:S(2)}, u32[]{:S(2)}) %collective-permute-start) | collective-permute-done | bytes 524320 | tf_op jit(solution)/shard_map/ppermute | solution.py:282
  35.3 2.0 %weight_taps.1 = f32[16,2,4,1152]{3,2,1,0:T(4,128)} custom-call(bf16[32,16,512]{2,1,0:T(8,128)(2,1)S(1)} %all-to-all-done.own_ref.own_in_ref, bf16[32,16,512]{2,1,0:T(8,128)(2,1)S(1)} %collective-permute-done.other_ref.other_in_ref, bf16[8,64,64]{2,1,0:T(8,128)(2,1)S(1)} %compare_convert_fusion.sel_ref), custom_call_target="tpu_custom_call" | custom-call | tf_op jit(solution)/shard_map/weight_taps/pallas_call | solution.py:284
  37.3 6.3 %all-to-all-start.1 = ((f32[16,2,4,1152]{3,2,1,0:T(4,128)}), f32[16,2,4,1152]{3,2,1,0:T(4,128)S(1)}, u32[]{:S(2)}, u32[]{:S(2)}) async-start(f32[16,2,4,1152]{3,2,1,0:T(4,128)} %weight_taps.1), calls=%async_computation.1 | async-start | bytes 1179648 | tf_op jit(solution)/shard_map/all_to_all | solution.py:309
  43.6 0.3 copy.21.wo_ref
  43.9 4.0 %conv_taps.1 = (bf16[32,16,128]{2,1,0:T(8,128)(2,1)S(1)}, bf16[32,16,128]{2,1,0:T(8,128)(2,1)S(1)}) custom-call(bf16[32,16,512]{2,1,0:T(8,128)(2,1)S(1)} %all-to-all-done.own_ref.own_in_ref, bf16[32,16,512]{2,1,0:T(8,128)(2,1)S(1)} %collective-permute-done.other_ref.other_in_ref, bf16[8,64,64]{2,1,0:T(8,128)(2,1)S(1)} %compare_convert_fusion.sel_ref, ...), custom_call_target="tpu_custom_call" | custom-call | tf_op jit(solution)/shard_map/conv_taps/pallas_call | solution.py:311
  48.0 2.6 %collective-permute-start.1 = (bf16[32,16,128]{2,1,0:T(8,128)(2,1)S(1)}, bf16[32,16,128]{2,1,0:T(8,128)(2,1)S(1)}, u32[]{:S(2)}, u32[]{:S(2)}) collective-permute-start(bf16[32,16,128]{2,1,0:T(8,128)(2,1)S(1)} %get-tuple-element.19), channel_id=1, source_target_pairs={{0,1},{1,0},{2,3},{3,2},{4,5},{5,4},{6,7},{7,6},{8,9},{9,8},{10,11... | collective-permute-start | bytes 393224 | tf_op jit(solution)/shard_map/ppermute | solution.py:320
  50.5 1.0 collective-permute-done.1.other_ref
  51.5 2.2 %all-to-all-done.1 = f32[16,2,4,1152]{3,2,1,0:T(4,128)S(1)} async-done(((f32[16,2,4,1152]{3,2,1,0:T(4,128)}), f32[16,2,4,1152]{3,2,1,0:T(4,128)S(1)}, u32[]{:S(2)}, u32[]{:S(2)}) %all-to-all-start.1) | async-done | bytes 589856 | tf_op jit(solution)/shard_map/all_to_all | solution.py:309
  53.7 0.1 reduce_sum.29
  53.8 21.1 %all_to_all.20.parts_ref = f32[16,4,1152]{2,1,0:T(4,128)S(1)} all-to-all(f32[16,4,1152]{2,1,0:T(4,128)S(1)} %bitcast.17), channel_id=1, replica_groups={{0,64,128,192,256,320,384,448,4,68,132,196,260,324,388,452},{1,65,129,1..., dimensions={0} | all-to-all | bytes 589824 | tf_op jit(solution)/shard_map/all_to_all | solution.py:332
  74.9 0.1 pack.1
  75.0 23.9 %all_to_all.21.recv_ref.mine_ref = bf16[32,104,128]{2,1,0:T(8,128)(2,1)S(1)} all-to-all(bf16[32,104,128]{2,1,0:T(8,128)(2,1)S(1)} %pack.1), channel_id=1, replica_groups={{0,2,4,6,8,10,12,14,16,18,20,22,24,26,28,30,32,34,36,38,40,42,44,46,48,..., dimensions={0} | all-to-all | bytes 1703936 | tf_op jit(solution)/shard_map/all_to_all | solution.py:343
  99.0 7.7 %collective-permute-start.2 = (bf16[32,104,128]{2,1,0:T(8,128)(2,1)S(1)}, bf16[32,104,128]{2,1,0:T(8,128)(2,1)S(1)}, u32[]{:S(2)}, u32[]{:S(2)}) collective-permute-start(bf16[32,104,128]{2,1,0:T(8,128)(2,1)S(1)} %all_to_all.21.recv_ref.mine_ref), channel_id=1, source_target_pairs={{0,1},{1,0},{2,3},{3,2},{4,5},{5,4},{6,7},{7,6},{8,9},{9,8},{10,11... | collective-permute-start | bytes 2555912 | tf_op jit(solution)/shard_map/ppermute | solution.py:344
  106.7 1.1 join.1
  107.7 0.9 collective-permute-done.2.other_ref
  108.7 1.3 %rows.1 = bf16[9,256,256]{2,1,0:T(8,128)(2,1)} custom-call(bf16[32,104,128]{2,1,0:T(8,128)(2,1)S(1)} %all_to_all.21.recv_ref.mine_ref, bf16[32,104,128]{2,1,0:T(8,128)(2,1)S(1)} %collective-permute-done.2.other_ref), custom_call_target="tpu_custom_call" | custom-call | tf_op jit(solution)/shard_map/rows/pallas_call | solution.py:345
  (11 shorter events, 0.1 us)
Async XLA Ops:
  0.6 13.4 %copy-start = (s32[1,64]{1,0:T(1,128)S(1)}, s32[1,64]{1,0:T(1,128)}, u32[]{:S(2)}) copy-start(s32[1,64]{1,0:T(1,128)} %owner_ref.1) | copy-start | bytes 772
  0.6 13.5 %copy-start.2 = (bf16[3,3,256,256]{3,2,1,0:T(8,128)(2,1)S(1)}, bf16[3,3,256,256]{3,2,1,0:T(8,128)(2,1)}, u32[]{:S(2)}) copy-start(bf16[3,3,256,256]{3,2,1,0:T(8,128)(2,1)} %param.8) | copy-start | bytes 3538948
  3.5 24.8 %all-to-all-start = ((bf16[32,16,512]{2,1,0:T(8,128)(2,1)}), bf16[32,16,512]{2,1,0:T(8,128)(2,1)S(1)}, u32[]{:S(2)}, u32[]{:S(2)}) async-start(bf16[32,16,512]{2,1,0:T(8,128)(2,1)} %split.1), calls=%async_computation | async-start | bytes 1048576 | tf_op jit(solution)/shard_map/all_to_all | solution.py:271
  14.1 0.8 copy-start.3
  18.8 24.8 %copy-start.1 = (bf16[9,256,64]{1,2,0:T(8,128)(2,1)S(1)}, bf16[9,256,64]{1,2,0:T(8,128)(2,1)}, u32[]{:S(2)}) copy-start(bf16[9,256,64]{1,2,0:T(8,128)(2,1)} %constant_dynamic-slice_fusion) | copy-start | bytes 884740
  28.3 6.9 %collective-permute-start = (bf16[32,16,512]{2,1,0:T(8,128)(2,1)S(1)}, bf16[32,16,512]{2,1,0:T(8,128)(2,1)S(1)}, u32[]{:S(2)}, u32[]{:S(2)}) collective-permute-start(bf16[32,16,512]{2,1,0:T(8,128)(2,1)S(1)} %all-to-all-done.own_ref.own_in_ref), channel_id=1, source_target_pairs={{0,1},{1,0},{2,3},{3,2},{4,5},{5,4},{6,7},{7,6},{8,9},{9,8},{10,11... | collective-permute-start | bytes 1572872 | tf_op jit(solution)/shard_map/ppermute | solution.py:282
  37.3 16.4 %all-to-all-start.1 = ((f32[16,2,4,1152]{3,2,1,0:T(4,128)}), f32[16,2,4,1152]{3,2,1,0:T(4,128)S(1)}, u32[]{:S(2)}, u32[]{:S(2)}) async-start(f32[16,2,4,1152]{3,2,1,0:T(4,128)} %weight_taps.1), calls=%async_computation.1 | async-start | bytes 1179648 | tf_op jit(solution)/shard_map/all_to_all | solution.py:309
  48.0 3.5 %collective-permute-start.1 = (bf16[32,16,128]{2,1,0:T(8,128)(2,1)S(1)}, bf16[32,16,128]{2,1,0:T(8,128)(2,1)S(1)}, u32[]{:S(2)}, u32[]{:S(2)}) collective-permute-start(bf16[32,16,128]{2,1,0:T(8,128)(2,1)S(1)} %get-tuple-element.19), channel_id=1, source_target_pairs={{0,1},{1,0},{2,3},{3,2},{4,5},{5,4},{6,7},{7,6},{8,9},{9,8},{10,11... | collective-permute-start | bytes 393224 | tf_op jit(solution)/shard_map/ppermute | solution.py:320
  99.0 9.7 %collective-permute-start.2 = (bf16[32,104,128]{2,1,0:T(8,128)(2,1)S(1)}, bf16[32,104,128]{2,1,0:T(8,128)(2,1)S(1)}, u32[]{:S(2)}, u32[]{:S(2)}) collective-permute-start(bf16[32,104,128]{2,1,0:T(8,128)(2,1)S(1)} %all_to_all.21.recv_ref.mine_ref), channel_id=1, source_target_pairs={{0,1},{1,0},{2,3},{3,2},{4,5},{5,4},{6,7},{7,6},{8,9},{9,8},{10,11... | collective-permute-start | bytes 2555912 | tf_op jit(solution)/shard_map/ppermute | solution.py:344

commit v7 on v6

--- a/solution.py
+++ b/solution.py
@@ -218,21 +218,26 @@
     grad_ref[...] = join(QUARTER)
 
 
-def rows_kernel(mine_ref, other_ref, out_ref):
+def rows_kernel(mine_ref, other_ref, out_hbm, out_ref, sems):
     low = lax.axis_index("tile") % 2 == 0
     taps = out_ref.shape[0]
 
     def half(ref, ho):
         chips = [device_of(m, 0, ho) // 2 for m in range(CLASSES)]
-        return jnp.concatenate([ref[c, 2 * CELLS :, :].astype(f32) for c in chips], axis=0)
-
-    for ho in range(2):
-        mine, other = half(mine_ref, ho), half(other_ref, ho)
-        columns = slice(ho * HALF, (ho + 1) * HALF)
-        for tap in range(taps):
-            rows = slice(tap * HALF, (tap + 1) * HALF)
+        return jnp.concatenate([ref[c].astype(f32) for c in chips], axis=0)
+
+    halves = [(half(mine_ref, ho), half(other_ref, ho)) for ho in range(2)]
+    copies = []
+    for tap in range(taps):
+        rows = slice(tap * HALF, (tap + 1) * HALF)
+        for ho, (mine, other) in enumerate(halves):
+            columns = slice(ho * HALF, (ho + 1) * HALF)
             out_ref[tap, :HALF, columns] = jnp.where(low, mine[rows], other[rows]).astype(bf16)
             out_ref[tap, HALF:, columns] = jnp.where(low, other[rows], mine[rows]).astype(bf16)
+        copies.append(pltpu.make_async_copy(out_ref.at[tap], out_hbm.at[tap], sems.at[tap]))
+        copies[-1].start()
+    for copy in copies:
+        copy.wait()
 
 
 def neighbour_table(owner, neighbors, names):
@@ -341,15 +346,17 @@
         name="pack",
     )(back_own, back_other, parts)
     mine = lax.all_to_all(packed, "tile", 0, 0, tiled=True, axis_index_groups=same_core)
-    other = lax.ppermute(mine, "tile", core)
+    pieces = mine[:, 2 * CELLS :, :]
+    other = lax.ppermute(pieces, "tile", core)
     grad_weight = pl.pallas_call(
         rows_kernel,
         out_shape=jax.ShapeDtypeStruct((taps, width, width), bf16),
         in_specs=vmem(2),
-        out_specs=vmem(1)[0],
+        out_specs=hbm,
+        scratch_shapes=[pltpu.VMEM((taps, width, width), bf16), pltpu.SemaphoreType.DMA((taps,))],
         compiler_params=PARAMS,
         name="rows",
-    )(mine, other).reshape(weight.shape)
+    )(pieces, other).reshape(weight.shape)
 
     out, grad = pl.pallas_call(
         join_kernel,

time: 110 us -> 110 us (level)
  no operation moved by 1% of the time
where the time goes in v7:
time: 110 us; the launch traced here: 109 us
  blocking collectives  45 us (41%)
  starting transfers between devices  32.5 us (30%)
  waiting for transfers between devices  15.5 us (14%)
  Pallas kernels  10.4 us (9%)
  other arithmetic  2.79 us (3%)
  local copies, waits for them, and re-layouts  1.61 us (1%)
  between operations  1.61 us (1%)
    all_to_all x1, blocking collectives, local(): lax.all_to_all(packed, 'tile', 0, 0, tiled=True, axis_index_groups=same_c...  23.9 us
    all_to_all x1, blocking collectives, local(): lax.all_to_all(shares, ('dp', 'tile'), 0, 0, tiled=True, axis_index_group...  21.1 us
    all_to_all x1, starting transfers between devices, local(): lax.all_to_all(send, 'tile', 0, 0, tiled=True, axis_index_groups=same_core)  10.5 us
    all_to_all x1, waiting for transfers between devices, local(): lax.all_to_all(send, 'tile', 0, 0, tiled=True, axis_index_groups=same_core)  10.3 us
    ppermute x1, starting transfers between devices, local(): other = lax.ppermute(pieces, 'tile', core)  7.75 us
    all_to_all x1, starting transfers between devices, local(): lax.all_to_all(partial, ('dp', 'tile'), 0, 0, tiled=True, axis_index_grou...  6.29 us
    ppermute x1, starting transfers between devices, local(): other = lax.ppermute(own, 'tile', core)  5.4 us
    pallas_call x1, Pallas kernels, local(): pl.pallas_call(conv_kernel, out_shape=[outgoing, outgoing], in_specs=vmem...  4.04 us
  transfers between devices with their start and end apart: 5, of which 5 were waited for; matrix products, arithmetic and copies ran while one was open for 4% of the time, Pallas kernels for 5%

profile of v7, /device:TPU:1, one launch (start us, length us, event | category | flops | bytes accessed | tf_op | source)
XLA Modules:
  0.0 109.5 jit_solution(16811685244281030091)
XLA Ops:
  0.6 0.0 copy-start
  0.6 0.0 copy-start.2
  1.4 2.1 %split.1 = bf16[32,16,512]{2,1,0:T(8,128)(2,1)} custom-call(s32[1]{0:T(128)S(6)} %copy.22.count_ref, s32[1,64]{1,0:T(1,128)} %owner_ref.1, bf16[256,256]{1,0:T(8,128)(2,1)} %bitcast.19, bf16[256,256]{1,0:T(8,128)(2,1)} %bitcast.20), custom_call_target="tpu_custom_call" | custom-call | tf_op jit(solution)/shard_map/split/pallas_call | solution.py:263
  3.5 10.5 %all-to-all-start = ((bf16[32,16,512]{2,1,0:T(8,128)(2,1)}), bf16[32,16,512]{2,1,0:T(8,128)(2,1)S(1)}, u32[]{:S(2)}, u32[]{:S(2)}) async-start(bf16[32,16,512]{2,1,0:T(8,128)(2,1)} %split.1), calls=%async_computation | async-start | bytes 1048576 | tf_op jit(solution)/shard_map/all_to_all | solution.py:276
  14.1 0.1 copy.17
  14.2 1.2 %select_reduce_fusion.1 = s32[64,8]{1,0:T(8,128)S(1)} fusion(s32[64]{0:T(128)S(1)} %broadcast_add_fusion.1, s32[64,8]{1,0:T(8,128)S(1)} %copy.17), kind=kLoop, calls=%fused_computation.2 | loop fusion | flops 97792 | bytes 4352 | tf_op jit(solution)/shard_map/reduce_sum | solution.py:245
  15.4 0.1 copy.18
  15.5 0.1 pad_add_fusion
  15.6 0.1 broadcast_compare_fusion
  15.7 1.2 %select_reduce_fusion = s32[64,8]{1,0:T(8,128)S(1)} fusion(s32[64,8]{0,1:T(8,128)S(1)} %broadcast_add_fusion, pred[64,64]{1,0:T(8,128)(4,1)S(1)} %broadcast_compare_fusion), kind=kLoop, calls=%fused_computation.1 | loop fusion | flops 65024 | bytes 8192 | tf_op jit(solution)/shard_map/reduce_sum | solution.py:246
  16.8 0.1 copy.19
  16.9 0.7 copy.20
  17.7 0.2 dynamic-slice_bitcast_fusion.wg_ref
  17.9 0.1 compare_convert_fusion.sel_ref
  18.1 10.3 %all-to-all-done.own_ref.own_in_ref = bf16[32,16,512]{2,1,0:T(8,128)(2,1)S(1)} async-done(((bf16[32,16,512]{2,1,0:T(8,128)(2,1)}), bf16[32,16,512]{2,1,0:T(8,128)(2,1)S(1)}, u32[]{:S(2)}, u32[]{:S(2)}) %all-to-all-start) | async-done | bytes 524320 | tf_op jit(solution)/shard_map/all_to_all | solution.py:276
  28.3 5.4 %collective-permute-start = (bf16[32,16,512]{2,1,0:T(8,128)(2,1)S(1)}, bf16[32,16,512]{2,1,0:T(8,128)(2,1)S(1)}, u32[]{:S(2)}, u32[]{:S(2)}) collective-permute-start(bf16[32,16,512]{2,1,0:T(8,128)(2,1)S(1)} %all-to-all-done.own_ref.own_in_ref), channel_id=1, source_target_pairs={{0,1},{1,0},{2,3},{3,2},{4,5},{5,4},{6,7},{7,6},{8,9},{9,8},{10,11... | collective-permute-start | bytes 1572872 | tf_op jit(solution)/shard_map/ppermute | solution.py:287
  33.7 1.5 %collective-permute-done.other_ref.other_in_ref = bf16[32,16,512]{2,1,0:T(8,128)(2,1)S(1)} collective-permute-done((bf16[32,16,512]{2,1,0:T(8,128)(2,1)S(1)}, bf16[32,16,512]{2,1,0:T(8,128)(2,1)S(1)}, u32[]{:S(2)}, u32[]{:S(2)}) %collective-permute-start) | collective-permute-done | bytes 524320 | tf_op jit(solution)/shard_map/ppermute | solution.py:287
  35.2 2.0 %weight_taps.1 = f32[16,2,4,1152]{3,2,1,0:T(4,128)} custom-call(bf16[32,16,512]{2,1,0:T(8,128)(2,1)S(1)} %all-to-all-done.own_ref.own_in_ref, bf16[32,16,512]{2,1,0:T(8,128)(2,1)S(1)} %collective-permute-done.other_ref.other_in_ref, bf16[8,64,64]{2,1,0:T(8,128)(2,1)S(1)} %compare_convert_fusion.sel_ref), custom_call_target="tpu_custom_call" | custom-call | tf_op jit(solution)/shard_map/weight_taps/pallas_call | solution.py:289
  37.3 6.3 %all-to-all-start.1 = ((f32[16,2,4,1152]{3,2,1,0:T(4,128)}), f32[16,2,4,1152]{3,2,1,0:T(4,128)S(1)}, u32[]{:S(2)}, u32[]{:S(2)}) async-start(f32[16,2,4,1152]{3,2,1,0:T(4,128)} %weight_taps.1), calls=%async_computation.1 | async-start | bytes 1179648 | tf_op jit(solution)/shard_map/all_to_all | solution.py:314
  43.6 0.3 copy.21.wo_ref
  43.9 4.0 %conv_taps.1 = (bf16[32,16,128]{2,1,0:T(8,128)(2,1)S(1)}, bf16[32,16,128]{2,1,0:T(8,128)(2,1)S(1)}) custom-call(bf16[32,16,512]{2,1,0:T(8,128)(2,1)S(1)} %all-to-all-done.own_ref.own_in_ref, bf16[32,16,512]{2,1,0:T(8,128)(2,1)S(1)} %collective-permute-done.other_ref.other_in_ref, bf16[8,64,64]{2,1,0:T(8,128)(2,1)S(1)} %compare_convert_fusion.sel_ref, ...), custom_call_target="tpu_custom_call" | custom-call | tf_op jit(solution)/shard_map/conv_taps/pallas_call | solution.py:316
  48.0 2.6 %collective-permute-start.1 = (bf16[32,16,128]{2,1,0:T(8,128)(2,1)S(1)}, bf16[32,16,128]{2,1,0:T(8,128)(2,1)S(1)}, u32[]{:S(2)}, u32[]{:S(2)}) collective-permute-start(bf16[32,16,128]{2,1,0:T(8,128)(2,1)S(1)} %get-tuple-element.19), channel_id=1, source_target_pairs={{0,1},{1,0},{2,3},{3,2},{4,5},{5,4},{6,7},{7,6},{8,9},{9,8},{10,11... | collective-permute-start | bytes 393224 | tf_op jit(solution)/shard_map/ppermute | solution.py:325
  50.5 1.0 collective-permute-done.1.other_ref
  51.5 2.2 %all-to-all-done.1 = f32[16,2,4,1152]{3,2,1,0:T(4,128)S(1)} async-done(((f32[16,2,4,1152]{3,2,1,0:T(4,128)}), f32[16,2,4,1152]{3,2,1,0:T(4,128)S(1)}, u32[]{:S(2)}, u32[]{:S(2)}) %all-to-all-start.1) | async-done | bytes 589856 | tf_op jit(solution)/shard_map/all_to_all | solution.py:314
  53.7 0.1 reduce_sum.29
  53.8 21.1 %all_to_all.20.parts_ref = f32[16,4,1152]{2,1,0:T(4,128)S(1)} all-to-all(f32[16,4,1152]{2,1,0:T(4,128)S(1)} %bitcast.17), channel_id=1, replica_groups={{0,64,128,192,256,320,384,448,4,68,132,196,260,324,388,452},{1,65,129,1..., dimensions={0} | all-to-all | bytes 589824 | tf_op jit(solution)/shard_map/all_to_all | solution.py:337
  75.0 0.1 pack.1
  75.1 23.9 %all_to_all.21.recv_ref = bf16[32,104,128]{2,1,0:T(8,128)(2,1)S(1)} all-to-all(bf16[32,104,128]{2,1,0:T(8,128)(2,1)S(1)} %pack.1), channel_id=1, replica_groups={{0,2,4,6,8,10,12,14,16,18,20,22,24,26,28,30,32,34,36,38,40,42,44,46,48,..., dimensions={0} | all-to-all | bytes 1703936 | tf_op jit(solution)/shard_map/all_to_all | solution.py:348
  99.0 7.7 %collective-permute-start.2 = (bf16[32,72,128]{2,1,0:T(8,128)(2,1)S(1)}, bf16[32,72,128]{2,1,0:T(8,128)(2,1)S(1)}, u32[]{:S(2)}, u32[]{:S(2)}) collective-permute-start(bf16[32,72,128]{2,1,0:T(8,128)(2,1)S(1)} %slice.4.mine_ref), channel_id=1, source_target_pairs={{0,1},{1,0},{2,3},{3,2},{4,5},{5,4},{6,7},{7,6},{8,9},{9,8},{10,11... | collective-permute-start | bytes 1769480 | tf_op jit(solution)/shard_map/ppermute | solution.py:350
  106.7 1.1 join.1
  107.8 0.5 collective-permute-done.2.other_ref
  108.4 1.1 %rows.1 = bf16[9,256,256]{2,1,0:T(8,128)(2,1)} custom-call(bf16[32,72,128]{2,1,0:T(8,128)(2,1)S(1)} %slice.4.mine_ref, bf16[32,72,128]{2,1,0:T(8,128)(2,1)S(1)} %collective-permute-done.2.other_ref), custom_call_target="tpu_custom_call" | custom-call | tf_op jit(solution)/shard_map/rows/pallas_call | solution.py:351
  (10 shorter events, 0.1 us)
Async XLA Ops:
  0.6 13.4 %copy-start = (s32[1,64]{1,0:T(1,128)S(1)}, s32[1,64]{1,0:T(1,128)}, u32[]{:S(2)}) copy-start(s32[1,64]{1,0:T(1,128)} %owner_ref.1) | copy-start | bytes 772
  0.6 13.5 %copy-start.2 = (s32[1,64,8]{1,2,0:T(8,128)S(1)}, s32[1,64,8]{1,2,0:T(8,128)}, u32[]{:S(2)}) copy-start(s32[1,64,8]{1,2,0:T(8,128)} %param.10) | copy-start | bytes 6148
  0.7 16.2 %copy-start.1 = (bf16[3,3,256,256]{3,2,1,0:T(8,128)(2,1)S(1)}, bf16[3,3,256,256]{3,2,1,0:T(8,128)(2,1)}, u32[]{:S(2)}) copy-start(bf16[3,3,256,256]{3,2,1,0:T(8,128)(2,1)} %param.8) | copy-start | bytes 3538948
  3.5 24.8 %all-to-all-start = ((bf16[32,16,512]{2,1,0:T(8,128)(2,1)}), bf16[32,16,512]{2,1,0:T(8,128)(2,1)S(1)}, u32[]{:S(2)}, u32[]{:S(2)}) async-start(bf16[32,16,512]{2,1,0:T(8,128)(2,1)} %split.1), calls=%async_computation | async-start | bytes 1048576 | tf_op jit(solution)/shard_map/all_to_all | solution.py:276
  28.3 6.9 %collective-permute-start = (bf16[32,16,512]{2,1,0:T(8,128)(2,1)S(1)}, bf16[32,16,512]{2,1,0:T(8,128)(2,1)S(1)}, u32[]{:S(2)}, u32[]{:S(2)}) collective-permute-start(bf16[32,16,512]{2,1,0:T(8,128)(2,1)S(1)} %all-to-all-done.own_ref.own_in_ref), channel_id=1, source_target_pairs={{0,1},{1,0},{2,3},{3,2},{4,5},{5,4},{6,7},{7,6},{8,9},{9,8},{10,11... | collective-permute-start | bytes 1572872 | tf_op jit(solution)/shard_map/ppermute | solution.py:287
  37.3 16.4 %all-to-all-start.1 = ((f32[16,2,4,1152]{3,2,1,0:T(4,128)}), f32[16,2,4,1152]{3,2,1,0:T(4,128)S(1)}, u32[]{:S(2)}, u32[]{:S(2)}) async-start(f32[16,2,4,1152]{3,2,1,0:T(4,128)} %weight_taps.1), calls=%async_computation.1 | async-start | bytes 1179648 | tf_op jit(solution)/shard_map/all_to_all | solution.py:314
  48.0 3.5 %collective-permute-start.1 = (bf16[32,16,128]{2,1,0:T(8,128)(2,1)S(1)}, bf16[32,16,128]{2,1,0:T(8,128)(2,1)S(1)}, u32[]{:S(2)}, u32[]{:S(2)}) collective-permute-start(bf16[32,16,128]{2,1,0:T(8,128)(2,1)S(1)} %get-tuple-element.19), channel_id=1, source_target_pairs={{0,1},{1,0},{2,3},{3,2},{4,5},{5,4},{6,7},{7,6},{8,9},{9,8},{10,11... | collective-permute-start | bytes 393224 | tf_op jit(solution)/shard_map/ppermute | solution.py:325
  99.0 9.4 %collective-permute-start.2 = (bf16[32,72,128]{2,1,0:T(8,128)(2,1)S(1)}, bf16[32,72,128]{2,1,0:T(8,128)(2,1)S(1)}, u32[]{:S(2)}, u32[]{:S(2)}) collective-permute-start(bf16[32,72,128]{2,1,0:T(8,128)(2,1)S(1)} %slice.4.mine_ref), channel_id=1, source_target_pairs={{0,1},{1,0},{2,3},{3,2},{4,5},{5,4},{6,7},{7,6},{8,9},{9,8},{10,11... | collective-permute-start | bytes 1769480 | tf_op jit(solution)/shard_map/ppermute | solution.py:350

commit v8 on v7

--- a/solution.py
+++ b/solution.py
@@ -55,7 +55,7 @@
     return jnp.dot(a, b, preferred_element_type=f32)
 
 
-def split_kernel(count_ref, owner_hbm, x_hbm, g_hbm, send_ref, owner_ref, x_ref, g_ref, sems):
+def split_kernel(count_ref, owner_hbm, x_hbm, g_hbm, send_hbm, send_ref, owner_ref, x_ref, g_ref, sems, out_sems):
     pairs = [(owner_hbm, owner_ref), (x_hbm, x_ref), (g_hbm, g_ref)]
     copies = [pltpu.make_async_copy(src, dst, sems.at[n]) for n, (src, dst) in enumerate(pairs)]
     for copy in copies:
@@ -65,14 +65,23 @@
         copy.wait()
     live = live_mask(owner_ref[...], count_ref[0])
     order = jnp.where(order & live, 1.0, 0.0).astype(bf16)
-    x = dot(order, x_ref[...]).astype(bf16)
-    g = dot(order, g_ref[...]).astype(bf16)
-    for m in range(CLASSES):
-        rows = slice(m * CELLS, (m + 1) * CELLS)
-        for ho in range(2):
-            chip = device_of(m, 0, ho) // 2
-            send_ref[chip, :, : 2 * HALF] = x[rows]
-            send_ref[chip, :, 2 * HALF :] = g[rows]
+    column = send_ref.shape[0] // 4
+    outs = []
+    for n in range(4):
+        block = order[n * 4 * CELLS : (n + 1) * 4 * CELLS]
+        x = dot(block, x_ref[...]).astype(bf16)
+        g = dot(block, g_ref[...]).astype(bf16)
+        for k in range(4):
+            rows = slice(k * CELLS, (k + 1) * CELLS)
+            for ho in range(2):
+                chip = device_of(n * 4 + k, 0, ho) // 2
+                send_ref[chip, :, : 2 * HALF] = x[rows]
+                send_ref[chip, :, 2 * HALF :] = g[rows]
+        part = pl.ds(n * column, column)
+        outs.append(pltpu.make_async_copy(send_ref.at[part], send_hbm.at[part], out_sems.at[n]))
+        outs[-1].start()
+    for copy in outs:
+        copy.wait()
 
 
 def surround(padded, cells, sel_ref):
@@ -264,12 +273,14 @@
         split_kernel,
         out_shape=jax.ShapeDtypeStruct((chips, CELLS, 4 * HALF), bf16),
         in_specs=[smem, hbm, hbm, hbm],
-        out_specs=vmem(1)[0],
+        out_specs=hbm,
         scratch_shapes=[
+            pltpu.VMEM((chips, CELLS, 4 * HALF), bf16),
             pltpu.VMEM((1, tiles), jnp.int32),
             pltpu.VMEM((cells, width), bf16),
             pltpu.VMEM((cells, width), bf16),
             pltpu.SemaphoreType.DMA((3,)),
+            pltpu.SemaphoreType.DMA((4,)),
         ],
         name="split",
     )(tile_counts, tile_owner, features.reshape(cells, width), cotangent.reshape(cells, width))

time: 110 us -> 110 us (level)
  no operation moved by 1% of the time
where the time goes in v8:
time: 110 us; the launch traced here: 109 us
  blocking collectives  45 us (41%)
  starting transfers between devices  32.5 us (30%)
  waiting for transfers between devices  15.5 us (14%)
  Pallas kernels  10.5 us (10%)
  other arithmetic  2.79 us (3%)
  local copies, waits for them, and re-layouts  1.61 us (1%)
  between operations  1.61 us (1%)
    all_to_all x1, blocking collectives, local(): lax.all_to_all(packed, 'tile', 0, 0, tiled=True, axis_index_groups=same_c...  23.9 us
    all_to_all x1, blocking collectives, local(): lax.all_to_all(shares, ('dp', 'tile'), 0, 0, tiled=True, axis_index_group...  21.1 us
    all_to_all x1, starting transfers between devices, local(): lax.all_to_all(send, 'tile', 0, 0, tiled=True, axis_index_groups=same_core)  10.5 us
    all_to_all x1, waiting for transfers between devices, local(): lax.all_to_all(send, 'tile', 0, 0, tiled=True, axis_index_groups=same_core)  10.3 us
    ppermute x1, starting transfers between devices, local(): other = lax.ppermute(pieces, 'tile', core)  7.74 us
    all_to_all x1, starting transfers between devices, local(): lax.all_to_all(partial, ('dp', 'tile'), 0, 0, tiled=True, axis_index_grou...  6.28 us
    ppermute x1, starting transfers between devices, local(): other = lax.ppermute(own, 'tile', core)  5.4 us
    pallas_call x1, Pallas kernels, local(): pl.pallas_call(conv_kernel, out_shape=[outgoing, outgoing], in_specs=vmem...  4.04 us
  transfers between devices with their start and end apart: 5, of which 5 were waited for; matrix products, arithmetic and copies ran while one was open for 4% of the time, Pallas kernels for 5%

profile of v8, /device:TPU:1, one launch (start us, length us, event | category | flops | bytes accessed | tf_op | source)
XLA Modules:
  0.0 109.5 jit_solution(17827738194230816036)
XLA Ops:
  0.6 0.0 copy-start
  1.4 2.1 %split.1 = bf16[32,16,512]{2,1,0:T(8,128)(2,1)} custom-call(s32[1]{0:T(128)S(6)} %copy.22.count_ref, s32[1,64]{1,0:T(1,128)} %owner_ref.1, bf16[256,256]{1,0:T(8,128)(2,1)} %bitcast.19, bf16[256,256]{1,0:T(8,128)(2,1)} %bitcast.20), custom_call_target="tpu_custom_call" | custom-call | tf_op jit(solution)/shard_map/split/pallas_call | solution.py:272
  3.5 10.5 %all-to-all-start = ((bf16[32,16,512]{2,1,0:T(8,128)(2,1)}), bf16[32,16,512]{2,1,0:T(8,128)(2,1)S(1)}, u32[]{:S(2)}, u32[]{:S(2)}) async-start(bf16[32,16,512]{2,1,0:T(8,128)(2,1)} %split.1), calls=%async_computation | async-start | bytes 1048576 | tf_op jit(solution)/shard_map/all_to_all | solution.py:287
  14.1 0.1 copy.17
  14.2 1.2 %select_reduce_fusion.1 = s32[64,8]{1,0:T(8,128)S(1)} fusion(s32[64]{0:T(128)S(1)} %broadcast_add_fusion.1, s32[64,8]{1,0:T(8,128)S(1)} %copy.17), kind=kLoop, calls=%fused_computation.2 | loop fusion | flops 97792 | bytes 4352 | tf_op jit(solution)/shard_map/reduce_sum | solution.py:254
  15.4 0.1 copy.18
  15.5 0.1 pad_add_fusion
  15.6 0.1 broadcast_compare_fusion
  15.7 1.2 %select_reduce_fusion = s32[64,8]{1,0:T(8,128)S(1)} fusion(s32[64,8]{0,1:T(8,128)S(1)} %broadcast_add_fusion, pred[64,64]{1,0:T(8,128)(4,1)S(1)} %broadcast_compare_fusion), kind=kLoop, calls=%fused_computation.1 | loop fusion | flops 65024 | bytes 8192 | tf_op jit(solution)/shard_map/reduce_sum | solution.py:255
  16.8 0.1 copy.19
  16.9 0.0 copy-done.1
  16.9 0.7 copy.20
  17.7 0.2 dynamic-slice_bitcast_fusion.wg_ref
  17.9 0.1 compare_convert_fusion.sel_ref
  18.1 10.3 %all-to-all-done.own_ref.own_in_ref = bf16[32,16,512]{2,1,0:T(8,128)(2,1)S(1)} async-done(((bf16[32,16,512]{2,1,0:T(8,128)(2,1)}), bf16[32,16,512]{2,1,0:T(8,128)(2,1)S(1)}, u32[]{:S(2)}, u32[]{:S(2)}) %all-to-all-start) | async-done | bytes 524320 | tf_op jit(solution)/shard_map/all_to_all | solution.py:287
  28.3 5.4 %collective-permute-start = (bf16[32,16,512]{2,1,0:T(8,128)(2,1)S(1)}, bf16[32,16,512]{2,1,0:T(8,128)(2,1)S(1)}, u32[]{:S(2)}, u32[]{:S(2)}) collective-permute-start(bf16[32,16,512]{2,1,0:T(8,128)(2,1)S(1)} %all-to-all-done.own_ref.own_in_ref), channel_id=1, source_target_pairs={{0,1},{1,0},{2,3},{3,2},{4,5},{5,4},{6,7},{7,6},{8,9},{9,8},{10,11... | collective-permute-start | bytes 1572872 | tf_op jit(solution)/shard_map/ppermute | solution.py:298
  33.7 1.5 %collective-permute-done.other_ref.other_in_ref = bf16[32,16,512]{2,1,0:T(8,128)(2,1)S(1)} collective-permute-done((bf16[32,16,512]{2,1,0:T(8,128)(2,1)S(1)}, bf16[32,16,512]{2,1,0:T(8,128)(2,1)S(1)}, u32[]{:S(2)}, u32[]{:S(2)}) %collective-permute-start) | collective-permute-done | bytes 524320 | tf_op jit(solution)/shard_map/ppermute | solution.py:298
  35.3 2.1 %weight_taps.1 = f32[16,2,4,1152]{3,2,1,0:T(4,128)} custom-call(bf16[32,16,512]{2,1,0:T(8,128)(2,1)S(1)} %all-to-all-done.own_ref.own_in_ref, bf16[32,16,512]{2,1,0:T(8,128)(2,1)S(1)} %collective-permute-done.other_ref.other_in_ref, bf16[8,64,64]{2,1,0:T(8,128)(2,1)S(1)} %compare_convert_fusion.sel_ref), custom_call_target="tpu_custom_call" | custom-call | tf_op jit(solution)/shard_map/weight_taps/pallas_call | solution.py:300
  37.3 6.3 %all-to-all-start.1 = ((f32[16,2,4,1152]{3,2,1,0:T(4,128)}), f32[16,2,4,1152]{3,2,1,0:T(4,128)S(1)}, u32[]{:S(2)}, u32[]{:S(2)}) async-start(f32[16,2,4,1152]{3,2,1,0:T(4,128)} %weight_taps.1), calls=%async_computation.1 | async-start | bytes 1179648 | tf_op jit(solution)/shard_map/all_to_all | solution.py:325
  43.6 0.3 copy.21.wo_ref
  43.9 4.0 %conv_taps.1 = (bf16[32,16,128]{2,1,0:T(8,128)(2,1)S(1)}, bf16[32,16,128]{2,1,0:T(8,128)(2,1)S(1)}) custom-call(bf16[32,16,512]{2,1,0:T(8,128)(2,1)S(1)} %all-to-all-done.own_ref.own_in_ref, bf16[32,16,512]{2,1,0:T(8,128)(2,1)S(1)} %collective-permute-done.other_ref.other_in_ref, bf16[8,64,64]{2,1,0:T(8,128)(2,1)S(1)} %compare_convert_fusion.sel_ref, ...), custom_call_target="tpu_custom_call" | custom-call | tf_op jit(solution)/shard_map/conv_taps/pallas_call | solution.py:327
  48.0 2.5 %collective-permute-start.1 = (bf16[32,16,128]{2,1,0:T(8,128)(2,1)S(1)}, bf16[32,16,128]{2,1,0:T(8,128)(2,1)S(1)}, u32[]{:S(2)}, u32[]{:S(2)}) collective-permute-start(bf16[32,16,128]{2,1,0:T(8,128)(2,1)S(1)} %get-tuple-element.19), channel_id=1, source_target_pairs={{0,1},{1,0},{2,3},{3,2},{4,5},{5,4},{6,7},{7,6},{8,9},{9,8},{10,11... | collective-permute-start | bytes 393224 | tf_op jit(solution)/shard_map/ppermute | solution.py:336
  50.5 1.0 collective-permute-done.1.other_ref
  51.5 2.2 %all-to-all-done.1 = f32[16,2,4,1152]{3,2,1,0:T(4,128)S(1)} async-done(((f32[16,2,4,1152]{3,2,1,0:T(4,128)}), f32[16,2,4,1152]{3,2,1,0:T(4,128)S(1)}, u32[]{:S(2)}, u32[]{:S(2)}) %all-to-all-start.1) | async-done | bytes 589856 | tf_op jit(solution)/shard_map/all_to_all | solution.py:325
  53.7 0.1 reduce_sum.29
  53.8 21.1 %all_to_all.20.parts_ref = f32[16,4,1152]{2,1,0:T(4,128)S(1)} all-to-all(f32[16,4,1152]{2,1,0:T(4,128)S(1)} %bitcast.17), channel_id=1, replica_groups={{0,64,128,192,256,320,384,448,4,68,132,196,260,324,388,452},{1,65,129,1..., dimensions={0} | all-to-all | bytes 589824 | tf_op jit(solution)/shard_map/all_to_all | solution.py:348
  75.0 0.1 pack.1
  75.0 23.9 %all_to_all.21.recv_ref = bf16[32,104,128]{2,1,0:T(8,128)(2,1)S(1)} all-to-all(bf16[32,104,128]{2,1,0:T(8,128)(2,1)S(1)} %pack.1), channel_id=1, replica_groups={{0,2,4,6,8,10,12,14,16,18,20,22,24,26,28,30,32,34,36,38,40,42,44,46,48,..., dimensions={0} | all-to-all | bytes 1703936 | tf_op jit(solution)/shard_map/all_to_all | solution.py:359
  99.0 7.7 %collective-permute-start.2 = (bf16[32,72,128]{2,1,0:T(8,128)(2,1)S(1)}, bf16[32,72,128]{2,1,0:T(8,128)(2,1)S(1)}, u32[]{:S(2)}, u32[]{:S(2)}) collective-permute-start(bf16[32,72,128]{2,1,0:T(8,128)(2,1)S(1)} %slice.4.mine_ref), channel_id=1, source_target_pairs={{0,1},{1,0},{2,3},{3,2},{4,5},{5,4},{6,7},{7,6},{8,9},{9,8},{10,11... | collective-permute-start | bytes 1769480 | tf_op jit(solution)/shard_map/ppermute | solution.py:361
  106.7 1.1 join.1
  107.8 0.5 collective-permute-done.2.other_ref
  108.4 1.1 %rows.1 = bf16[9,256,256]{2,1,0:T(8,128)(2,1)} custom-call(bf16[32,72,128]{2,1,0:T(8,128)(2,1)S(1)} %slice.4.mine_ref, bf16[32,72,128]{2,1,0:T(8,128)(2,1)S(1)} %collective-permute-done.2.other_ref), custom_call_target="tpu_custom_call" | custom-call | tf_op jit(solution)/shard_map/rows/pallas_call | solution.py:362
  (10 shorter events, 0.1 us)
Async XLA Ops:
  0.6 13.4 %copy-start = (s32[1,64]{1,0:T(1,128)S(1)}, s32[1,64]{1,0:T(1,128)}, u32[]{:S(2)}) copy-start(s32[1,64]{1,0:T(1,128)} %owner_ref.1) | copy-start | bytes 772
  0.6 13.5 %copy-start.2 = (s32[1,64,8]{1,2,0:T(8,128)S(1)}, s32[1,64,8]{1,2,0:T(8,128)}, u32[]{:S(2)}) copy-start(s32[1,64,8]{1,2,0:T(8,128)} %param.10) | copy-start | bytes 6148
  0.7 16.2 %copy-start.1 = (bf16[3,3,256,256]{3,2,1,0:T(8,128)(2,1)S(1)}, bf16[3,3,256,256]{3,2,1,0:T(8,128)(2,1)}, u32[]{:S(2)}) copy-start(bf16[3,3,256,256]{3,2,1,0:T(8,128)(2,1)} %param.8) | copy-start | bytes 3538948
  3.5 24.8 %all-to-all-start = ((bf16[32,16,512]{2,1,0:T(8,128)(2,1)}), bf16[32,16,512]{2,1,0:T(8,128)(2,1)S(1)}, u32[]{:S(2)}, u32[]{:S(2)}) async-start(bf16[32,16,512]{2,1,0:T(8,128)(2,1)} %split.1), calls=%async_computation | async-start | bytes 1048576 | tf_op jit(solution)/shard_map/all_to_all | solution.py:287
  28.3 6.9 %collective-permute-start = (bf16[32,16,512]{2,1,0:T(8,128)(2,1)S(1)}, bf16[32,16,512]{2,1,0:T(8,128)(2,1)S(1)}, u32[]{:S(2)}, u32[]{:S(2)}) collective-permute-start(bf16[32,16,512]{2,1,0:T(8,128)(2,1)S(1)} %all-to-all-done.own_ref.own_in_ref), channel_id=1, source_target_pairs={{0,1},{1,0},{2,3},{3,2},{4,5},{5,4},{6,7},{7,6},{8,9},{9,8},{10,11... | collective-permute-start | bytes 1572872 | tf_op jit(solution)/shard_map/ppermute | solution.py:298
  37.3 16.4 %all-to-all-start.1 = ((f32[16,2,4,1152]{3,2,1,0:T(4,128)}), f32[16,2,4,1152]{3,2,1,0:T(4,128)S(1)}, u32[]{:S(2)}, u32[]{:S(2)}) async-start(f32[16,2,4,1152]{3,2,1,0:T(4,128)} %weight_taps.1), calls=%async_computation.1 | async-start | bytes 1179648 | tf_op jit(solution)/shard_map/all_to_all | solution.py:325
  48.0 3.5 %collective-permute-start.1 = (bf16[32,16,128]{2,1,0:T(8,128)(2,1)S(1)}, bf16[32,16,128]{2,1,0:T(8,128)(2,1)S(1)}, u32[]{:S(2)}, u32[]{:S(2)}) collective-permute-start(bf16[32,16,128]{2,1,0:T(8,128)(2,1)S(1)} %get-tuple-element.19), channel_id=1, source_target_pairs={{0,1},{1,0},{2,3},{3,2},{4,5},{5,4},{6,7},{7,6},{8,9},{9,8},{10,11... | collective-permute-start | bytes 393224 | tf_op jit(solution)/shard_map/ppermute | solution.py:336
  99.0 9.4 %collective-permute-start.2 = (bf16[32,72,128]{2,1,0:T(8,128)(2,1)S(1)}, bf16[32,72,128]{2,1,0:T(8,128)(2,1)S(1)}, u32[]{:S(2)}, u32[]{:S(2)}) collective-permute-start(bf16[32,72,128]{2,1,0:T(8,128)(2,1)S(1)} %slice.4.mine_ref), channel_id=1, source_target_pairs={{0,1},{1,0},{2,3},{3,2},{4,5},{5,4},{6,7},{7,6},{8,9},{9,8},{10,11... | collective-permute-start | bytes 1769480 | tf_op jit(solution)/shard_map/ppermute | solution.py:361
